TPU v7x, 32 devices: a whole 2x2x4 slice. The times are simulated.
32 devices in a mesh: dp: 8 (over z, x), mp: 4 (over y, core).
Axes of the slice: x: 2, y: 2, z: 4, core: 2. Of those that a mesh axis runs over, the one named last changes fastest.
Arguments:
- tokens: bfloat16 [8192, 2048], P('dp'), may hold values from -6 to 6
- cotangent: bfloat16 [8192, 2048], P('dp'), may hold values from -6 to 6
- segment_ids: int32 [8, 1024], P('dp'), may hold values from 0 to 7, never falling along the last dimension, each value on 1 to 512 neighbouring positions
- w_query: float32 [2048, 2048], P('dp', 'mp'), may hold values from -3 to 3
- w_key: float32 [2048, 1024], P('dp', 'mp'), may hold values from -3 to 3
- w_value: float32 [2048, 1024], P('dp', 'mp'), may hold values from -3 to 3
- w_out: float32 [2048, 2048], P(('mp', 'dp')), may hold values from -3 to 3
- w_gate_up: float32 [2, 2048, 8192], P(None, 'dp', 'mp'), may hold values from -3 to 3
- w_down: float32 [8192, 2048], P(('mp', 'dp')), may hold values from -3 to 3
- norm_gains: float32 [2, 2048], P(None, 'dp'), may hold values from 0.5 to 1.5
- query_moments: float32 [2, 2048, 2048], P(None, 'dp', 'mp'), may hold values from -65536 to 131072, as said below
- key_moments: float32 [2, 2048, 1024], P(None, 'dp', 'mp'), may hold values from -65536 to 131072, as said below
- value_moments: float32 [2, 2048, 1024], P(None, 'dp', 'mp'), may hold values from -65536 to 131072, as said below
- out_moments: float32 [2, 2048, 2048], P(None, ('mp', 'dp')), may hold values from -65536 to 131072, as said below
- gate_up_moments: float32 [2, 2, 2048, 8192], P(None, None, 'dp', 'mp'), may hold values from -65536 to 131072, as said below
- down_moments: float32 [2, 8192, 2048], P(None, ('mp', 'dp')), may hold values from -65536 to 131072, as said below
- gains_moments: float32 [2, 2, 2048], P(None, None, 'dp'), may hold values from -65536 to 131072, as said below
Outputs:
- block_output: bfloat16 [8192, 2048], P('dp')
- input_grad: float32 [8192, 2048], P('dp')
- grad_query: float32 [2048, 2048], P('dp', 'mp')
- grad_key: float32 [2048, 1024], P('dp', 'mp')
- grad_value: float32 [2048, 1024], P('dp', 'mp')
- grad_out: float32 [2048, 2048], P(('mp', 'dp'))
- grad_gate_up: float32 [2, 2048, 8192], P(None, 'dp', 'mp')
- grad_down: float32 [8192, 2048], P(('mp', 'dp'))
- grad_gains: float32 [2, 2048], P(None, 'dp')
- moments_query: float32 [2048, 2048], P('dp', 'mp')
- moments_key: float32 [2048, 1024], P('dp', 'mp')
- moments_value: float32 [2048, 1024], P('dp', 'mp')
- moments_out: float32 [2048, 2048], P(('mp', 'dp'))
- moments_gate_up: float32 [2, 2048, 8192], P(None, 'dp', 'mp')
- moments_down: float32 [8192, 2048], P(('mp', 'dp'))
- moments_gains: float32 [2, 2048], P(None, 'dp')
- new_query: float32 [2048, 2048], P('dp', 'mp')
- new_key: float32 [2048, 1024], P('dp', 'mp')
- new_value: float32 [2048, 1024], P('dp', 'mp')
- new_out: float32 [2048, 2048], P(('mp', 'dp'))
- new_gate_up: float32 [2, 2048, 8192], P(None, 'dp', 'mp')
- new_down: float32 [8192, 2048], P(('mp', 'dp'))
- new_gains: float32 [2, 2048], P(None, 'dp')
- copy_query: bfloat16 [2048, 2048], P('dp', 'mp')
- copy_key: bfloat16 [2048, 1024], P('dp', 'mp')
- copy_value: bfloat16 [2048, 1024], P('dp', 'mp')
- copy_out: bfloat16 [2048, 2048], P(('mp', 'dp'))
- copy_gate_up: bfloat16 [2, 2048, 8192], P(None, 'dp', 'mp')
- copy_down: bfloat16 [8192, 2048], P(('mp', 'dp'))
- copy_gains: bfloat16 [2, 2048], P(None, 'dp')
- norms: float32 [2, 7], replicated
- head_maxima: float32 [16], replicated
Inputs may be any that keep to these rules, and one draw needn't show every extreme that they name: `segment_ids`: ids never fall along a sequence; a document spans at most 512 tokens, and one in every sequence spans exactly that many. `query_moments`: the second moments are positive. `key_moments`: the second moments are positive. `value_moments`: the second moments are positive. `out_moments`: the second moments are positive. `gate_up_moments`: the second moments are positive. `down_moments`: the second moments are positive. `gains_moments`: the second moments are positive.
All inputs are finite; a program needn't handle non-finite values.
Results may differ from a plain program's by a relative error of at most 0.015.
The roundings to bfloat16 on the way count: a program that leaves them out, or rounds other values in their place, can miss the bound.
Values may be sent and summed in bfloat16 or wider, within the bound.
A program may use at most 320 MiB of HBM per device.

v0:
```python
import math

import jax
import jax.numpy as jnp
from jax import lax
from jax.sharding import PartitionSpec as P

HEADS = 16
HEAD = 128
BLOCK = 512
CLIP = 10


NORM_EPS = 1e-05
ROPE_BASE = 1000000.0
RATE = 0.4
DECAY = 0.5
WEIGHT_DECAY = 0.01
STEP_EPS = 1e-06
MASKED = -1e30


def rope_tables(length):
    positions = jnp.arange(length, dtype=jnp.float32)
    frequency = ROPE_BASE ** (-(jnp.arange(HEAD // 2, dtype=jnp.float32) * 2.0) / HEAD)
    angles = positions[:, None] * frequency[None, :]
    return (
        jnp.concatenate([jnp.cos(angles), jnp.cos(angles)], 1),
        jnp.concatenate([jnp.sin(angles), jnp.sin(angles)], 1),
    )


def rotate(values, cosine_table, sine_table):
    half_width = values.shape[-1] // 2
    turned = jnp.concatenate([-values[..., half_width:], values[..., :half_width]], -1)
    return values * cosine_table[:, None, :] + turned * sine_table[:, None, :]


def rms_scale(values, gain_row):
    return values * lax.rsqrt(jnp.mean(values * values, -1, keepdims=True) + NORM_EPS) * gain_row


def gated_unit(gate_part, up_part):
    return jax.nn.silu(gate_part) * up_part


def fetch_weights(w_query, w_key, w_value, w_out, w_gate_up, w_down, norm_gains):
    return (
        lax.all_gather(w_query.astype(jnp.bfloat16), "dp", axis=0, tiled=True),
        lax.all_gather(w_key.astype(jnp.bfloat16), "dp", axis=0, tiled=True),
        lax.all_gather(w_value.astype(jnp.bfloat16), "dp", axis=0, tiled=True),
        lax.all_gather(w_out.astype(jnp.bfloat16), "dp", axis=0, tiled=True),
        lax.all_gather(w_gate_up.astype(jnp.bfloat16), "dp", axis=1, tiled=True),
        lax.all_gather(w_down.astype(jnp.bfloat16), "dp", axis=0, tiled=True),
        lax.all_gather(norm_gains.astype(jnp.bfloat16), "dp", axis=1, tiled=True),
    )


def head_sum(partial_value):
    return lax.psum(partial_value, "mp")


def input_sum(partial_value):
    return lax.psum(partial_value, "mp")


def body(
    tokens,
    cotangent,
    segment_ids,
    w_query,
    w_key,
    w_value,
    w_out,
    w_gate_up,
    w_down,
    norm_gains,
    query_moments,
    key_moments,
    value_moments,
    out_moments,
    gate_up_moments,
    down_moments,
    gains_moments,
):
    query_full, key_full, value_full, out_full, gate_up_full, down_full, gains_full = fetch_weights(
        w_query, w_key, w_value, w_out, w_gate_up, w_down, norm_gains
    )
    rows_dev = tokens.shape[0]
    seq_count = segment_ids.shape[0]
    seq_len = segment_ids.shape[1]
    heads_local = w_query.shape[1] // HEAD
    kv_local = w_key.shape[1] // HEAD
    group_size = heads_local // kv_local
    blocks = rows_dev // BLOCK
    scale_factor = 1.0 / math.sqrt(HEAD)
    cosine_one, sine_one = rope_tables(seq_len)
    cosine_table = jnp.tile(cosine_one, (seq_count, 1))
    sine_table = jnp.tile(sine_one, (seq_count, 1))
    seg_flat = segment_ids.reshape(-1)
    inputs = tokens.astype(jnp.float32)
    gain_first = gains_full[0].astype(jnp.float32)
    gain_second = gains_full[1].astype(jnp.float32)
    normed_first, norm_pull_one = jax.vjp(rms_scale, inputs, gain_first)
    normed_one = normed_first.astype(jnp.bfloat16)
    query_raw = jnp.dot(normed_one, query_full, preferred_element_type=jnp.float32).reshape(
        rows_dev, heads_local, HEAD
    )
    key_raw = jnp.dot(normed_one, key_full, preferred_element_type=jnp.float32).reshape(
        rows_dev, kv_local, HEAD
    )
    value_rows = (
        jnp.dot(normed_one, value_full, preferred_element_type=jnp.float32)
        .astype(jnp.bfloat16)
        .reshape(rows_dev, kv_local, HEAD)
    )
    query_turned, query_pull = jax.vjp(
        lambda values: rotate(values, cosine_table, sine_table), query_raw
    )
    key_turned, key_pull = jax.vjp(lambda values: rotate(values, cosine_table, sine_table), key_raw)
    query_rot = query_turned.astype(jnp.bfloat16)
    key_rot = key_turned.astype(jnp.bfloat16)

    def block_scores(block_index):
        block_start = block_index * BLOCK
        seq_start = block_start // seq_len * seq_len
        query_block = lax.dynamic_slice_in_dim(query_rot, block_start, BLOCK, 0).reshape(
            BLOCK, kv_local, group_size, HEAD
        )
        scores = (
            jnp.einsum("qkgd,skd->kgqs", query_block, key_rot, preferred_element_type=jnp.float32)
            * scale_factor
        )
        query_seg = lax.dynamic_slice_in_dim(seg_flat, block_start, BLOCK, 0)
        query_pos = block_start - seq_start + jnp.arange(BLOCK, dtype=jnp.int32)
        key_pos = jnp.arange(seq_len, dtype=jnp.int32)
        allowed = (key_pos[None, :] <= query_pos[:, None]) & (
            query_seg[:, None] == seg_flat[None, :]
        )
        masked = jnp.where(allowed[None, None], scores, MASKED)
        return (masked, query_block, key_rot, seq_start, block_start)

    def forward_block(block_index):
        masked, query_block, key_block, seq_start, block_start = block_scores(block_index)
        row_top = jnp.max(masked, -1, keepdims=True)
        exponent = jnp.exp(masked - row_top)
        row_total = jnp.sum(exponent, -1, keepdims=True)
        attn_probs = (exponent / row_total).astype(jnp.bfloat16)
        mixed_rows = jnp.einsum(
            "kgqs,skd->qkgd", attn_probs, value_rows, preferred_element_type=jnp.float32
        )
        head_peak = jnp.max(masked, axis=(2, 3)).reshape(heads_local)
        return (
            mixed_rows.reshape(BLOCK, heads_local * HEAD),
            row_top[..., 0],
            row_total[..., 0],
            head_peak,
        )

    mixed_all, row_tops, row_totals, block_peaks = lax.map(
        forward_block, jnp.arange(blocks, dtype=jnp.int32)
    )
    out_rows = mixed_all.reshape(rows_dev, heads_local * HEAD).astype(jnp.bfloat16)
    middle = inputs + head_sum(jnp.dot(out_rows, out_full, preferred_element_type=jnp.float32))
    normed_second, norm_pull_two = jax.vjp(rms_scale, middle, gain_second)
    normed_two = normed_second.astype(jnp.bfloat16)
    gate_act = jnp.dot(normed_two, gate_up_full[0], preferred_element_type=jnp.float32)
    up_act = jnp.dot(normed_two, gate_up_full[1], preferred_element_type=jnp.float32)
    hidden_full, gate_pull = jax.vjp(gated_unit, gate_act, up_act)
    hidden = hidden_full.astype(jnp.bfloat16)
    block_output = (
        middle + head_sum(jnp.dot(hidden, down_full, preferred_element_type=jnp.float32))
    ).astype(jnp.bfloat16)
    local_peak = jnp.max(block_peaks, 0)
    peak_vector = lax.dynamic_update_slice(
        jnp.full((HEADS,), MASKED, jnp.float32), local_peak, (lax.axis_index("mp") * heads_local,)
    )
    peak_all = lax.pmax(peak_vector, ("dp", "mp"))
    grad_down_w = jnp.einsum("tf,td->fd", hidden, cotangent, preferred_element_type=jnp.float32)
    grad_hidden = jnp.einsum("td,fd->tf", cotangent, down_full, preferred_element_type=jnp.float32)
    grad_gate, grad_up = gate_pull(grad_hidden)
    grad_gate_low = grad_gate.astype(jnp.bfloat16)
    grad_up_low = grad_up.astype(jnp.bfloat16)
    grad_gate_up_w = jnp.stack(
        [
            jnp.einsum("td,tf->df", normed_two, grad_gate_low, preferred_element_type=jnp.float32),
            jnp.einsum("td,tf->df", normed_two, grad_up_low, preferred_element_type=jnp.float32),
        ]
    )
    grad_normed_two = input_sum(
        jnp.einsum("tf,df->td", grad_gate_low, gate_up_full[0], preferred_element_type=jnp.float32)
        + jnp.einsum("tf,df->td", grad_up_low, gate_up_full[1], preferred_element_type=jnp.float32)
    )
    grad_middle_norm, grad_gain_two = norm_pull_two(grad_normed_two)
    grad_middle = cotangent.astype(jnp.float32) + grad_middle_norm
    grad_middle_low = grad_middle.astype(jnp.bfloat16)
    grad_out_w = jnp.einsum(
        "tc,td->cd", out_rows, grad_middle_low, preferred_element_type=jnp.float32
    )
    grad_attended = jnp.einsum(
        "td,cd->tc", grad_middle_low, out_full, preferred_element_type=jnp.float32
    ).astype(jnp.bfloat16)

    def backward_block(carried, element):
        key_acc, value_acc = carried
        block_index, row_top, row_total = element
        masked, query_block, key_block, seq_start, block_start = block_scores(block_index)
        attn_probs = jnp.exp(masked - row_top[..., None]) / row_total[..., None]
        probs_low = attn_probs.astype(jnp.bfloat16)
        grad_block = lax.dynamic_slice_in_dim(grad_attended, block_start, BLOCK, 0).reshape(
            BLOCK, kv_local, group_size, HEAD
        )
        grad_probs = jnp.einsum(
            "qkgd,skd->kgqs", grad_block, value_rows, preferred_element_type=jnp.float32
        )
        grad_scores = (
            attn_probs * (grad_probs - jnp.sum(attn_probs * grad_probs, -1, keepdims=True))
        ).astype(jnp.bfloat16)
        grad_query_block = (
            jnp.einsum("kgqs,skd->qkgd", grad_scores, key_block, preferred_element_type=jnp.float32)
            * scale_factor
        )
        grad_key_block = (
            jnp.einsum(
                "kgqs,qkgd->skd", grad_scores, query_block, preferred_element_type=jnp.float32
            )
            * scale_factor
        )
        grad_value_block = jnp.einsum(
            "kgqs,qkgd->skd", probs_low, grad_block, preferred_element_type=jnp.float32
        )
        key_acc = key_acc + grad_key_block
        value_acc = value_acc + grad_value_block
        return ((key_acc, value_acc), grad_query_block.reshape(BLOCK, heads_local, HEAD))

    start_acc = jnp.zeros((rows_dev, kv_local, HEAD), jnp.float32)
    (grad_key_rot, grad_value_rows), grad_query_blocks = lax.scan(
        backward_block,
        (start_acc, start_acc),
        (jnp.arange(blocks, dtype=jnp.int32), row_tops, row_totals),
    )
    grad_query_rot = grad_query_blocks.reshape(rows_dev, heads_local, HEAD)
    grad_query_low = (
        query_pull(grad_query_rot)[0].reshape(rows_dev, heads_local * HEAD).astype(jnp.bfloat16)
    )
    grad_key_low = key_pull(grad_key_rot)[0].reshape(rows_dev, kv_local * HEAD).astype(jnp.bfloat16)
    grad_value_low = grad_value_rows.reshape(rows_dev, kv_local * HEAD).astype(jnp.bfloat16)
    grad_query_w = jnp.einsum(
        "td,tc->dc", normed_one, grad_query_low, preferred_element_type=jnp.float32
    )
    grad_key_w = jnp.einsum(
        "td,tc->dc", normed_one, grad_key_low, preferred_element_type=jnp.float32
    )
    grad_value_w = jnp.einsum(
        "td,tc->dc", normed_one, grad_value_low, preferred_element_type=jnp.float32
    )
    grad_normed_one = input_sum(
        jnp.einsum("tc,dc->td", grad_query_low, query_full, preferred_element_type=jnp.float32)
        + jnp.einsum("tc,dc->td", grad_key_low, key_full, preferred_element_type=jnp.float32)
        + jnp.einsum("tc,dc->td", grad_value_low, value_full, preferred_element_type=jnp.float32)
    )
    grad_inputs_norm, grad_gain_one = norm_pull_one(grad_normed_one)
    input_grad = grad_middle + grad_inputs_norm
    grad_gains_w = jnp.stack([grad_gain_one, grad_gain_two])
    reduced = (
        lax.psum_scatter(grad_query_w, "dp", scatter_dimension=0, tiled=True),
        lax.psum_scatter(grad_key_w, "dp", scatter_dimension=0, tiled=True),
        lax.psum_scatter(grad_value_w, "dp", scatter_dimension=0, tiled=True),
        lax.psum_scatter(grad_out_w, "dp", scatter_dimension=0, tiled=True),
        lax.psum_scatter(grad_gate_up_w, "dp", scatter_dimension=1, tiled=True),
        lax.psum_scatter(grad_down_w, "dp", scatter_dimension=0, tiled=True),
        lax.psum_scatter(grad_gains_w, "dp", scatter_dimension=1, tiled=True),
    )
    masters = (w_query, w_key, w_value, w_out, w_gate_up, w_down, norm_gains)
    moment_list = (
        query_moments,
        key_moments,
        value_moments,
        out_moments,
        gate_up_moments,
        down_moments,
        gains_moments,
    )
    owner = (lax.axis_index("mp") == 0).astype(jnp.float32)
    new_moments = []
    directions = []
    weight_sq = []
    update_sq = []
    for number in range(7):
        master = masters[number]
        grad_sum = reduced[number]
        moment = moment_list[number]
        share = owner if number == 6 else 1.0
        first_moment = DECAY * moment[0] + (1.0 - DECAY) * grad_sum
        second_moment = DECAY * moment[1] + (1.0 - DECAY) * grad_sum * grad_sum
        direction = first_moment / (jnp.sqrt(second_moment) + STEP_EPS) + WEIGHT_DECAY * master
        new_moments.append(second_moment)
        directions.append(direction)
        weight_sq.append(jnp.sum(master * master) * share)
        update_sq.append(jnp.sum(direction * direction) * share)
    weight_local = jnp.stack(weight_sq)
    update_local = jnp.stack(update_sq)
    weight_total, update_total = lax.psum((weight_local, update_local), ("dp", "mp"))
    weight_norm = jnp.sqrt(weight_total)
    update_norm = jnp.sqrt(update_total)
    ratio = weight_norm / (update_norm + STEP_EPS)
    stepped = [masters[number] - RATE * ratio[number] * directions[number] for number in range(7)]
    gamma = CLIP / jnp.maximum(peak_all, CLIP)
    local_gamma = lax.dynamic_slice_in_dim(
        gamma, lax.axis_index("mp") * heads_local, heads_local, 0
    )
    query_scale = jnp.sqrt(local_gamma)
    key_scale = jnp.sqrt(jnp.min(local_gamma.reshape(kv_local, group_size), 1))
    query_rows = w_query.shape[0]
    new_query = (
        stepped[0].reshape(query_rows, heads_local, HEAD) * query_scale[None, :, None]
    ).reshape(query_rows, heads_local * HEAD)
    new_key = (stepped[1].reshape(query_rows, kv_local, HEAD) * key_scale[None, :, None]).reshape(
        query_rows, kv_local * HEAD
    )
    new_value = stepped[2]
    new_out = stepped[3]
    new_gate_up = stepped[4]
    new_down = stepped[5]
    new_gains = stepped[6]
    norms = jnp.stack([weight_norm, update_norm])
    return (
        block_output,
        input_grad,
        reduced[0],
        reduced[1],
        reduced[2],
        reduced[3],
        reduced[4],
        reduced[5],
        reduced[6],
        new_moments[0],
        new_moments[1],
        new_moments[2],
        new_moments[3],
        new_moments[4],
        new_moments[5],
        new_moments[6],
        new_query,
        new_key,
        new_value,
        new_out,
        new_gate_up,
        new_down,
        new_gains,
        new_query.astype(jnp.bfloat16),
        new_key.astype(jnp.bfloat16),
        new_value.astype(jnp.bfloat16),
        new_out.astype(jnp.bfloat16),
        new_gate_up.astype(jnp.bfloat16),
        new_down.astype(jnp.bfloat16),
        new_gains.astype(jnp.bfloat16),
        norms,
        peak_all,
    )


def solution(mesh):
    placed = (
        P("dp", None),
        P("dp", None),
        P("dp", None),
        P("dp", "mp"),
        P("dp", "mp"),
        P("dp", "mp"),
        P(("mp", "dp"), None),
        P(None, "dp", "mp"),
        P(("mp", "dp"), None),
        P(None, "dp"),
        P(None, "dp", "mp"),
        P(None, "dp", "mp"),
        P(None, "dp", "mp"),
        P(None, ("mp", "dp"), None),
        P(None, None, "dp", "mp"),
        P(None, ("mp", "dp"), None),
        P(None, None, "dp"),
    )
    return jax.shard_map(
        body,
        mesh=mesh,
        in_specs=placed,
        out_specs=(
            P("dp", None),
            P("dp", None),
            P("dp", "mp"),
            P("dp", "mp"),
            P("dp", "mp"),
            P(("mp", "dp"), None),
            P(None, "dp", "mp"),
            P(("mp", "dp"), None),
            P(None, "dp"),
            P("dp", "mp"),
            P("dp", "mp"),
            P("dp", "mp"),
            P(("mp", "dp"), None),
            P(None, "dp", "mp"),
            P(("mp", "dp"), None),
            P(None, "dp"),
            P("dp", "mp"),
            P("dp", "mp"),
            P("dp", "mp"),
            P(("mp", "dp"), None),
            P(None, "dp", "mp"),
            P(("mp", "dp"), None),
            P(None, "dp"),
            P("dp", "mp"),
            P("dp", "mp"),
            P("dp", "mp"),
            P(("mp", "dp"), None),
            P(None, "dp", "mp"),
            P(("mp", "dp"), None),
            P(None, "dp"),
            P(),
            P(),
        ),
        check_vma=False,
    )
```

profile of v0, /device:TPU:0, one launch (start us, length us, event | category | flops | bytes accessed | tf_op | source)
XLA Modules:
  0.0 2618.3 jit_solution(2305196865678936326)
XLA Ops:
  18.9 22.2 all_gather.21
  60.7 34.6 %all-gather.11.cloned.1.call-done = bf16[2048,256]{1,0:T(8,128)(2,1)} async-done(((bf16[256,256]{1,0:T(8,128)(2,1)}), bf16[2048,256]{1,0:T(8,128)(2,1)}) %all-gather.11.cloned.1.call-update) | async-done | bytes 1048592 | tf_op jit(solution)/shard_map/all_gather | solution.py:51
  99.9 46.2 %all-gather.7.cloned.1.call-done = bf16[2048,512]{1,0:T(8,128)(2,1)} async-done(((bf16[256,512]{1,0:T(8,128)(2,1)}), bf16[2048,512]{1,0:T(8,128)(2,1)}) %all-gather.7.cloned.1.call-update) | async-done | bytes 2097168 | tf_op jit(solution)/shard_map/all_gather | solution.py:49
  158.6 25.9 while.35
  213.0 142.8 %all-reduce.10.cloned.1.call-done = f32[1024,2048]{1,0:T(8,128)} async-done(((f32[1024,2048]{1,0:T(8,128)}), f32[1024,2048]{1,0:T(8,128)}) %all-reduce.10.cloned.1.call-update) | async-done | bytes 8388624 | tf_op jit(solution)/shard_map/psum | solution.py:60
  367.8 218.3 %all-gather.15.cloned.1.call-done = bf16[2,2048,2048]{2,1,0:T(8,128)(2,1)} async-done(((bf16[2,256,2048]{2,1,0:T(8,128)(2,1)}), bf16[2,2048,2048]{2,1,0:T(8,128)(2,1)}) %all-gather.15.cloned.1.call-update) | async-done | bytes 16777232 | tf_op jit(solution)/shard_map/all_gather | solution.py:53
  586.2 15.9 fusion.43
  613.2 98.8 %all-gather.17.cloned.1.call-done = bf16[2048,2048]{1,0:T(8,128)(2,1)} async-done(((bf16[256,2048]{1,0:T(8,128)(2,1)}), bf16[2048,2048]{1,0:T(8,128)(2,1)}) %all-gather.17.cloned.1.call-update) | async-done | bytes 8388624 | tf_op jit(solution)/shard_map/all_gather | solution.py:54
  711.9 21.8 multiply_convert_fusion
  746.6 13.6 fusion.46
  762.3 15.5 fusion.112
  777.8 133.6 %all-reduce.12.cloned.1.call-done = f32[1024,2048]{1,0:T(8,128)} async-done(((f32[1024,2048]{1,0:T(8,128)}), f32[1024,2048]{1,0:T(8,128)}) %all-reduce.12.cloned.1.call-update) | async-done | bytes 8388624 | tf_op jit(solution)/shard_map/psum | solution.py:64
  929.4 63.4 %while.36 = (s32[]{:T(128)}, f32[1024,2,128]{0,2,1:T(8,128)S(1)}, f32[1024,2,128]{0,2,1:T(8,128)}, f32[2,512,4,128]{3,1,0,2:T(8,128)}, s32[2]{0:T(128)S(1)}, /*i...) while((s32[]{:T(128)}, f32[1024,2,128]{0,2,1:T(8,128)S(1)}, ...), condition=%wide.region_13.14_spmd.clone, body=%wide.region_11.13_spmd.clone.sunk | while | flops 2708470272 | bytes 212417232 | solution.py:237
  1037.7 262.6 %all-reduce.14.cloned.1.call-done = (f32[1024,2048]{1,0:T(8,128)}, f32[1024,2048]{1,0:T(8,128)}) async-done(((f32[1024,2048]{1,0:T(8,128)}, f32[1024,2048]{1,0:T(8,128)}), (f32[1024,2048]{1,0:T(8,128)}, f32[1024,2048]{1,0:T(8,128)})) %all-reduce.14.cloned.1.call-update) | async-done | bytes 16777232 | tf_op jit(solution)/shard_map/psum | solution.py:60
  1307.8 15.4 fusion.118
  1348.2 18.7 pad_maximum_fusion
  1372.1 40.4 %pmax.7 = f32[16]{0:T(128)S(1)} all-reduce(f32[16]{0:T(128)S(1)} %dynamic_update_slice.37), channel_id=1, replica_groups=mesh['dp'=8,'mp'=4] {'dp','mp'}, use_global_device_ids=true, to_apply=%region_42.43 | all-reduce | flops 16 | bytes 128 | tf_op jit(solution)/shard_map/pmax | solution.py:178
  1415.5 29.3 %reduce-scatter.14.cloned.1.call-done = f32[256,256]{1,0:T(8,128)} async-done(((f32[2048,256]{1,0:T(8,128)}), f32[256,256]{1,0:T(8,128)}) %reduce-scatter.14.cloned.1.call-update) | async-done | bytes 262160 | tf_op jit(solution)/shard_map/reduce_scatter | solution.py:268
  1447.4 88.4 %reduce-scatter.10.cloned.1.call-done = f32[256,512]{1,0:T(8,128)} async-done(((f32[2048,512]{1,0:T(8,128)}), f32[256,512]{1,0:T(8,128)}) %reduce-scatter.10.cloned.1.call-update) | async-done | bytes 524304 | tf_op jit(solution)/shard_map/reduce_scatter | solution.py:266
  1538.8 89.4 %reduce-scatter.16.cloned.1.call-done = f32[64,2048]{1,0:T(8,128)} async-done(((f32[512,2048]{1,0:T(8,128)}), f32[64,2048]{1,0:T(8,128)}) %reduce-scatter.16.cloned.1.call-update) | async-done | bytes 524304 | tf_op jit(solution)/shard_map/reduce_scatter | solution.py:269
  1643.2 51.9 %reduce-scatter.22.cloned.1.call-done = f32[256,2]{1,0:T(8,128)} async-done(((f32[2048,2]{1,0:T(8,128)}), f32[256,2]{1,0:T(8,128)}) %reduce-scatter.22.cloned.1.call-update) | async-done | bytes 2064
  1698.0 283.6 %reduce-scatter.20.cloned.1.call-done = f32[256,2048]{1,0:T(8,128)} async-done(((f32[2048,2048]{1,0:T(8,128)}), f32[256,2048]{1,0:T(8,128)}) %reduce-scatter.20.cloned.1.call-update) | async-done | bytes 2097168 | tf_op jit(solution)/shard_map/reduce_scatter | solution.py:271
  1988.4 539.7 %reduce-scatter.18.cloned.1.call-done = f32[2,256,2048]{2,1,0:T(8,128)} async-done(((f32[2,2048,2048]{2,1,0:T(8,128)}), f32[2,256,2048]{2,1,0:T(8,128)}) %reduce-scatter.18.cloned.1.call-update) | async-done | bytes 4194320 | tf_op jit(solution)/shard_map/reduce_scatter | solution.py:270
  2551.2 38.5 %all-reduce.4 = (f32[7]{0:T(128)S(1)}, f32[7]{0:T(128)S(1)}) all-reduce(f32[7]{0:T(128)S(1)} %stack.90, f32[7]{0:T(128)S(1)} %stack.82), channel_id=1, replica_groups=mesh['dp'=8,'mp'=4] {'dp','mp'}, use_global_device_ids=true, to_apply=%region_40.41 | all-reduce | flops 14 | bytes 112 | tf_op jit(solution)/shard_map/psum | solution.py:303
  (351 shorter events, 372.7 us)
Async XLA Ops:
  7.2 46.5 %all-gather.9.cloned.1.call-start = ((), (), s32[]{:S(2)}) async-start(), calls=%async_computation.8 | async-start | bytes 1179648 | tf_op jit(solution)/shard_map/all_gather | solution.py:50
  9.6 85.7 %all-gather.11.cloned.1.call-start = ((), (), s32[]{:S(2)}) async-start(), calls=%async_computation.9 | async-start | bytes 1179648 | tf_op jit(solution)/shard_map/all_gather | solution.py:51
  12.0 134.1 %all-gather.7.cloned.1.call-start = ((), (), s32[]{:S(2)}) async-start(), calls=%async_computation.7 | async-start | bytes 2359296 | tf_op jit(solution)/shard_map/all_gather | solution.py:49
  14.8 181.7 %all-gather.13.cloned.1.call-start = ((), (), s32[]{:S(2)}) async-start(), calls=%async_computation.10 | async-start | bytes 2359296 | tf_op jit(solution)/shard_map/all_gather | solution.py:52
  17.4 338.4 %all-reduce.10.cloned.1.call-start = ((), (), s32[]{:S(2)}) async-start(), calls=%async_computation.11 | async-start | bytes 16777216 | tf_op jit(solution)/shard_map/psum | solution.py:60
  204.2 381.9 %all-gather.15.cloned.1.call-start = ((), (), s32[]{:S(2)}) async-start(), calls=%async_computation.12 | async-start | bytes 18874368 | tf_op jit(solution)/shard_map/all_gather | solution.py:53
  210.8 501.1 %all-gather.17.cloned.1.call-start = ((), (), s32[]{:S(2)}) async-start(), calls=%async_computation.13 | async-start | bytes 9437184 | tf_op jit(solution)/shard_map/all_gather | solution.py:54
  213.0 698.5 %all-reduce.12.cloned.1.call-start = ((), (), s32[]{:S(2)}) async-start(), calls=%async_computation.14 | async-start | bytes 16777216 | tf_op jit(solution)/shard_map/psum | solution.py:64
  760.2 540.0 %all-reduce.14.cloned.1.call-start = ((), (), s32[]{:S(2)}) async-start(), calls=%async_computation.22 | async-start | bytes 33554432 | tf_op jit(solution)/shard_map/psum | solution.py:60
  1011.1 401.9 %reduce-scatter.12.cloned.1.call-start = ((), (), s32[]{:S(2)}) async-start(), calls=%async_computation.16 | async-start | bytes 2359296 | tf_op jit(solution)/shard_map/reduce_scatter | solution.py:267
  1016.0 428.7 %reduce-scatter.14.cloned.1.call-start = ((), (), s32[]{:S(2)}) async-start(), calls=%async_computation.17 | async-start | bytes 2359296 | tf_op jit(solution)/shard_map/reduce_scatter | solution.py:268
  1021.8 514.0 %reduce-scatter.10.cloned.1.call-start = ((), (), s32[]{:S(2)}) async-start(), calls=%async_computation.15 | async-start | bytes 4718592 | tf_op jit(solution)/shard_map/reduce_scatter | solution.py:266
  1028.5 599.7 %reduce-scatter.16.cloned.1.call-start = ((), (), s32[]{:S(2)}) async-start(), calls=%async_computation.18 | async-start | bytes 4718592 | tf_op jit(solution)/shard_map/reduce_scatter | solution.py:269
  1037.6 262.6 %copy-start.46 = (f32[1,2048]{1,0:T(1,128)S(1)}, f32[1,2048]{1,0:T(1,128)}, u32[]{:S(2)}) copy-start(f32[1,2048]{1,0:T(1,128)} %copy-done.45) | copy-start | bytes 24580
  1037.6 262.6 %copy-start.52 = (f32[1024]{0:T(1024)S(1)}, f32[1024]{0:T(1024)}, u32[]{:S(2)}) copy-start(f32[1024]{0:T(1024)} %copy-done.51) | copy-start | bytes 12292
  1037.6 657.5 %reduce-scatter.22.cloned.1.call-start = ((), (), s32[]{:S(2)}) async-start(), calls=%async_computation.21 | async-start | bytes 1179648
  1307.8 673.8 %reduce-scatter.20.cloned.1.call-start = ((), (), s32[]{:S(2)}) async-start(), calls=%async_computation.20 | async-start | bytes 18874368 | tf_op jit(solution)/shard_map/reduce_scatter | solution.py:271
  1323.2 1204.8 %reduce-scatter.18.cloned.1.call-start = ((), (), s32[]{:S(2)}) async-start(), calls=%async_computation.19 | async-start | bytes 37748736 | tf_op jit(solution)/shard_map/reduce_scatter | solution.py:270
  1366.9 168.9 %copy-start.22 = (f32[256,512]{1,0:T(8,128)S(1)}, f32[256,512]{1,0:T(8,128)}, u32[]{:S(2)}) copy-start(f32[256,512]{1,0:T(8,128)} %param.24) | copy-start | bytes 1572868
  1367.0 168.9 %copy-start.35 = (f32[2,256,512]{2,1,0:T(8,128)S(1)}, f32[2,256,512]{2,1,0:T(8,128)}, u32[]{:S(2)}) copy-start(f32[2,256,512]{2,1,0:T(8,128)} %param.31) | copy-start | bytes 3145732
  1367.0 261.2 %copy-start.25 = (f32[64,2048]{1,0:T(8,128)S(1)}, f32[64,2048]{1,0:T(8,128)}, u32[]{:S(2)}) copy-start(f32[64,2048]{1,0:T(8,128)} %param.27) | copy-start | bytes 1572868
  1412.5 218.9 %copy-start.64 = (f32[16]{0:T(128)}, f32[16]{0:T(128)S(1)}, u32[]{:S(2)}) copy-start(f32[16]{0:T(128)S(1)} %pmax.7) | copy-start | bytes 196
  1631.4 350.2 %copy-start.12 = (f32[256,2048]{1,0:T(8,128)S(1)}, f32[256,2048]{1,0:T(8,128)}, u32[]{:S(2)}) copy-start(f32[256,2048]{1,0:T(8,128)} %param.29) | copy-start | bytes 6291460
  1696.1 292.3 %copy-start.57 = (f32[2,256]{1,0:T(2,128)}, f32[2,256]{1,0:T(2,128)S(1)}, u32[]{:S(2)}) copy-start(f32[2,256]{1,0:T(2,128)S(1)} %copy.96) | copy-start | bytes 6148
  (72 other events, 984.5 us)
Sparse Core Ops, SparseCore 0:
  10.7 42.8 all-gather.8
  56.4 38.8 all-gather.10
  98.0 48.0 all-gather.6
  148.6 47.8 all-gather.12
  204.3 151.3 all-reduce.9
  358.4 227.7 all-gather.14
  588.8 123.0 all-gather.16
  760.3 151.0 all-reduce.11
  1011.2 288.9 all-reduce.13
  1304.8 67.7 reduce-scatter.11
  1377.2 67.4 reduce-scatter.13
  1448.8 86.9 reduce-scatter.9
  1540.4 87.6 reduce-scatter.15
  1632.0 63.0 reduce-scatter.21
  1699.8 281.7 reduce-scatter.19
  1985.8 542.2 reduce-scatter.17
where the time goes:
time: 2630 us; the launch traced here: 2620 us
  waiting for transfers between devices  2030 us (77%)
  matrix products  241 us (9%)
  other arithmetic  166 us (6%)
  blocking collectives  101 us (4%)
  local copies, waits for them, and re-layouts  52.3 us (2%)
    reduce_scatter x1, waiting for transfers between devices, body(): lax.psum_scatter(grad_gate_up_w, 'dp', scatter_dimension=1, tiled=True)  540 us
    psum x2, waiting for transfers between devices, head_sum(): return lax.psum(partial_value, 'mp')  405 us
    reduce_scatter x1, waiting for transfers between devices, body(): lax.psum_scatter(grad_down_w, 'dp', scatter_dimension=0, tiled=True)  284 us
    all_gather x1, waiting for transfers between devices, fetch_weights(): lax.all_gather(w_gate_up.astype(jnp.bfloat16), 'dp', axis=1, tiled=True)  218 us
    psum x1, waiting for transfers between devices, input_sum(): return lax.psum(partial_value, 'mp')  134 us
    all_gather x1, waiting for transfers between devices, fetch_weights(): lax.all_gather(w_down.astype(jnp.bfloat16), 'dp', axis=0, tiled=True)  98.8 us
    reduce_scatter x1, waiting for transfers between devices, body(): lax.psum_scatter(grad_out_w, 'dp', scatter_dimension=0, tiled=True)  89.4 us
    reduce_scatter x1, waiting for transfers between devices, body(): lax.psum_scatter(grad_query_w, 'dp', scatter_dimension=0, tiled=True)  88.4 us
  transfers between devices with their start and end apart: 16, of which 15 were waited for; matrix products, arithmetic and copies ran while one was open for 10% of the time, Pallas kernels for 0%

commit v1 on v0

v1 whole, which is shorter than its diff:
```python
import functools
import math

import jax
import jax.numpy as jnp
from jax import lax
from jax.experimental import pallas as pl
from jax.experimental.pallas import tpu as pltpu
from jax.sharding import PartitionSpec as P

HEADS = 16
HEAD = 128
BLOCK = 512
CLIP = 10
TILE = 256
SLICES = 2

NORM_EPS = 1e-05
ROPE_BASE = 1000000.0
RATE = 0.4
DECAY = 0.5
WEIGHT_DECAY = 0.01
STEP_EPS = 1e-06
MASKED = -1e30

F32 = jnp.float32
BF16 = jnp.bfloat16


def rope_tables(length):
    positions = jnp.arange(length, dtype=F32)
    frequency = ROPE_BASE ** (-(jnp.arange(HEAD // 2, dtype=F32) * 2.0) / HEAD)
    angles = positions[:, None] * frequency[None, :]
    cosine, sine = jnp.cos(angles), jnp.sin(angles)
    return jnp.concatenate([cosine, cosine], 1), jnp.concatenate([-sine, sine], 1)


def turn(values, cosine, sine):
    return values * cosine + pltpu.roll(values, HEAD // 2, 1) * sine


def allowed_mask(seg_row_ref, seg_col_ref, row_start, low, high):
    query_pos = row_start + lax.broadcasted_iota(jnp.int32, (TILE, high - low), 0)
    key_pos = low + lax.broadcasted_iota(jnp.int32, (TILE, high - low), 1)
    same = seg_col_ref[row_start : row_start + TILE, :] == seg_row_ref[0, :, low:high]
    return (key_pos <= query_pos) & same


def dot_nt(left, right):
    return lax.dot_general(left, right, (((1,), (1,)), ((), ())), preferred_element_type=F32)


def dot_nn(left, right):
    return lax.dot_general(left, right, (((1,), (0,)), ((), ())), preferred_element_type=F32)


def dot_tn(left, right):
    return lax.dot_general(left, right, (((0,), (0,)), ((), ())), preferred_element_type=F32)


def attend_forward(group, qkv_ref, cos_ref, sin_ref, seg_row_ref, seg_col_ref, out_ref, rot_ref, lse_ref, peak_ref):
    length = qkv_ref.shape[0]
    scale = 1.0 / math.sqrt(HEAD)
    for part in range(group + 1):
        columns = slice(part * HEAD, (part + 1) * HEAD)
        rot_ref[:, columns] = turn(qkv_ref[:, columns], cos_ref[...], sin_ref[...]).astype(BF16)
    value_columns = slice((group + 1) * HEAD, (group + 2) * HEAD)
    rot_ref[:, value_columns] = qkv_ref[:, value_columns].astype(BF16)
    key_columns = slice(group * HEAD, (group + 1) * HEAD)
    peak_ref[...] = jnp.full(peak_ref.shape, MASKED, F32)
    peaks = [None] * group
    for start in range(0, length, TILE):
        low, high = max(0, start - BLOCK), start + TILE
        rows = slice(start, start + TILE)
        mask = allowed_mask(seg_row_ref, seg_col_ref, start, low, high)
        keys = rot_ref[low:high, key_columns]
        values = rot_ref[low:high, value_columns]
        for head in range(group):
            columns = slice(head * HEAD, (head + 1) * HEAD)
            scores = jnp.where(mask, dot_nt(rot_ref[rows, columns], keys) * scale, MASKED)
            top = jnp.max(scores, 1, keepdims=True)
            exponent = jnp.exp(scores - top)
            total = jnp.sum(exponent, 1, keepdims=True)
            probs = (exponent * (1.0 / total)).astype(BF16)
            out_ref[rows, columns] = dot_nn(probs, values).astype(BF16)
            lse_ref[rows, columns] = jnp.broadcast_to(top + jnp.log(total), (TILE, HEAD))
            peak = jnp.max(top, 0, keepdims=True)
            peaks[head] = peak if peaks[head] is None else jnp.maximum(peaks[head], peak)
    for head in range(group):
        peak_ref[0, head : head + 1, :] = jnp.broadcast_to(peaks[head], (1, HEAD))


def attend_backward(group, rot_ref, grad_ref, lse_ref, cos_ref, sin_ref, seg_row_ref, seg_col_ref, out_ref, dk_ref, dv_ref):
    length = rot_ref.shape[0]
    scale = 1.0 / math.sqrt(HEAD)
    key_columns = slice(group * HEAD, (group + 1) * HEAD)
    value_columns = slice((group + 1) * HEAD, (group + 2) * HEAD)
    dk_ref[...] = jnp.zeros(dk_ref.shape, F32)
    dv_ref[...] = jnp.zeros(dv_ref.shape, F32)
    for start in range(0, length, TILE):
        low, high = max(0, start - BLOCK), start + TILE
        rows = slice(start, start + TILE)
        mask = allowed_mask(seg_row_ref, seg_col_ref, start, low, high)
        keys = rot_ref[low:high, key_columns]
        values = rot_ref[low:high, value_columns]
        for head in range(group):
            columns = slice(head * HEAD, (head + 1) * HEAD)
            queries = rot_ref[rows, columns]
            grads = grad_ref[rows, columns]
            scores = dot_nt(queries, keys) * scale
            probs = jnp.exp(jnp.where(mask, scores - lse_ref[rows, columns][:, :1], MASKED))
            grad_probs = dot_nt(grads, values)
            inner = jnp.sum(probs * grad_probs, 1, keepdims=True)
            grad_scores = (probs * (grad_probs - inner)).astype(BF16)
            dv_ref[low:high, :] += dot_tn(probs.astype(BF16), grads)
            dk_ref[low:high, :] += dot_tn(grad_scores, queries)
            grad_query = dot_nn(grad_scores, keys) * scale
            out_ref[rows, columns] = turn(grad_query, cos_ref[rows, :], -sin_ref[rows, :]).astype(BF16)
    out_ref[:, key_columns] = turn(dk_ref[...] * scale, cos_ref[...], -sin_ref[...]).astype(BF16)
    out_ref[:, value_columns] = dv_ref[...].astype(BF16)


def attention_specs(length, group):
    wide = pl.BlockSpec((length, (group + 2) * HEAD), lambda seq, kv: (seq, kv))
    narrow = pl.BlockSpec((length, group * HEAD), lambda seq, kv: (seq, kv))
    table = pl.BlockSpec((length, HEAD), lambda seq, kv: (0, 0))
    seg_row = pl.BlockSpec((1, 1, length), lambda seq, kv: (seq, 0, 0))
    seg_col = pl.BlockSpec((length, 1), lambda seq, kv: (seq, 0))
    return wide, narrow, table, seg_row, seg_col


def attention_forward(qkv, cosine, sine, segments, group, kv_count):
    count, length = segments.shape
    rows = count * length
    wide, narrow, table, seg_row, seg_col = attention_specs(length, group)
    return pl.pallas_call(
        functools.partial(attend_forward, group),
        grid=(count, kv_count),
        in_specs=[wide, table, table, seg_row, seg_col],
        out_specs=[
            narrow,
            wide,
            narrow,
            pl.BlockSpec((1, 8, HEAD), lambda seq, kv: (seq * kv_count + kv, 0, 0)),
        ],
        out_shape=[
            jax.ShapeDtypeStruct((rows, kv_count * group * HEAD), BF16),
            jax.ShapeDtypeStruct((rows, kv_count * (group + 2) * HEAD), BF16),
            jax.ShapeDtypeStruct((rows, kv_count * group * HEAD), F32),
            jax.ShapeDtypeStruct((count * kv_count, 8, HEAD), F32),
        ],
        compiler_params=pltpu.CompilerParams(vmem_limit_bytes=48 * 2**20),
        name="attention_forward",
    )(qkv, cosine, sine, segments.reshape(count, 1, length), segments.reshape(rows, 1))


def attention_backward(rotated, grads, lse, cosine, sine, segments, group, kv_count):
    count, length = segments.shape
    rows = count * length
    wide, narrow, table, seg_row, seg_col = attention_specs(length, group)
    return pl.pallas_call(
        functools.partial(attend_backward, group),
        grid=(count, kv_count),
        in_specs=[wide, narrow, narrow, table, table, seg_row, seg_col],
        out_specs=wide,
        out_shape=jax.ShapeDtypeStruct((rows, kv_count * (group + 2) * HEAD), BF16),
        scratch_shapes=[pltpu.VMEM((length, HEAD), F32), pltpu.VMEM((length, HEAD), F32)],
        compiler_params=pltpu.CompilerParams(vmem_limit_bytes=48 * 2**20),
        name="attention_backward",
    )(rotated, grads, lse, cosine, sine, segments.reshape(count, 1, length), segments.reshape(rows, 1))


class Links:
    def __init__(self, dp_size, mp_size):
        self.dp, self.mp, self.line = dp_size, mp_size, dp_size // 2
        self.index = lax.axis_index("dp")
        self.place, self.side, self.rank = self.index // 2, self.index % 2, lax.axis_index("mp")

    def swap_mp(self, value, bit):
        return lax.ppermute(value, "mp", [(i, i ^ bit) for i in range(self.mp)])

    def swap_side(self, value, places=None):
        places = range(self.line) if places is None else places
        return lax.ppermute(value, "dp", [(p * 2 + s, p * 2 + 1 - s) for p in places for s in range(2)])

    def move(self, value, places, by):
        return lax.ppermute(value, "dp", [(p * 2 + s, (p + by) * 2 + s) for p in places for s in range(2)])


    def spread(self, own):
        ups, downs = {}, {}
        up = down = own
        for step in range(1, self.line):
            up = ups[step] = self.move(up, range(step - 1, self.line - 1), 1)
            down = downs[step] = self.move(down, range(1, self.line - step + 1), -1)
        return ups, downs

    def from_below(self, step):
        return range(step, self.line)

    def from_above(self, step):
        return range(0, self.line - step)

    def pick(self, ups, downs, step):
        return jnp.where(self.place >= step, ups[step], downs[self.line - step])

    def gather_line(self, own):
        ups, downs = self.spread(own)
        rows = own.shape[0]
        full = jnp.zeros((self.line * rows, own.shape[1]), own.dtype)
        full = lax.dynamic_update_slice(full, own, (self.place * rows, 0))
        for step in range(1, self.line):
            slot = (self.place - step) % self.line
            full = lax.dynamic_update_slice(full, self.pick(ups, downs, step), (slot * rows, 0))
        return full

    def gather_dp(self, own):
        ups, downs = self.spread(own)
        other = self.swap_side(own)
        other_ups = {s: self.swap_side(v, self.from_below(s)) for s, v in ups.items()}
        other_downs = {s: self.swap_side(v, self.from_above(s)) for s, v in downs.items()}
        rows = own.shape[0]
        full = jnp.zeros((self.dp * rows, own.shape[1]), own.dtype)

        def put(full, value, place, side):
            return lax.dynamic_update_slice(full, value, ((place * 2 + side) * rows, 0))

        full = put(full, own, self.place, self.side)
        full = put(full, other, self.place, 1 - self.side)
        for step in range(1, self.line):
            slot = (self.place - step) % self.line
            full = put(full, self.pick(ups, downs, step), slot, self.side)
            full = put(full, self.pick(other_ups, other_downs, step), slot, 1 - self.side)
        return full

    def sum_line(self, part):
        up = down = None
        for step in range(self.line - 1, 0, -1):
            term = part(jnp.minimum(self.place + step, self.line - 1)).astype(F32)
            term = term if up is None else term + up.astype(F32)
            up = self.move(term.astype(BF16), range(0, self.line - step), 1)
            term = part(jnp.maximum(self.place - step, 0)).astype(F32)
            term = term if down is None else term + down.astype(F32)
            down = self.move(term.astype(BF16), range(step, self.line), -1)
        return part(self.place).astype(F32) + up.astype(F32) + down.astype(F32)

    def sum_dp(self, partial):
        rows = partial.shape[0] // self.dp

        def cut(place, side):
            return lax.dynamic_slice_in_dim(partial, (place * 2 + side) * rows, rows, 0)

        def paired(place, places):
            received = self.swap_side(cut(place, 1 - self.side), places)
            return cut(place, self.side).astype(F32) + received.astype(F32)

        last = self.line - 1
        up = down = None
        for step in range(last, 0, -1):
            term = paired(jnp.minimum(self.place + step, last), range(0, self.line - step))
            term = term if up is None else term + up.astype(F32)
            up = self.move(term.astype(BF16), range(0, self.line - step), 1)
            term = paired(jnp.maximum(self.place - step, 0), range(step, self.line))
            term = term if down is None else term + down.astype(F32)
            down = self.move(term.astype(BF16), range(step, self.line), -1)
        return paired(self.place, None) + up.astype(F32) + down.astype(F32)


    def to_slots(self, values):
        rows = values.shape[0] // self.mp
        return jnp.concatenate(
            [lax.dynamic_slice_in_dim(values, (self.rank ^ k) * rows, rows, 0) for k in range(self.mp)], 0
        )

    def from_slots(self, values):
        rows = values.shape[0] // self.mp
        cuts = [values[k * rows : (k + 1) * rows] for k in range(self.mp)]
        odd = (self.rank & 1) == 1
        high = (self.rank & 2) == 2
        cuts = [jnp.where(odd, cuts[k ^ 1], cuts[k]) for k in range(self.mp)]
        cuts = [jnp.where(high, cuts[k ^ 2], cuts[k]) for k in range(self.mp)]
        return jnp.concatenate(cuts, 0)

    def own_quarter(self, values):
        rows = values.shape[0] // self.mp
        return lax.dynamic_slice_in_dim(values, self.rank * rows, rows, 0)

    def sum_core(self, slots):
        rows = slots.shape[0] // 4
        cut = lambda k: slots[k * rows : (k + 1) * rows]
        received = self.swap_mp(jnp.concatenate([cut(1), cut(3)], 0).astype(BF16), 1)
        return jnp.concatenate([cut(0), cut(2)], 0).astype(F32) + received.astype(F32)

    def sum_far(self, pair):
        rows = pair.shape[0] // 2
        received = self.swap_mp(pair[rows:].astype(BF16), 2)
        return pair[:rows].astype(F32) + received.astype(F32)

    def gather_mp(self, quarter):
        rows = quarter.shape[0]
        pair = jnp.concatenate([quarter, self.swap_mp(quarter, 2)], 0)
        near = self.swap_mp(pair, 1)
        return jnp.concatenate([pair[:rows], near[:rows], pair[rows:], near[rows:]], 0)

    def gather_pair(self, quarter):
        rows, columns = quarter.shape
        half = columns // 2
        left, right = quarter[:, :half], quarter[:, half:]
        left_side = self.swap_side(left)
        right_far = self.swap_mp(right, 2)
        left_far = self.swap_mp(jnp.concatenate([left, left_side], 0), 2)
        right_side = self.swap_side(jnp.concatenate([right, right_far], 0))
        left_all = jnp.concatenate([left, left_far[:rows], left_side, left_far[rows:]], 0)
        right_all = jnp.concatenate([right, right_far, right_side[:rows], right_side[rows:]], 0)
        even = jnp.concatenate([left_all, right_all], 1)
        near = self.swap_mp(even, 1)
        cut = lambda v, k: v[k * rows : (k + 1) * rows]
        return jnp.concatenate([cut(v, k) for k in range(4) for v in (even, near)], 0)

    def sum_pair(self, slots):
        total, columns = slots.shape
        rows, half = total // 8, columns // 2
        cut = lambda k: slots[k * rows : (k + 1) * rows]
        near = self.swap_mp(jnp.concatenate([cut(1), cut(3), cut(5), cut(7)], 0).astype(BF16), 1)
        mine = jnp.concatenate([cut(0), cut(2), cut(4), cut(6)], 0).astype(F32) + near.astype(F32)
        mine = mine.astype(BF16)
        left, right = mine[:, :half], mine[:, half:]
        cut = lambda v, k: v[k * rows : (k + 1) * rows]
        left = left[: 2 * rows].astype(F32) + self.swap_side(left[2 * rows :]).astype(F32)
        far = self.swap_mp(jnp.concatenate([cut(right, 1), cut(right, 3)], 0), 2)
        right = jnp.concatenate([cut(right, 0), cut(right, 2)], 0).astype(F32) + far.astype(F32)
        left = left[:rows] + self.swap_mp(left[rows:].astype(BF16), 2).astype(F32)
        right = right[:rows] + self.swap_side(right[rows:].astype(BF16)).astype(F32)
        return jnp.concatenate([left, right], 1)


def after(value, *others):
    return lax.optimization_barrier((value, *others))[0]


def inverse_rms(values):
    return lax.rsqrt(jnp.mean(values * values, -1, keepdims=True) + NORM_EPS)


def norm_pull(values, scale, gain, grad):
    turned = grad * gain
    back = scale * turned - (scale * scale * scale) * values * jnp.mean(turned * values, -1, keepdims=True)
    return back, jnp.sum(grad * values * scale, 0)


def body(
    dp_size,
    mp_size,
    tokens,
    cotangent,
    segment_ids,
    w_query,
    w_key,
    w_value,
    w_out,
    w_gate_up,
    w_down,
    norm_gains,
    query_moments,
    key_moments,
    value_moments,
    out_moments,
    gate_up_moments,
    down_moments,
    gains_moments,
):
    links = Links(dp_size, mp_size)
    line, side = links.line, links.side
    heads = w_query.shape[1] // HEAD
    kvs = w_key.shape[1] // HEAD
    group = heads // kvs
    width = tokens.shape[1]
    shard = w_query.shape[0]
    units = w_gate_up.shape[2]
    block = units // (line * 2)
    piece = block // SLICES

    def interleave(query, key, value):
        parts = []
        for kv in range(kvs):
            parts.append(query[..., kv * group * HEAD : (kv + 1) * group * HEAD])
            parts.append(key[..., kv * HEAD : (kv + 1) * HEAD])
            parts.append(value[..., kv * HEAD : (kv + 1) * HEAD])
        return jnp.concatenate(parts, -1)

    def untangle(values):
        step = (group + 2) * HEAD
        cut = lambda low, high: jnp.concatenate(
            [values[..., kv * step + low * HEAD : kv * step + high * HEAD] for kv in range(kvs)], -1
        )
        return cut(0, group), cut(group, group + 1), cut(group + 1, group + 2)

    qkv_full = links.gather_dp(interleave(w_query, w_key, w_value).astype(BF16))
    gains_full = lax.all_gather(norm_gains.astype(BF16), "dp", axis=1, tiled=True).astype(F32)

    by_side = w_gate_up.reshape(2, shard, line, 2, block)

    def side_units(which):
        cut = lax.dynamic_index_in_dim(by_side, which, 3, keepdims=False).astype(BF16)
        return [cut[..., j * piece : (j + 1) * piece] for j in range(SLICES)]

    def flat(cut):
        return jnp.concatenate([cut[0].reshape(shard, -1), cut[1].reshape(shard, -1)], 1)

    own_units = [flat(cut) for cut in side_units(side)]
    sent_units = [links.swap_side(flat(cut)) for cut in side_units(1 - side)]
    out_full = links.gather_dp(after(w_out.astype(BF16), qkv_full))
    down_low = w_down.astype(BF16)
    gate_up_full, down_full = [], []
    for j in range(SLICES):
        mine, theirs = own_units[j], sent_units[j]
        rows_pair = jnp.where(
            side == 0, jnp.concatenate([mine, theirs], 0), jnp.concatenate([theirs, mine], 0)
        )
        gate_up_full.append(links.gather_line(after(rows_pair, out_full)))
        down_full.append(links.gather_line(after(down_low[j * piece : (j + 1) * piece], out_full)))

    grad_own = links.to_slots(cotangent)
    quarter = grad_own.shape[0] // 4
    cut = lambda v, k: v[k * quarter : (k + 1) * quarter]
    grad_side = links.swap_side(jnp.concatenate([cut(grad_own, 0), cut(grad_own, 2)], 0))
    grad_near = links.swap_mp(grad_side, 1)
    grad_rows = jnp.concatenate(
        [grad_own, grad_side[:quarter], grad_near[:quarter], grad_side[quarter:], grad_near[quarter:]], 0
    )

    cosine, sine = rope_tables(segment_ids.shape[1])
    inputs = tokens.astype(F32)
    normed_one = (inputs * inverse_rms(inputs) * gains_full[0]).astype(BF16)
    qkv = jnp.dot(normed_one, qkv_full, preferred_element_type=F32)
    mixed, rotated, lse, peaks = attention_forward(qkv, cosine, sine, segment_ids, group, kvs)
    mixed_slots = links.to_slots(mixed)
    attended = links.sum_far(links.sum_core(jnp.dot(mixed_slots, out_full, preferred_element_type=F32)))
    inputs_own = links.own_quarter(tokens).astype(F32)
    middle = inputs_own + attended
    scale_two = inverse_rms(middle)
    normed_two = (middle * scale_two * gains_full[1]).astype(BF16)
    rows_two = links.gather_pair(normed_two)

    output_part = grad_normed_part = None
    grad_gate_up_parts, grad_down_parts = [], []
    for j in range(SLICES):
        columns = line * piece
        both = jnp.dot(rows_two, gate_up_full[j], preferred_element_type=F32)
        gate, up = both[:, :columns], both[:, columns:]
        sigmoid = jax.nn.sigmoid(gate)
        hidden = (gate * sigmoid * up).astype(BF16)
        grad_hidden = dot_nt(grad_rows, down_full[j])
        grad_gate = (grad_hidden * up * sigmoid * (1.0 + gate * (1.0 - sigmoid))).astype(BF16)
        grad_up = (grad_hidden * gate * sigmoid).astype(BF16)
        grad_both = jnp.concatenate([grad_gate, grad_up], 1)
        grad_down_parts.append(dot_tn(hidden, grad_rows).astype(BF16))
        grad_gate_up_parts.append(dot_tn(rows_two, grad_both).astype(BF16))
        back = dot_nt(grad_both, gate_up_full[j])
        grad_normed_part = back if grad_normed_part is None else grad_normed_part + back
        forth = jnp.dot(hidden, down_full[j], preferred_element_type=F32)
        output_part = forth if output_part is None else output_part + forth
    grad_normed_two = links.sum_pair(grad_normed_part)

    back_two, gain_two = norm_pull(middle, scale_two, gains_full[1], grad_normed_two)
    grad_middle = links.own_quarter(cotangent).astype(F32) + back_two
    grad_middle_slots = links.gather_mp(grad_middle.astype(BF16))
    grad_mixed = links.from_slots(dot_nt(grad_middle_slots, out_full).astype(BF16))
    grad_out_part = dot_tn(mixed_slots, grad_middle_slots).astype(BF16)

    grad_qkv = attention_backward(rotated, grad_mixed, lse, cosine, sine, segment_ids, group, kvs)
    grad_qkv_part = dot_tn(normed_one, grad_qkv).astype(BF16)
    grad_normed_one = links.sum_far(links.sum_core(dot_nt(links.to_slots(grad_qkv), qkv_full)))
    back_one, gain_one = norm_pull(inputs_own, inverse_rms(inputs_own), gains_full[0], grad_normed_one)
    input_grad = links.from_slots(links.gather_mp((grad_middle + back_one).astype(BF16))).astype(F32)

    output_own = middle + links.sum_pair(output_part)
    block_output = links.from_slots(links.gather_mp(output_own.astype(BF16)))

    gate_up_pieces, down_pieces = [], []
    for j in range(SLICES):
        gate_up_part, down_part = grad_gate_up_parts[j], grad_down_parts[j]
        pair_rows = 2 * shard
        summed = links.sum_line(
            lambda place: lax.dynamic_slice_in_dim(gate_up_part, place * pair_rows, pair_rows, 0)
        )
        mine = lax.dynamic_slice_in_dim(summed, side * shard, shard, 0)
        theirs = links.swap_side(lax.dynamic_slice_in_dim(summed, (1 - side) * shard, shard, 0).astype(BF16))
        theirs = theirs.astype(F32)
        gate_up_pieces.append(
            jnp.stack(
                [jnp.where(side == 0, mine, theirs), jnp.where(side == 0, theirs, mine)], 0
            ).reshape(2, shard, 2, line, piece)
        )
        down_pieces.append(
            links.sum_line(lambda place: lax.dynamic_slice_in_dim(down_part, place * piece, piece, 0))
        )
    grad_gate_up = jnp.transpose(jnp.stack(gate_up_pieces, 4), (2, 1, 3, 0, 4, 5)).reshape(w_gate_up.shape)
    grad_down = jnp.concatenate(down_pieces, 0)
    grad_out = links.sum_dp(grad_out_part)
    grad_query, grad_key, grad_value = untangle(links.sum_dp(grad_qkv_part))
    gain_terms = lax.psum(jnp.stack([gain_one, gain_two]), ("dp", "mp"))
    gain_width = norm_gains.shape[1]
    grad_gains = lax.dynamic_slice_in_dim(gain_terms, links.index * gain_width, gain_width, 1)

    count = segment_ids.shape[0]
    local_peak = jnp.max(peaks.reshape(count, kvs, 8, HEAD)[:, :, :group, 0], 0).reshape(heads)
    peak_vector = lax.dynamic_update_slice(
        jnp.full((HEADS,), MASKED, F32), local_peak, (links.rank * heads,)
    )
    peak_all = lax.pmax(peak_vector, ("dp", "mp"))

    reduced = (grad_query, grad_key, grad_value, grad_out, grad_gate_up, grad_down, grad_gains)
    masters = (w_query, w_key, w_value, w_out, w_gate_up, w_down, norm_gains)
    moment_list = (
        query_moments,
        key_moments,
        value_moments,
        out_moments,
        gate_up_moments,
        down_moments,
        gains_moments,
    )
    owner = (links.rank == 0).astype(F32)
    new_moments, directions, weight_sq, update_sq = [], [], [], []
    for number in range(7):
        master, grad_sum, moment = masters[number], reduced[number], moment_list[number]
        share = owner if number == 6 else 1.0
        first_moment = DECAY * moment[0] + (1.0 - DECAY) * grad_sum
        second_moment = DECAY * moment[1] + (1.0 - DECAY) * grad_sum * grad_sum
        direction = first_moment / (jnp.sqrt(second_moment) + STEP_EPS) + WEIGHT_DECAY * master
        new_moments.append(second_moment)
        directions.append(direction)
        weight_sq.append(jnp.sum(master * master) * share)
        update_sq.append(jnp.sum(direction * direction) * share)
    totals = lax.psum(jnp.stack(weight_sq + update_sq), ("dp", "mp"))
    weight_norm, update_norm = jnp.sqrt(totals[:7]), jnp.sqrt(totals[7:])
    ratio = weight_norm / (update_norm + STEP_EPS)
    stepped = [masters[number] - RATE * ratio[number] * directions[number] for number in range(7)]
    gamma = CLIP / jnp.maximum(peak_all, CLIP)
    local_gamma = lax.dynamic_slice_in_dim(gamma, links.rank * heads, heads, 0)
    query_scale = jnp.repeat(jnp.sqrt(local_gamma), HEAD)
    key_scale = jnp.repeat(jnp.sqrt(jnp.min(local_gamma.reshape(kvs, group), 1)), HEAD)
    stepped[0] = stepped[0] * query_scale[None, :]
    stepped[1] = stepped[1] * key_scale[None, :]
    copies = [value.astype(BF16) for value in stepped]
    norms = jnp.stack([weight_norm, update_norm])
    return (block_output, input_grad, *reduced, *new_moments, *stepped, *copies, norms, peak_all)


def solution(mesh):
    column = P("dp", "mp")
    row = P(("mp", "dp"), None)
    gate_up = P(None, "dp", "mp")
    gains = P(None, "dp")
    params = (column, column, column, row, gate_up, row, gains)
    moments = (
        P(None, "dp", "mp"),
        P(None, "dp", "mp"),
        P(None, "dp", "mp"),
        P(None, ("mp", "dp"), None),
        P(None, None, "dp", "mp"),
        P(None, ("mp", "dp"), None),
        P(None, None, "dp"),
    )
    tokens = P("dp", None)
    return jax.shard_map(
        functools.partial(body, mesh.shape["dp"], mesh.shape["mp"]),
        mesh=mesh,
        in_specs=(tokens, tokens, tokens, *params, *moments),
        out_specs=(tokens, tokens, *params, *params, *params, *params, P(), P()),
        check_vma=False,
    )
```

time: 2630 us -> 1380 us (0.52)
  waiting for transfers between devices: 2030 us -> 316 us
  starting transfers between devices: 1.05 us -> 295 us
  local copies, waits for them, and re-layouts: 52.3 us -> 182 us
  blocking collectives: 101 us -> 165 us
  matrix products: 241 us -> 184 us
    reduce_scatter x6 -> x0, waiting for transfers between devices: 1030 us -> none  [the longest x1 540 us: body(): lax.psum_scatter(grad_gate_up_w, 'dp', scatter_dimension=1, tiled=True)]
    psum x3 -> x0, waiting for transfers between devices: 539 us -> none  [the longest x2 405 us: head_sum(): return lax.psum(partial_value, 'mp')]
    all_gather x6 -> x0, waiting for transfers between devices: 411 us -> none  [the longest x1 218 us: fetch_weights(): lax.all_gather(w_gate_up.astype(jnp.bfloat16), 'dp', axis=1, tiled=True)]
    ppermute x0 -> x131, waiting for transfers between devices: none -> 316 us  [the longest x72 192 us: move(): lax.ppermute(value, 'dp', [(p * 2 + s, (p + by) * 2 + s) for p in places...]
    ppermute x0 -> x131, starting transfers between devices: none -> 295 us  [the longest x72 216 us: move(): lax.ppermute(value, 'dp', [(p * 2 + s, (p + by) * 2 + s) for p in places...]
    psum x1 -> x2, blocking collectives: 38.5 us -> 103 us  [the longest x1 55.5 us: body(): totals = lax.psum(jnp.stack(weight_sq + update_sq), ('dp', 'mp'))]
    unnamed x119 -> x261, local copies, waits for them, and re-layouts: 13.4 us -> 71.8 us
    dot_general x35 -> x18, matrix products: 241 us -> 184 us  [the longest x6 70.7 us: dot_nt(): lax.dot_general(left, right, (((1,), (1,)), ((), ())), preferred_element_...]
  transfers between devices with their start and end apart: 16 -> 131, of which waited for: 15 -> 31; matrix products, arithmetic and copies ran while one was open for 10% -> 32% of each run, Pallas kernels for 0% -> 2%
where the time goes in v1:
time: 1380 us; the launch traced here: 1360 us
  waiting for transfers between devices  316 us (23%)
  starting transfers between devices  295 us (21%)
  other arithmetic  184 us (13%)
  matrix products  184 us (13%)
  local copies, waits for them, and re-layouts  182 us (13%)
  blocking collectives  165 us (12%)
  Pallas kernels  24.4 us (2%)
    ppermute x72, starting transfers between devices, move(): lax.ppermute(value, 'dp', [(p * 2 + s, (p + by) * 2 + s) for p in places...  216 us
    ppermute x72, waiting for transfers between devices, move(): lax.ppermute(value, 'dp', [(p * 2 + s, (p + by) * 2 + s) for p in places...  192 us
    ppermute x39, waiting for transfers between devices, swap_side(): lax.ppermute(value, 'dp', [(p * 2 + s, p * 2 + 1 - s) for p in places for...  95.4 us
    unnamed x261, local copies, waits for them, and re-layouts  71.8 us
    dot_general x6, matrix products, dot_nt(): lax.dot_general(left, right, (((1,), (1,)), ((), ())), preferred_element_...  70.7 us
    ppermute x39, starting transfers between devices, swap_side(): lax.ppermute(value, 'dp', [(p * 2 + s, p * 2 + 1 - s) for p in places for...  66.4 us
    psum x1, blocking collectives, body(): totals = lax.psum(jnp.stack(weight_sq + update_sq), ('dp', 'mp'))  55.5 us
    dot_general x6, matrix products, dot_tn(): lax.dot_general(left, right, (((0,), (0,)), ((), ())), preferred_element_...  52.1 us
  transfers between devices with their start and end apart: 131, of which 31 were waited for; matrix products, arithmetic and copies ran while one was open for 32% of the time, Pallas kernels for 2%

profile of v1, /device:TPU:0, one launch (start us, length us, event | category | flops | bytes accessed | tf_op | source)
XLA Modules:
  0.0 1362.0 jit_solution(7522172649342001895)
XLA Ops:
  30.6 24.2 %all_gather.3 = bf16[2,2048]{1,0:T(2,128)(2,1)S(1)} all-gather(bf16[2,256]{1,0:T(2,128)(2,1)S(1)} %get-tuple-element.343), channel_id=1, replica_groups=mesh['dp'=8,'mp'=4] {'dp'}, dimensions={1}, use_global_device_ids=true | all-gather | bytes 9216 | tf_op jit(solution)/shard_map/all_gather | solution.py:399
  222.4 46.1 %collective-permute-done.25 = bf16[64,2048]{1,0:T(8,128)(2,1)S(1)} collective-permute-done((bf16[64,2048]{1,0:T(8,128)(2,1)S(1)}, bf16[64,2048]{1,0:T(8,128)(2,1)S(1)}, u32[]{:S(2)}, u32[]{:S(2)}) %collective-permute-start.25) | collective-permute-done | bytes 262176 | tf_op jit(solution)/shard_map/ppermute | solution.py:184
  282.7 38.5 %pmax.7 = f32[16]{0:T(128)S(1)} all-reduce(f32[16]{0:T(128)S(1)} %dynamic_update_slice.131), channel_id=1, replica_groups=mesh['dp'=8,'mp'=4] {'dp','mp'}, use_global_device_ids=true, to_apply=%region_23.24 | all-reduce | flops 16 | bytes 128 | tf_op jit(solution)/shard_map/pmax | solution.py:511
  404.2 15.5 %collective-permute-done.35 = bf16[512,1024]{0,1:T(8,128)(2,1)S(1)} collective-permute-done((bf16[512,1024]{0,1:T(8,128)(2,1)S(1)}, bf16[512,1024]{0,1:T(8,128)(2,1)S(1)}, u32[]{:S(2)}, u32[]{:S(2)}) %collective-permute-start.35) | collective-permute-done | bytes 1048608 | tf_op jit(solution)/shard_map/ppermute | solution.py:187
  422.5 19.7 %collective-permute-done.48 = bf16[512,1024]{0,1:T(8,128)(2,1)S(1)} collective-permute-done((bf16[512,1024]{0,1:T(8,128)(2,1)S(1)}, bf16[512,1024]{0,1:T(8,128)(2,1)S(1)}, u32[]{:S(2)}, u32[]{:S(2)}) %collective-permute-start.48) | collective-permute-done | bytes 1048608 | tf_op jit(solution)/shard_map/ppermute | solution.py:187
  445.4 29.1 %maximum_maximum_fusion = bf16[1024,2048]{1,0:T(8,128)(2,1)S(1)} fusion(bf16[512,1024]{1,0:T(8,128)(2,1)S(1)} %collective-permute-done.31, bf16[256,1024]{1,0:T(8,128)(2,1)S(1)} %collective-permute-done.30, bf16[256,1024]{1,0:T(8,128)(2,1)S(1)} %get-tuple-element.318, bf16[256,1024]{1,0:T(8,128)(2,1)S(1)} %get-tuple-element.316, ...), kind=kLoop, calls=%fused_computation.17 | loop fusion | flops 29360128 | bytes 8388608 | tf_op jit(solution)/shard_map/concatenate | solution.py:315
  482.3 20.8 %collective-permute-done.36 = bf16[512,1024]{0,1:T(8,128)(2,1)S(1)} collective-permute-done((bf16[512,1024]{0,1:T(8,128)(2,1)S(1)}, bf16[512,1024]{0,1:T(8,128)(2,1)S(1)}, u32[]{:S(2)}, u32[]{:S(2)}) %collective-permute-start.36) | collective-permute-done | bytes 1048608 | tf_op jit(solution)/shard_map/ppermute | solution.py:187
  506.2 19.4 %collective-permute-done.50 = bf16[512,1024]{0,1:T(8,128)(2,1)S(1)} collective-permute-done((bf16[512,1024]{0,1:T(8,128)(2,1)S(1)}, bf16[512,1024]{0,1:T(8,128)(2,1)S(1)}, u32[]{:S(2)}, u32[]{:S(2)}) %collective-permute-start.50) | collective-permute-done | bytes 1048608 | tf_op jit(solution)/shard_map/ppermute | solution.py:187
  526.9 14.5 %collective-permute-done.37 = bf16[512,1024]{0,1:T(8,128)(2,1)S(1)} collective-permute-done((bf16[512,1024]{0,1:T(8,128)(2,1)S(1)}, bf16[512,1024]{0,1:T(8,128)(2,1)S(1)}, u32[]{:S(2)}, u32[]{:S(2)}) %collective-permute-start.37) | collective-permute-done | bytes 1048608 | tf_op jit(solution)/shard_map/ppermute | solution.py:187
  551.9 13.3 fusion.107
  589.0 14.7 %fusion.8 = f32[2048,2048]{1,0:T(8,128)} fusion(bf16[2048,1024]{0,1:T(8,128)(2,1)S(1)} %select_dynamic-update-slice_fusion, bf16[2048,512]{0,1:T(8,128)(2,1)} %get-tuple-element.206, bf16[2048,512]{0,1:T(8,128)(2,1)S(1)} %get-tuple-element.205), kind=kOutput, calls=%fused_computation.51 | convolution fusion | flops 8598323200 | bytes 25165824 | tf_op jit(solution)/shard_map/dot_general | solution.py:50
  627.8 13.7 %fusion.106 = f32[2048,1024]{0,1:T(8,128)} fusion(bf16[2048,2048]{1,0:T(8,128)(2,1)} %slice_dynamic-update-slice_fusion.4, bf16[2048,1024]{0,1:T(8,128)(2,1)S(1)} %select_dynamic-update-slice_fusion.3), kind=kOutput, calls=%fused_computation.389 | convolution fusion | flops 8589934592 | bytes 20971520 | tf_op jit(solution)/shard_map/dot_general | solution.py:449
  676.4 19.1 %fusion.103 = (bf16[2048,2048]{1,0:T(8,128)(2,1)}, f32[2048,2048]{1,0:T(8,128)}) fusion(f32[2048,2048]{1,0:T(8,128)} %fusion.8, bf16[2048,1024]{0,1:T(8,128)(2,1)} %copy-done.42, bf16[2048,512]{0,1:T(8,128)(2,1)} %copy-done.107, bf16[2048,512]{0,1:T(8,128)(2,1)} %copy-done.106), kind=kOutput, calls=%fused_computation.386 | convolution fusion | flops 8606711808 | bytes 50331648 | tf_op jit(solution)/shard_map/dot_general | solution.py:50
  711.5 14.4 %fusion.104 = (bf16[2048,2048]{1,0:T(8,128)(2,1)}, f32[2048,2048]{1,0:T(8,128)}) fusion(f32[2048,2048]{1,0:T(8,128)} %fusion.108, bf16[2048,512]{0,1:T(8,128)(2,1)S(1)} %copy-done.30, bf16[512,2048]{1,0:T(8,128)(2,1)S(1)} %copy-done.19), kind=kOutput, calls=%fused_computation.387 | convolution fusion | flops 4303355904 | bytes 46137344 | tf_op jit(solution)/shard_map/dot_general | solution.py:461
  742.4 32.5 %collective-permute-start.105 = (bf16[512,1024]{0,1:T(8,128)(2,1)S(1)}, bf16[512,1024]{0,1:T(8,128)(2,1)S(1)}, u32[]{:S(2)}, u32[]{:S(2)}) collective-permute-start(bf16[512,1024]{0,1:T(8,128)(2,1)S(1)} %get-tuple-element.224), channel_id=1, source_target_pairs={{0,8},{4,12},{1,9},{5,13},{2,10},{6,14},{3,11},{7,15}} | collective-permute-start | bytes 3145736 | tf_op jit(solution)/shard_map/ppermute | solution.py:187
  787.7 20.6 %collective-permute-done.120 = bf16[128,2048]{1,0:T(8,128)(2,1)S(1)} collective-permute-done((bf16[128,2048]{1,0:T(8,128)(2,1)S(1)}, bf16[128,2048]{1,0:T(8,128)(2,1)S(1)}, u32[]{:S(2)}, u32[]{:S(2)}) %collective-permute-start.120) | collective-permute-done | bytes 524320 | tf_op jit(solution)/shard_map/ppermute | solution.py:187
  818.3 19.9 %collective-permute-start.127 = (bf16[128,2048]{1,0:T(8,128)(2,1)S(1)}, bf16[128,2048]{1,0:T(8,128)(2,1)S(1)}, u32[]{:S(2)}, u32[]{:S(2)}) collective-permute-start(bf16[128,2048]{1,0:T(8,128)(2,1)S(1)} %get-tuple-element.270), channel_id=1, source_target_pairs={{0,8},{4,12},{8,16},{12,20},{16,24},{20,28},{1,9},{5,13},{9,17},{1... | collective-permute-start | bytes 1572872 | tf_op jit(solution)/shard_map/ppermute | solution.py:187
  841.5 26.1 %collective-permute-done.127 = bf16[128,2048]{1,0:T(8,128)(2,1)S(1)} collective-permute-done((bf16[128,2048]{1,0:T(8,128)(2,1)S(1)}, bf16[128,2048]{1,0:T(8,128)(2,1)S(1)}, u32[]{:S(2)}, u32[]{:S(2)}) %collective-permute-start.127) | collective-permute-done | bytes 524320 | tf_op jit(solution)/shard_map/ppermute | solution.py:187
  911.4 13.1 collective-permute-done.69
  924.5 25.3 %collective-permute-start.107 = (bf16[512,1024]{0,1:T(8,128)(2,1)}, bf16[512,1024]{0,1:T(8,128)(2,1)}, u32[]{:S(2)}, u32[]{:S(2)}) collective-permute-start(bf16[512,1024]{0,1:T(8,128)(2,1)} %get-tuple-element.222), channel_id=1, source_target_pairs={{0,8},{4,12},{8,16},{12,20},{16,24},{20,28},{1,9},{5,13},{9,17},{1... | collective-permute-start | bytes 3145736 | tf_op jit(solution)/shard_map/ppermute | solution.py:187
  992.2 13.1 collective-permute-done.110
  1072.0 13.1 attention_backward.1
  1187.7 47.0 %psum.14 = f32[2,2048]{1,0:T(2,128)S(1)} all-reduce(f32[2,2048]{1,0:T(2,128)S(1)} %pad_maximum_fusion.35), channel_id=1, replica_groups=mesh['dp'=8,'mp'=4] {'dp','mp'}, use_global_device_ids=true, to_apply=%region_7.8 | all-reduce | flops 4096 | bytes 32768 | tf_op jit(solution)/shard_map/psum | solution.py:502
  1256.5 55.5 %psum.15 = f32[14]{0:T(128)S(1)} all-reduce(f32[14]{0:T(128)S(1)} %stack.108), channel_id=1, replica_groups=mesh['dp'=8,'mp'=4] {'dp','mp'}, use_global_device_ids=true, to_apply=%region_22.23 | all-reduce | flops 14 | bytes 112 | tf_op jit(solution)/shard_map/psum | solution.py:536
  (749 shorter events, 782.0 us)
Async XLA Ops:
  10.0 65.8 %collective-permute-start.2 = (bf16[256,1024]{1,0:T(8,128)(2,1)}, bf16[256,1024]{1,0:T(8,128)(2,1)}, u32[]{:S(2)}, u32[]{:S(2)}) collective-permute-start(bf16[256,1024]{1,0:T(8,128)(2,1)} %slice_dynamic-update-slice_fusion.14), channel_id=1, source_target_pairs={{8,0},{12,4},{16,8},{20,12},{24,16},{28,20},{9,1},{13,5},{17,9},{2... | collective-permute-start | bytes 1572872 | tf_op jit(solution)/shard_map/ppermute | solution.py:187
  11.3 90.5 %collective-permute-start.1 = (bf16[256,1024]{1,0:T(8,128)(2,1)}, bf16[256,1024]{1,0:T(8,128)(2,1)}, u32[]{:S(2)}, u32[]{:S(2)}) collective-permute-start(bf16[256,1024]{1,0:T(8,128)(2,1)} %slice_dynamic-update-slice_fusion.14), channel_id=1, source_target_pairs={{0,8},{4,12},{8,16},{12,20},{16,24},{20,28},{1,9},{5,13},{9,17},{1... | collective-permute-start | bytes 1572872 | tf_op jit(solution)/shard_map/ppermute | solution.py:187
  17.6 91.6 %collective-permute-start = (bf16[256,1024]{1,0:T(8,128)(2,1)}, bf16[256,1024]{1,0:T(8,128)(2,1)}, u32[]{:S(2)}, u32[]{:S(2)}) collective-permute-start(bf16[256,1024]{1,0:T(8,128)(2,1)} %slice_dynamic-update-slice_fusion.14), channel_id=1, source_target_pairs={{0,4},{4,0},{8,12},{12,8},{16,20},{20,16},{24,28},{28,24},{1,5},{5... | collective-permute-start | bytes 1572872 | tf_op jit(solution)/shard_map/ppermute | solution.py:184
  26.8 251.6 %collective-permute-start.33 = (bf16[256,1024]{0,1:T(8,128)(2,1)}, bf16[256,1024]{0,1:T(8,128)(2,1)}, u32[]{:S(2)}, u32[]{:S(2)}) collective-permute-start(bf16[256,1024]{0,1:T(8,128)(2,1)} %pad_maximum_fusion.28), channel_id=1, source_target_pairs={{0,4},{4,0},{8,12},{12,8},{16,20},{20,16},{24,28},{28,24},{1,5},{5... | collective-permute-start | bytes 1572872 | tf_op jit(solution)/shard_map/ppermute | solution.py:184
  140.1 141.1 %collective-permute-start.46 = (bf16[256,1024]{0,1:T(8,128)(2,1)}, bf16[256,1024]{0,1:T(8,128)(2,1)}, u32[]{:S(2)}, u32[]{:S(2)}) collective-permute-start(bf16[256,1024]{0,1:T(8,128)(2,1)} %pad_maximum_fusion.29), channel_id=1, source_target_pairs={{0,4},{4,0},{8,12},{12,8},{16,20},{20,16},{24,28},{28,24},{1,5},{5... | collective-permute-start | bytes 1572872 | tf_op jit(solution)/shard_map/ppermute | solution.py:184
  217.4 104.6 %collective-permute-start.66 = (bf16[512,2048]{1,0:T(8,128)(2,1)}, bf16[512,2048]{1,0:T(8,128)(2,1)}, u32[]{:S(2)}, u32[]{:S(2)}) collective-permute-start(bf16[512,2048]{1,0:T(8,128)(2,1)} %pad_maximum_fusion.12), channel_id=1, source_target_pairs={{0,4},{4,0},{8,12},{12,8},{16,20},{20,16},{24,28},{28,24},{1,5},{5... | collective-permute-start | bytes 6291464 | tf_op jit(solution)/shard_map/ppermute | solution.py:184
  399.6 74.8 %collective-permute-start.47 = (bf16[512,1024]{0,1:T(8,128)(2,1)S(1)}, bf16[512,1024]{0,1:T(8,128)(2,1)S(1)}, u32[]{:S(2)}, u32[]{:S(2)}) collective-permute-start(bf16[512,1024]{0,1:T(8,128)(2,1)S(1)} %maximum_select_fusion.1), channel_id=1, source_target_pairs={{0,8},{4,12},{8,16},{12,20},{16,24},{20,28},{1,9},{5,13},{9,17},{1... | collective-permute-start | bytes 3145736 | tf_op jit(solution)/shard_map/ppermute | solution.py:187
  419.7 57.3 %collective-permute-start.45 = (bf16[128,2048]{1,0:T(8,128)(2,1)}, bf16[128,2048]{1,0:T(8,128)(2,1)}, u32[]{:S(2)}, u32[]{:S(2)}) collective-permute-start(bf16[128,2048]{1,0:T(8,128)(2,1)} %collective-permute-done.44), channel_id=1, source_target_pairs={{16,24},{20,28},{17,25},{21,29},{18,26},{22,30},{19,27},{23,31}} | collective-permute-start | bytes 1572872 | tf_op jit(solution)/shard_map/ppermute | solution.py:187
  475.8 68.3 %collective-permute-start.32 = (bf16[1024,2048]{1,0:T(8,128)(2,1)S(1)}, bf16[1024,2048]{1,0:T(8,128)(2,1)S(1)}, u32[]{:S(2)}, u32[]{:S(2)}) collective-permute-start(bf16[1024,2048]{1,0:T(8,128)(2,1)S(1)} %maximum_maximum_fusion), channel_id=1, source_target_pairs={{0,1},{1,0},{2,3},{3,2},{4,5},{5,4},{6,7},{7,6},{8,9},{9,8},{10,11... | collective-permute-start | bytes 12582920 | tf_op jit(solution)/shard_map/ppermute | solution.py:180
  621.0 116.8 %collective-permute-start.125 = (bf16[128,2048]{1,0:T(8,128)(2,1)}, bf16[128,2048]{1,0:T(8,128)(2,1)S(1)}, u32[]{:S(2)}, u32[]{:S(2)}) collective-permute-start(bf16[128,2048]{1,0:T(8,128)(2,1)} %get-tuple-element.272), channel_id=1, source_target_pairs={{0,8},{4,12},{1,9},{5,13},{2,10},{6,14},{3,11},{7,15}} | collective-permute-start | bytes 1572872 | tf_op jit(solution)/shard_map/ppermute | solution.py:187
  622.5 119.9 %collective-permute-start.128 = (bf16[128,2048]{1,0:T(8,128)(2,1)}, bf16[128,2048]{1,0:T(8,128)(2,1)}, u32[]{:S(2)}, u32[]{:S(2)}) collective-permute-start(bf16[128,2048]{1,0:T(8,128)(2,1)} %get-tuple-element.273), channel_id=1, source_target_pairs={{24,16},{28,20},{25,17},{29,21},{26,18},{30,22},{27,19},{31,23}} | collective-permute-start | bytes 1572872 | tf_op jit(solution)/shard_map/ppermute | solution.py:187
  625.5 150.2 %collective-permute-start.112 = (bf16[512,1024]{0,1:T(8,128)(2,1)}, bf16[512,1024]{0,1:T(8,128)(2,1)}, u32[]{:S(2)}, u32[]{:S(2)}) collective-permute-start(bf16[512,1024]{0,1:T(8,128)(2,1)} %get-tuple-element.228), channel_id=1, source_target_pairs={{0,8},{4,12},{1,9},{5,13},{2,10},{6,14},{3,11},{7,15}} | collective-permute-start | bytes 3145736 | tf_op jit(solution)/shard_map/ppermute | solution.py:187
  702.8 72.1 %collective-permute-start.122 = (bf16[128,2048]{1,0:T(8,128)(2,1)}, bf16[128,2048]{1,0:T(8,128)(2,1)}, u32[]{:S(2)}, u32[]{:S(2)}) collective-permute-start(bf16[128,2048]{1,0:T(8,128)(2,1)} %get-tuple-element.269), channel_id=1, source_target_pairs={{24,16},{28,20},{25,17},{29,21},{26,18},{30,22},{27,19},{31,23}} | collective-permute-start | bytes 1572872 | tf_op jit(solution)/shard_map/ppermute | solution.py:187
  742.4 72.0 %collective-permute-start.105 = (bf16[512,1024]{0,1:T(8,128)(2,1)S(1)}, bf16[512,1024]{0,1:T(8,128)(2,1)S(1)}, u32[]{:S(2)}, u32[]{:S(2)}) collective-permute-start(bf16[512,1024]{0,1:T(8,128)(2,1)S(1)} %get-tuple-element.224), channel_id=1, source_target_pairs={{0,8},{4,12},{1,9},{5,13},{2,10},{6,14},{3,11},{7,15}} | collective-permute-start | bytes 3145736 | tf_op jit(solution)/shard_map/ppermute | solution.py:187
  775.7 115.0 %collective-permute-start.68 = (bf16[1024,2048]{1,0:T(8,128)(2,1)S(1)}, bf16[1024,2048]{1,0:T(8,128)(2,1)S(1)}, u32[]{:S(2)}, u32[]{:S(2)}) collective-permute-start(bf16[1024,2048]{1,0:T(8,128)(2,1)S(1)} %pad_maximum_fusion.4), channel_id=1, source_target_pairs={{0,1},{1,0},{2,3},{3,2},{4,5},{5,4},{6,7},{7,6},{8,9},{9,8},{10,11... | collective-permute-start | bytes 12582920 | tf_op jit(solution)/shard_map/ppermute | solution.py:180
  814.4 86.3 %collective-permute-start.59 = (bf16[1024,2048]{1,0:T(8,128)(2,1)}, bf16[1024,2048]{1,0:T(8,128)(2,1)}, u32[]{:S(2)}, u32[]{:S(2)}) collective-permute-start(bf16[1024,2048]{1,0:T(8,128)(2,1)} %pad_maximum_fusion), channel_id=1, source_target_pairs={{0,1},{1,0},{2,3},{3,2},{4,5},{5,4},{6,7},{7,6},{8,9},{9,8},{10,11... | collective-permute-start | bytes 12582920 | tf_op jit(solution)/shard_map/ppermute | solution.py:180
  815.6 57.8 %collective-permute-start.106 = (bf16[512,1024]{0,1:T(8,128)(2,1)S(1)}, bf16[512,1024]{0,1:T(8,128)(2,1)S(1)}, u32[]{:S(2)}, u32[]{:S(2)}) collective-permute-start(bf16[512,1024]{0,1:T(8,128)(2,1)S(1)} %add_convert_fusion.7), channel_id=1, source_target_pairs={{0,8},{4,12},{8,16},{12,20},{1,9},{5,13},{9,17},{13,21},{2,10},{6,... | collective-permute-start | bytes 3145736 | tf_op jit(solution)/shard_map/ppermute | solution.py:187
  881.1 108.0 %collective-permute-start.114 = (bf16[512,1024]{0,1:T(8,128)(2,1)}, bf16[512,1024]{0,1:T(8,128)(2,1)}, u32[]{:S(2)}, u32[]{:S(2)}) collective-permute-start(bf16[512,1024]{0,1:T(8,128)(2,1)} %get-tuple-element.226), channel_id=1, source_target_pairs={{0,8},{4,12},{8,16},{12,20},{16,24},{20,28},{1,9},{5,13},{9,17},{1... | collective-permute-start | bytes 3145736 | tf_op jit(solution)/shard_map/ppermute | solution.py:187
  924.5 67.7 %collective-permute-start.107 = (bf16[512,1024]{0,1:T(8,128)(2,1)}, bf16[512,1024]{0,1:T(8,128)(2,1)}, u32[]{:S(2)}, u32[]{:S(2)}) collective-permute-start(bf16[512,1024]{0,1:T(8,128)(2,1)} %get-tuple-element.222), channel_id=1, source_target_pairs={{0,8},{4,12},{8,16},{12,20},{16,24},{20,28},{1,9},{5,13},{9,17},{1... | collective-permute-start | bytes 3145736 | tf_op jit(solution)/shard_map/ppermute | solution.py:187
  1059.2 67.0 %collective-permute-start.101 = (bf16[64,2048]{1,0:T(8,128)(2,1)}, bf16[64,2048]{1,0:T(8,128)(2,1)S(1)}, u32[]{:S(2)}, u32[]{:S(2)}) collective-permute-start(bf16[64,2048]{1,0:T(8,128)(2,1)} %get-tuple-element.275), channel_id=1, source_target_pairs={{24,28},{28,24},{25,29},{29,25},{26,30},{30,26},{27,31},{31,27}} | collective-permute-start | bytes 786440 | tf_op jit(solution)/shard_map/ppermute | solution.py:184
  1059.9 71.8 %collective-permute-start.100 = (bf16[64,2048]{1,0:T(8,128)(2,1)}, bf16[64,2048]{1,0:T(8,128)(2,1)S(1)}, u32[]{:S(2)}, u32[]{:S(2)}) collective-permute-start(bf16[64,2048]{1,0:T(8,128)(2,1)} %get-tuple-element.276), channel_id=1, source_target_pairs={{16,20},{20,16},{24,28},{28,24},{17,21},{21,17},{25,29},{29,25},{1... | collective-permute-start | bytes 786440 | tf_op jit(solution)/shard_map/ppermute | solution.py:184
  1169.1 70.5 %collective-permute-start.79 = (bf16[256,1024]{0,1:T(8,128)(2,1)}, bf16[256,1024]{0,1:T(8,128)(2,1)}, u32[]{:S(2)}, u32[]{:S(2)}) collective-permute-start(bf16[256,1024]{0,1:T(8,128)(2,1)} %get-tuple-element.230), channel_id=1, source_target_pairs={{0,4},{4,0},{8,12},{12,8},{16,20},{20,16},{24,28},{28,24},{1,5},{5... | collective-permute-start | bytes 1572872 | tf_op jit(solution)/shard_map/ppermute | solution.py:184
  1171.9 67.6 %collective-permute-start.85 = (bf16[256,1024]{0,1:T(8,128)(2,1)}, bf16[256,1024]{0,1:T(8,128)(2,1)}, u32[]{:S(2)}, u32[]{:S(2)}) collective-permute-start(bf16[256,1024]{0,1:T(8,128)(2,1)} %get-tuple-element.237), channel_id=1, source_target_pairs={{0,8},{4,12},{8,16},{12,20},{16,24},{20,28},{1,9},{5,13},{9,17},{1... | collective-permute-start | bytes 1572872 | tf_op jit(solution)/shard_map/ppermute | solution.py:187
  1254.1 66.7 %collective-permute-start.77 = (bf16[256,2048]{1,0:T(8,128)(2,1)S(1)}, bf16[256,2048]{1,0:T(8,128)(2,1)S(1)}, u32[]{:S(2)}, u32[]{:S(2)}) collective-permute-start(bf16[256,2048]{1,0:T(8,128)(2,1)S(1)} %fusion.16), channel_id=1, source_target_pairs={{0,2},{1,3},{2,0},{3,1},{4,6},{5,7},{6,4},{7,5},{8,10},{9,11},{10,... | collective-permute-start | bytes 3145736 | tf_op jit(solution)/shard_map/ppermute | solution.py:180
  (217 other events, 5281.8 us)

commit v2 on v1

--- a/solution.py
+++ b/solution.py
@@ -170,100 +170,627 @@
     )(rotated, grads, lse, cosine, sine, segments.reshape(count, 1, length), segments.reshape(rows, 1))
 
 
+MESH = pl.DeviceIdType.MESH
+WHOLE = pl.BlockSpec(memory_space=pltpu.VMEM)
+CHUNKS = 4
+
+
+def greet(partners):
+    barrier = pltpu.get_barrier_semaphore()
+    for partner in partners:
+        pl.semaphore_signal(barrier, inc=1, device_id=partner, device_id_type=MESH)
+    pl.semaphore_wait(barrier, len(partners))
+
+
+def sender(send_sems, recv_sems, log):
+    def copy(kind, chunk, source, target, device):
+        made = pltpu.make_async_remote_copy(
+            src_ref=source,
+            dst_ref=target,
+            send_sem=send_sems.at[kind, chunk],
+            recv_sem=recv_sems.at[kind, chunk],
+            device_id=device,
+            device_id_type=MESH,
+        )
+        log.append(made)
+        return made
+
+    return copy
+
+
+def partners_of():
+    rank, index = lax.axis_index("mp"), lax.axis_index("dp")
+    return {"mp": rank ^ 1}, {"mp": rank ^ 2}, {"dp": index ^ 1}
+
+
+def spread_forward(part_ref, tokens_ref, gain_ref, rows_ref, middle_ref, near_ref, out_ref, far_ref, send_sems, recv_sems):
+    core, far, pair = partners_of()
+    quarter, _ = tokens_ref.shape
+    size = quarter // CHUNKS
+    at = lambda slot, i: pl.ds(slot * quarter + i * size, size)
+    greet([core, far, pair])
+    log = []
+    copy = sender(send_sems, recv_sems, log)
+    near = {}
+    for i in range(CHUNKS):
+        for k in range(2):
+            near[k, i] = copy(k, i, part_ref.at[at(2 * k + 1, i)], near_ref.at[at(k, i)], core)
+            near[k, i].start()
+    sums = {}
+    for i in range(CHUNKS):
+        near[1, i].wait_recv()
+        total = part_ref[at(2, i), :].astype(F32) + near_ref[at(1, i), :].astype(F32)
+        out_ref[at(0, i), :] = total.astype(BF16)
+        sums[i] = copy(2, i, out_ref.at[at(0, i)], far_ref.at[at(0, i)], far)
+        sums[i].start()
+    moves = {}
+    for i in range(CHUNKS + 2):
+        if i < CHUNKS:
+            near[0, i].wait_recv()
+            sums[i].wait_recv()
+            middle = tokens_ref[at(0, i), :].astype(F32) + (
+                part_ref[at(0, i), :].astype(F32)
+                + near_ref[at(0, i), :].astype(F32)
+                + far_ref[at(0, i), :].astype(F32)
+            )
+            middle_ref[at(0, i), :] = middle
+            rows_ref[at(0, i), :] = (middle * inverse_rms(middle) * gain_ref[0:1, :]).astype(BF16)
+            own = rows_ref.at[at(0, i)]
+            for kind, slot, device in ((3, 2, far), (4, 4, pair), (6, 1, core)):
+                moves[kind, i] = copy(kind, i, own, rows_ref.at[at(slot, i)], device)
+                moves[kind, i].start()
+        j = i - 1
+        if 0 <= j < CHUNKS:
+            moves[3, j].wait_recv()
+            for kind, slot, device in ((5, 6, pair), (7, 3, core)):
+                moves[kind, j] = copy(kind, j, rows_ref.at[at(2, j)], rows_ref.at[at(slot, j)], device)
+                moves[kind, j].start()
+            moves[4, j].wait_recv()
+            moves[8, j] = copy(8, j, rows_ref.at[at(4, j)], rows_ref.at[at(5, j)], core)
+            moves[8, j].start()
+        j = i - 2
+        if 0 <= j < CHUNKS:
+            moves[5, j].wait_recv()
+            moves[9, j] = copy(9, j, rows_ref.at[at(6, j)], rows_ref.at[at(7, j)], core)
+            moves[9, j].start()
+    for i in range(CHUNKS):
+        for kind in (6, 7, 8, 9):
+            moves[kind, i].wait_recv()
+    for made in log:
+        made.wait_send()
+
+
+def call_spread_forward(part, tokens_own, gain):
+    quarter, width = tokens_own.shape
+    return pl.pallas_call(
+        spread_forward,
+        in_specs=[WHOLE] * 3,
+        out_specs=[WHOLE] * 2,
+        out_shape=[
+            jax.ShapeDtypeStruct((8 * quarter, width), BF16),
+            jax.ShapeDtypeStruct((quarter, width), F32),
+        ],
+        scratch_shapes=[
+            pltpu.VMEM((2 * quarter, width), BF16),
+            pltpu.VMEM((quarter, width), BF16),
+            pltpu.VMEM((quarter, width), BF16),
+            pltpu.SemaphoreType.DMA((10, CHUNKS)),
+            pltpu.SemaphoreType.DMA((10, CHUNKS)),
+        ],
+        compiler_params=pltpu.CompilerParams(
+            collective_id=1, has_side_effects=True, vmem_limit_bytes=50 * 2**20
+        ),
+        name="spread_forward",
+    )(part, tokens_own, gain)
+
+
+def pull_chunk(values, scale_gain, grad):
+    scale = inverse_rms(values)
+    turned = grad * scale_gain
+    inner = jnp.mean(turned * values, -1, keepdims=True)
+    return scale * turned - (scale * scale * scale) * values * inner, grad * values * scale
+
+
+def spread_backward(part_ref, middle_ref, grad_ref, gain_ref, rows_ref, total_ref, gain_out_ref, near_ref, side_out_ref, side_in_ref, far_out_ref, far_in_ref, send_sems, recv_sems):
+    core, far, pair = partners_of()
+    quarter, width = middle_ref.shape
+    size = quarter // CHUNKS
+    at = lambda slot, i: pl.ds(slot * quarter + i * size, size)
+    greet([core, far, pair])
+    log = []
+    copy = sender(send_sems, recv_sems, log)
+    near, side, sums, moves = {}, {}, {}, {}
+    for i in range(CHUNKS):
+        for k in (2, 3, 0, 1):
+            near[k, i] = copy(k, i, part_ref.at[at(2 * k + 1, i)], near_ref.at[at(k, i)], core)
+            near[k, i].start()
+
+    def pairs(k, i):
+        return part_ref[at(2 * k, i), :].astype(F32) + near_ref[at(k, i), :].astype(F32)
+
+    for i in range(CHUNKS):
+        for k in (1, 0):
+            near[2 + k, i].wait_recv()
+            side_out_ref[at(k, i), :] = pairs(2 + k, i).astype(BF16)
+            side[k, i] = copy(4 + k, i, side_out_ref.at[at(k, i)], side_in_ref.at[at(k, i)], pair)
+            side[k, i].start()
+    gain_sum = jnp.zeros((1, width), F32)
+    for i in range(CHUNKS + 2):
+        if i < CHUNKS:
+            near[1, i].wait_recv()
+            side[1, i].wait_recv()
+            far_out_ref[at(0, i), :] = (pairs(1, i) + side_in_ref[at(1, i), :].astype(F32)).astype(BF16)
+            sums[i] = copy(6, i, far_out_ref.at[at(0, i)], far_in_ref.at[at(0, i)], far)
+            sums[i].start()
+        j = i - 1
+        if 0 <= j < CHUNKS:
+            near[0, j].wait_recv()
+            side[0, j].wait_recv()
+            sums[j].wait_recv()
+            grad = pairs(0, j) + side_in_ref[at(0, j), :].astype(F32) + far_in_ref[at(0, j), :].astype(F32)
+            back, gain_part = pull_chunk(middle_ref[at(0, j), :], gain_ref[0:1, :], grad)
+            gain_sum = gain_sum + jnp.sum(gain_part, 0, keepdims=True)
+            total = grad_ref[at(0, j), :].astype(F32) + back
+            total_ref[at(0, j), :] = total
+            rows_ref[at(0, j), :] = total.astype(BF16)
+            own = rows_ref.at[at(0, j)]
+            for kind, slot, device in ((7, 2, far), (8, 1, core)):
+                moves[kind, j] = copy(kind, j, own, rows_ref.at[at(slot, j)], device)
+                moves[kind, j].start()
+        j = i - 2
+        if 0 <= j < CHUNKS:
+            moves[7, j].wait_recv()
+            moves[9, j] = copy(9, j, rows_ref.at[at(2, j)], rows_ref.at[at(3, j)], core)
+            moves[9, j].start()
+    gain_out_ref[...] = jnp.broadcast_to(gain_sum, gain_out_ref.shape)
+    for i in range(CHUNKS):
+        for kind in (8, 9):
+            moves[kind, i].wait_recv()
+    for made in log:
+        made.wait_send()
+
+
+def call_spread_backward(part, middle, grad_own, gain):
+    quarter, width = middle.shape
+    return pl.pallas_call(
+        spread_backward,
+        in_specs=[WHOLE] * 4,
+        out_specs=[WHOLE] * 3,
+        out_shape=[
+            jax.ShapeDtypeStruct((4 * quarter, width), BF16),
+            jax.ShapeDtypeStruct((quarter, width), F32),
+            jax.ShapeDtypeStruct((8, width), F32),
+        ],
+        scratch_shapes=[
+            pltpu.VMEM((4 * quarter, width), BF16),
+            pltpu.VMEM((2 * quarter, width), BF16),
+            pltpu.VMEM((2 * quarter, width), BF16),
+            pltpu.VMEM((quarter, width), BF16),
+            pltpu.VMEM((quarter, width), BF16),
+            pltpu.SemaphoreType.DMA((10, CHUNKS)),
+            pltpu.SemaphoreType.DMA((10, CHUNKS)),
+        ],
+        compiler_params=pltpu.CompilerParams(
+            collective_id=2, has_side_effects=True, vmem_limit_bytes=56 * 2**20
+        ),
+        name="spread_backward",
+    )(part, middle, grad_own, gain)
+
+
+def finish(line, part_ref, tokens_ref, total_ref, gain_ref, grads_ref, rows_ref, gain_out_ref, owned_ref, near_ref, far_out_ref, far_in_ref, side_in_ref, up_out_ref, up_in_ref, down_out_ref, down_in_ref, send_sems, recv_sems, side_send, side_recv, line_send, line_recv):
+    core, far, pair = partners_of()
+    index = lax.axis_index("dp")
+    place, side = index // 2, index % 2
+    above, below = {"dp": index + 2}, {"dp": index - 2}
+    quarter, width = tokens_ref.shape
+    size = quarter // CHUNKS
+    shard = owned_ref.shape[0]
+    last = line - 1
+    at = lambda slot, i: pl.ds(slot * quarter + i * size, size)
+    block = lambda where, which: pl.ds((where * 2 + which) * shard, shard)
+
+    barrier = pltpu.get_barrier_semaphore()
+    for partner in (core, far, pair):
+        pl.semaphore_signal(barrier, inc=1, device_id=partner, device_id_type=MESH)
+
+    @pl.when(place < last)
+    def _():
+        pl.semaphore_signal(barrier, inc=1, device_id=above, device_id_type=MESH)
+
+    @pl.when(place > 0)
+    def _():
+        pl.semaphore_signal(barrier, inc=1, device_id=below, device_id_type=MESH)
+
+    pl.semaphore_wait(barrier, 3 + (place < last).astype(jnp.int32) + (place > 0).astype(jnp.int32))
+
+    log = []
+    copy = sender(send_sems, recv_sems, log)
+    near, sums, moves = {}, {}, {}
+    for i in range(CHUNKS):
+        for k in (1, 0):
+            near[k, i] = copy(k, i, part_ref.at[at(2 * k + 1, i)], near_ref.at[at(k, i)], core)
+            near[k, i].start()
+
+    def side_copy(where):
+        return pltpu.make_async_remote_copy(
+            src_ref=grads_ref.at[block(where, 1 - side)],
+            dst_ref=side_in_ref.at[where],
+            send_sem=side_send.at[where],
+            recv_sem=side_recv.at[where],
+            device_id=pair,
+            device_id_type=MESH,
+        )
+
+    def line_copy(upward, step):
+        out_ref, in_ref = (up_out_ref, up_in_ref) if upward else (down_out_ref, down_in_ref)
+        way = 0 if upward else 1
+        return pltpu.make_async_remote_copy(
+            src_ref=out_ref.at[step - 1],
+            dst_ref=in_ref.at[step - 1],
+            send_sem=line_send.at[way, step - 1],
+            recv_sem=line_recv.at[way, step - 1],
+            device_id=above if upward else below,
+            device_id_type=MESH,
+        )
+
+    for step in range(last, 0, -1):
+
+        @pl.when(place + step <= last)
+        def _(step=step):
+            side_copy(place + step).start()
+
+        @pl.when(place - step >= 0)
+        def _(step=step):
+            side_copy(place - step).start()
+
+    side_copy(place).start()
+
+    for i in range(CHUNKS):
+        near[1, i].wait_recv()
+        summed = part_ref[at(2, i), :].astype(F32) + near_ref[at(1, i), :].astype(F32)
+        far_out_ref[at(0, i), :] = summed.astype(BF16)
+        sums[i] = copy(2, i, far_out_ref.at[at(0, i)], far_in_ref.at[at(0, i)], far)
+        sums[i].start()
+
+    def term(where):
+        return grads_ref[block(where, side), :].astype(F32) + side_in_ref[where].astype(F32)
+
+    def line_step(step):
+        @pl.when(place + step <= last)
+        def _():
+            side_copy(place + step).wait_recv()
+            value = term(place + step)
+
+            up_out_ref[step - 1] = value.astype(BF16)
+            if step < last:
+
+                @pl.when(place > 0)
+                def _():
+                    line_copy(True, step + 1).wait_recv()
+                    up_out_ref[step - 1] = (value + up_in_ref[step].astype(F32)).astype(BF16)
+
+            line_copy(True, step).start()
+
+        @pl.when(place - step >= 0)
+        def _():
+            side_copy(place - step).wait_recv()
+            value = term(place - step)
+
+            down_out_ref[step - 1] = value.astype(BF16)
+            if step < last:
+
+                @pl.when(place < last)
+                def _():
+                    line_copy(False, step + 1).wait_recv()
+                    down_out_ref[step - 1] = (value + down_in_ref[step].astype(F32)).astype(BF16)
+
+            line_copy(False, step).start()
+
+    gain_sum = jnp.zeros((1, width), F32)
+    steps = list(range(last, 0, -1))
+    for i in range(CHUNKS + 1):
+        if i < CHUNKS:
+            near[0, i].wait_recv()
+            sums[i].wait_recv()
+            grad = (
+                part_ref[at(0, i), :].astype(F32)
+                + near_ref[at(0, i), :].astype(F32)
+                + far_in_ref[at(0, i), :].astype(F32)
+            )
+            back, gain_part = pull_chunk(tokens_ref[at(0, i), :].astype(F32), gain_ref[0:1, :], grad)
+            gain_sum = gain_sum + jnp.sum(gain_part, 0, keepdims=True)
+            rows_ref[at(0, i), :] = (total_ref[at(0, i), :] + back).astype(BF16)
+            own = rows_ref.at[at(0, i)]
+            for kind, slot, device in ((3, 2, far), (4, 1, core)):
+                moves[kind, i] = copy(kind, i, own, rows_ref.at[at(slot, i)], device)
+                moves[kind, i].start()
+        if steps:
+            line_step(steps.pop(0))
+        j = i - 1
+        if 0 <= j < CHUNKS:
+            moves[3, j].wait_recv()
+            moves[5, j] = copy(5, j, rows_ref.at[at(2, j)], rows_ref.at[at(3, j)], core)
+            moves[5, j].start()
+    while steps:
+        line_step(steps.pop(0))
+    gain_out_ref[...] = jnp.broadcast_to(gain_sum, gain_out_ref.shape)
+
+    side_copy(place).wait_recv()
+    owned_ref[...] = term(place)
+
+    @pl.when(place > 0)
+    def _():
+        line_copy(True, 1).wait_recv()
+        owned_ref[...] += up_in_ref[0].astype(F32)
+
+    @pl.when(place < last)
+    def _():
+        line_copy(False, 1).wait_recv()
+        owned_ref[...] += down_in_ref[0].astype(F32)
+
+    for i in range(CHUNKS):
+        for kind in (4, 5):
+            moves[kind, i].wait_recv()
+    for made in log:
+        made.wait_send()
+    for where in range(line):
+        side_copy(where).wait_send()
+    for step in range(last, 0, -1):
+
+        @pl.when(place + step <= last)
+        def _(step=step):
+            line_copy(True, step).wait_send()
+
+        @pl.when(place - step >= 0)
+        def _(step=step):
+            line_copy(False, step).wait_send()
+
+
+def call_finish(dp_size, part, tokens_own, total, gain, grads):
+    quarter, width = tokens_own.shape
+    line = dp_size // 2
+    shard, columns = grads.shape[0] // dp_size, grads.shape[1]
+    hops = pltpu.VMEM((line - 1, shard, columns), BF16)
+    return pl.pallas_call(
+        functools.partial(finish, line),
+        in_specs=[WHOLE] * 5,
+        out_specs=[WHOLE] * 3,
+        out_shape=[
+            jax.ShapeDtypeStruct((4 * quarter, width), BF16),
+            jax.ShapeDtypeStruct((8, width), F32),
+            jax.ShapeDtypeStruct((shard, columns), F32),
+        ],
+        scratch_shapes=[
+            pltpu.VMEM((2 * quarter, width), BF16),
+            pltpu.VMEM((quarter, width), BF16),
+            pltpu.VMEM((quarter, width), BF16),
+            pltpu.VMEM((line, shard, columns), BF16),
+            hops,
+            hops,
+            hops,
+            hops,
+            pltpu.SemaphoreType.DMA((6, CHUNKS)),
+            pltpu.SemaphoreType.DMA((6, CHUNKS)),
+            pltpu.SemaphoreType.DMA((line,)),
+            pltpu.SemaphoreType.DMA((line,)),
+            pltpu.SemaphoreType.DMA((2, line)),
+            pltpu.SemaphoreType.DMA((2, line)),
+        ],
+        compiler_params=pltpu.CompilerParams(
+            collective_id=3, has_side_effects=True, vmem_limit_bytes=50 * 2**20
+        ),
+        name="finish",
+    )(part, tokens_own, total, gain, grads)
+
+
+def gather_weights(line, own_ref, gains_ref, full_ref, gains_full_ref, local_sems, side_send, side_recv, line_send, line_recv):
+    index = lax.axis_index("dp")
+    place, side = index // 2, index % 2
+    pair, above, below = {"dp": index ^ 1}, {"dp": index + 2}, {"dp": index - 2}
+    last = line - 1
+    shard = own_ref.shape[0]
+    block = lambda where, which: pl.ds((where * 2 + which) * shard, shard)
+
+    barrier = pltpu.get_barrier_semaphore()
+    pl.semaphore_signal(barrier, inc=1, device_id=pair, device_id_type=MESH)
+
+    @pl.when(place < last)
+    def _():
+        pl.semaphore_signal(barrier, inc=1, device_id=above, device_id_type=MESH)
+
+    @pl.when(place > 0)
+    def _():
+        pl.semaphore_signal(barrier, inc=1, device_id=below, device_id_type=MESH)
+
+    pl.semaphore_wait(barrier, 1 + (place < last).astype(jnp.int32) + (place > 0).astype(jnp.int32))
+
+    def views(which, where):
+        if which == 0:
+            return full_ref.at[block(where, side)]
+        return gains_full_ref.at[where * 2 + side]
+
+    def source(which, where, first):
+        if first:
+            return own_ref if which == 0 else gains_ref
+        return views(which, where)
+
+    def line_copy(which, upward, where, first=False):
+        way = 0 if upward else 1
+        return pltpu.make_async_remote_copy(
+            src_ref=source(which, where, first),
+            dst_ref=views(which, where),
+            send_sem=line_send.at[which, way, where],
+            recv_sem=line_recv.at[which, way, where],
+            device_id=above if upward else below,
+            device_id_type=MESH,
+        )
+
+    def side_copy(which, where, first=False):
+        return pltpu.make_async_remote_copy(
+            src_ref=source(which, where, first),
+            dst_ref=views(which, where),
+            send_sem=side_send.at[which, where],
+            recv_sem=side_recv.at[which, where],
+            device_id=pair,
+            device_id_type=MESH,
+        )
+
+    def side_arrival(which, where):
+        target = full_ref.at[block(where, 1 - side)] if which == 0 else gains_full_ref.at[where * 2 + 1 - side]
+        return pltpu.make_async_remote_copy(
+            src_ref=target,
+            dst_ref=target,
+            send_sem=side_send.at[which, where],
+            recv_sem=side_recv.at[which, where],
+            device_id=pair,
+            device_id_type=MESH,
+        )
+
+    @pl.when(place < last)
+    def _():
+        for which in (0, 1):
+            line_copy(which, True, place, True).start()
+
+    @pl.when(place > 0)
+    def _():
+        for which in (0, 1):
+            line_copy(which, False, place, True).start()
+
+    for which in (0, 1):
+        side_copy(which, place, True).start()
+    here = [pltpu.make_async_copy(source(w, place, True), views(w, place), local_sems.at[w]) for w in (0, 1)]
+    for made in here:
+        made.start()
+
+    for step in range(1, line):
+
+        @pl.when(place - step >= 0)
+        def _(step=step):
+            where = place - step
+            for which in (0, 1):
+                line_copy(which, True, where).wait_recv()
+
+                @pl.when(place < last)
+                def _(which=which):
+                    line_copy(which, True, where).start()
+
+                side_copy(which, where).start()
+
+        @pl.when(place + step <= last)
+        def _(step=step):
+            where = place + step
+            for which in (0, 1):
+                line_copy(which, False, where).wait_recv()
+
+                @pl.when(place > 0)
+                def _(which=which):
+                    line_copy(which, False, where).start()
+
+                side_copy(which, where).start()
+
+    for made in here:
+        made.wait()
+    for where in range(line):
+        for which in (0, 1):
+            side_arrival(which, where).wait_recv()
+            side_copy(which, where).wait_send()
+
+            @pl.when((where <= place) & (place < last))
+            def _(which=which, where=where):
+                line_copy(which, True, where).wait_send()
+
+            @pl.when((where >= place) & (place > 0))
+            def _(which=which, where=where):
+                line_copy(which, False, where).wait_send()
+
+
+def call_gather_weights(dp_size, own, gains):
+    line = dp_size // 2
+    hbm = pl.BlockSpec(memory_space=pl.ANY)
+    return pl.pallas_call(
+        functools.partial(gather_weights, line),
+        in_specs=[hbm] * 2,
+        out_specs=[hbm] * 2,
+        out_shape=[
+            jax.ShapeDtypeStruct((dp_size * own.shape[0], own.shape[1]), own.dtype),
+            jax.ShapeDtypeStruct((dp_size, *gains.shape), gains.dtype),
+        ],
+        scratch_shapes=[
+            pltpu.SemaphoreType.DMA((2,)),
+            pltpu.SemaphoreType.DMA((2, line)),
+            pltpu.SemaphoreType.DMA((2, line)),
+            pltpu.SemaphoreType.DMA((2, 2, line)),
+            pltpu.SemaphoreType.DMA((2, 2, line)),
+        ],
+        compiler_params=pltpu.CompilerParams(collective_id=4, has_side_effects=True),
+        name="gather_weights",
+    )(own, gains)
+
+
+def combine_all(line, sum_rows, value_ref, out_ref, inbox_ref, outbox_ref, send_sems, recv_sems):
+    index = lax.axis_index("dp")
+    partners = list(partners_of())
+    step = 1
+    while step < line:
+        partners.append({"dp": index ^ (2 * step)})
+        step *= 2
+    greet(partners)
+    adds = lax.broadcasted_iota(jnp.int32, value_ref.shape, 0) < sum_rows
+    value = value_ref[...]
+    for number, partner in enumerate(partners):
+        outbox_ref[number] = value
+        made = pltpu.make_async_remote_copy(
+            src_ref=outbox_ref.at[number],
+            dst_ref=inbox_ref.at[number],
+            send_sem=send_sems.at[number],
+            recv_sem=recv_sems.at[number],
+            device_id=partner,
+            device_id_type=MESH,
+        )
+        made.start()
+        made.wait()
+        other = inbox_ref[number]
+        value = jnp.where(adds, value + other, jnp.maximum(value, other))
+    out_ref[...] = value
+
+
+def call_combine_all(dp_size, value, sum_rows, collective_id):
+    line = dp_size // 2
+    rounds = 3 + max(0, (line - 1).bit_length())
+    return pl.pallas_call(
+        functools.partial(combine_all, line, sum_rows),
+        in_specs=[WHOLE],
+        out_specs=WHOLE,
+        out_shape=jax.ShapeDtypeStruct(value.shape, F32),
+        scratch_shapes=[
+            pltpu.VMEM((rounds, *value.shape), F32),
+            pltpu.VMEM((rounds, *value.shape), F32),
+            pltpu.SemaphoreType.DMA((rounds,)),
+            pltpu.SemaphoreType.DMA((rounds,)),
+        ],
+        compiler_params=pltpu.CompilerParams(collective_id=collective_id, has_side_effects=True),
+        name="combine_all",
+    )(value)
+
+
 class Links:
     def __init__(self, dp_size, mp_size):
         self.dp, self.mp, self.line = dp_size, mp_size, dp_size // 2
         self.index = lax.axis_index("dp")
         self.place, self.side, self.rank = self.index // 2, self.index % 2, lax.axis_index("mp")
+        self.lines = [[place * 2 + side for place in range(self.line)] for side in range(2)]
 
     def swap_mp(self, value, bit):
         return lax.ppermute(value, "mp", [(i, i ^ bit) for i in range(self.mp)])
 
-    def swap_side(self, value, places=None):
-        places = range(self.line) if places is None else places
-        return lax.ppermute(value, "dp", [(p * 2 + s, p * 2 + 1 - s) for p in places for s in range(2)])
-
-    def move(self, value, places, by):
-        return lax.ppermute(value, "dp", [(p * 2 + s, (p + by) * 2 + s) for p in places for s in range(2)])
-
-
-    def spread(self, own):
-        ups, downs = {}, {}
-        up = down = own
-        for step in range(1, self.line):
-            up = ups[step] = self.move(up, range(step - 1, self.line - 1), 1)
-            down = downs[step] = self.move(down, range(1, self.line - step + 1), -1)
-        return ups, downs
-
-    def from_below(self, step):
-        return range(step, self.line)
-
-    def from_above(self, step):
-        return range(0, self.line - step)
-
-    def pick(self, ups, downs, step):
-        return jnp.where(self.place >= step, ups[step], downs[self.line - step])
+    def swap_side(self, value):
+        return lax.ppermute(value, "dp", [(i, i ^ 1) for i in range(self.dp)])
 
     def gather_line(self, own):
-        ups, downs = self.spread(own)
-        rows = own.shape[0]
-        full = jnp.zeros((self.line * rows, own.shape[1]), own.dtype)
-        full = lax.dynamic_update_slice(full, own, (self.place * rows, 0))
-        for step in range(1, self.line):
-            slot = (self.place - step) % self.line
-            full = lax.dynamic_update_slice(full, self.pick(ups, downs, step), (slot * rows, 0))
-        return full
-
-    def gather_dp(self, own):
-        ups, downs = self.spread(own)
-        other = self.swap_side(own)
-        other_ups = {s: self.swap_side(v, self.from_below(s)) for s, v in ups.items()}
-        other_downs = {s: self.swap_side(v, self.from_above(s)) for s, v in downs.items()}
-        rows = own.shape[0]
-        full = jnp.zeros((self.dp * rows, own.shape[1]), own.dtype)
-
-        def put(full, value, place, side):
-            return lax.dynamic_update_slice(full, value, ((place * 2 + side) * rows, 0))
-
-        full = put(full, own, self.place, self.side)
-        full = put(full, other, self.place, 1 - self.side)
-        for step in range(1, self.line):
-            slot = (self.place - step) % self.line
-            full = put(full, self.pick(ups, downs, step), slot, self.side)
-            full = put(full, self.pick(other_ups, other_downs, step), slot, 1 - self.side)
-        return full
-
-    def sum_line(self, part):
-        up = down = None
-        for step in range(self.line - 1, 0, -1):
-            term = part(jnp.minimum(self.place + step, self.line - 1)).astype(F32)
-            term = term if up is None else term + up.astype(F32)
-            up = self.move(term.astype(BF16), range(0, self.line - step), 1)
-            term = part(jnp.maximum(self.place - step, 0)).astype(F32)
-            term = term if down is None else term + down.astype(F32)
-            down = self.move(term.astype(BF16), range(step, self.line), -1)
-        return part(self.place).astype(F32) + up.astype(F32) + down.astype(F32)
-
-    def sum_dp(self, partial):
-        rows = partial.shape[0] // self.dp
-
-        def cut(place, side):
-            return lax.dynamic_slice_in_dim(partial, (place * 2 + side) * rows, rows, 0)
-
-        def paired(place, places):
-            received = self.swap_side(cut(place, 1 - self.side), places)
-            return cut(place, self.side).astype(F32) + received.astype(F32)
-
-        last = self.line - 1
-        up = down = None
-        for step in range(last, 0, -1):
-            term = paired(jnp.minimum(self.place + step, last), range(0, self.line - step))
-            term = term if up is None else term + up.astype(F32)
-            up = self.move(term.astype(BF16), range(0, self.line - step), 1)
-            term = paired(jnp.maximum(self.place - step, 0), range(step, self.line))
-            term = term if down is None else term + down.astype(F32)
-            down = self.move(term.astype(BF16), range(step, self.line), -1)
-        return paired(self.place, None) + up.astype(F32) + down.astype(F32)
+        return lax.all_gather(own, "dp", axis=0, tiled=True, axis_index_groups=self.lines)
+
+    def sum_line(self, parts):
+        return lax.psum_scatter(parts, "dp", scatter_dimension=0, tiled=True, axis_index_groups=self.lines)
 
 
     def to_slots(self, values):
@@ -285,67 +812,24 @@
         rows = values.shape[0] // self.mp
         return lax.dynamic_slice_in_dim(values, self.rank * rows, rows, 0)
 
-    def sum_core(self, slots):
-        rows = slots.shape[0] // 4
-        cut = lambda k: slots[k * rows : (k + 1) * rows]
-        received = self.swap_mp(jnp.concatenate([cut(1), cut(3)], 0).astype(BF16), 1)
-        return jnp.concatenate([cut(0), cut(2)], 0).astype(F32) + received.astype(F32)
-
-    def sum_far(self, pair):
-        rows = pair.shape[0] // 2
-        received = self.swap_mp(pair[rows:].astype(BF16), 2)
-        return pair[:rows].astype(F32) + received.astype(F32)
-
     def gather_mp(self, quarter):
         rows = quarter.shape[0]
         pair = jnp.concatenate([quarter, self.swap_mp(quarter, 2)], 0)
         near = self.swap_mp(pair, 1)
         return jnp.concatenate([pair[:rows], near[:rows], pair[rows:], near[rows:]], 0)
 
-    def gather_pair(self, quarter):
-        rows, columns = quarter.shape
-        half = columns // 2
-        left, right = quarter[:, :half], quarter[:, half:]
-        left_side = self.swap_side(left)
-        right_far = self.swap_mp(right, 2)
-        left_far = self.swap_mp(jnp.concatenate([left, left_side], 0), 2)
-        right_side = self.swap_side(jnp.concatenate([right, right_far], 0))
-        left_all = jnp.concatenate([left, left_far[:rows], left_side, left_far[rows:]], 0)
-        right_all = jnp.concatenate([right, right_far, right_side[:rows], right_side[rows:]], 0)
-        even = jnp.concatenate([left_all, right_all], 1)
-        near = self.swap_mp(even, 1)
+    def sum_pair(self, slots):
+        rows = slots.shape[0] // 8
         cut = lambda v, k: v[k * rows : (k + 1) * rows]
-        return jnp.concatenate([cut(v, k) for k in range(4) for v in (even, near)], 0)
-
-    def sum_pair(self, slots):
-        total, columns = slots.shape
-        rows, half = total // 8, columns // 2
-        cut = lambda k: slots[k * rows : (k + 1) * rows]
-        near = self.swap_mp(jnp.concatenate([cut(1), cut(3), cut(5), cut(7)], 0).astype(BF16), 1)
-        mine = jnp.concatenate([cut(0), cut(2), cut(4), cut(6)], 0).astype(F32) + near.astype(F32)
-        mine = mine.astype(BF16)
-        left, right = mine[:, :half], mine[:, half:]
-        cut = lambda v, k: v[k * rows : (k + 1) * rows]
-        left = left[: 2 * rows].astype(F32) + self.swap_side(left[2 * rows :]).astype(F32)
-        far = self.swap_mp(jnp.concatenate([cut(right, 1), cut(right, 3)], 0), 2)
-        right = jnp.concatenate([cut(right, 0), cut(right, 2)], 0).astype(F32) + far.astype(F32)
-        left = left[:rows] + self.swap_mp(left[rows:].astype(BF16), 2).astype(F32)
-        right = right[:rows] + self.swap_side(right[rows:].astype(BF16)).astype(F32)
-        return jnp.concatenate([left, right], 1)
-
-
-def after(value, *others):
-    return lax.optimization_barrier((value, *others))[0]
+        picked = lambda ks: jnp.concatenate([cut(slots, k) for k in ks], 0)
+        near = self.swap_mp(picked((1, 3, 5, 7)).astype(BF16), 1)
+        mine = (picked((0, 2, 4, 6)).astype(F32) + near.astype(F32)).astype(BF16)
+        mine = mine[: 2 * rows].astype(F32) + self.swap_side(mine[2 * rows :]).astype(F32)
+        return mine[:rows] + self.swap_mp(mine[rows:].astype(BF16), 2).astype(F32)
 
 
 def inverse_rms(values):
     return lax.rsqrt(jnp.mean(values * values, -1, keepdims=True) + NORM_EPS)
-
-
-def norm_pull(values, scale, gain, grad):
-    turned = grad * gain
-    back = scale * turned - (scale * scale * scale) * values * jnp.mean(turned * values, -1, keepdims=True)
-    return back, jnp.sum(grad * values * scale, 0)
 
 
 def body(
@@ -395,9 +879,6 @@
         )
         return cut(0, group), cut(group, group + 1), cut(group + 1, group + 2)
 
-    qkv_full = links.gather_dp(interleave(w_query, w_key, w_value).astype(BF16))
-    gains_full = lax.all_gather(norm_gains.astype(BF16), "dp", axis=1, tiled=True).astype(F32)
-
     by_side = w_gate_up.reshape(2, shard, line, 2, block)
 
     def side_units(which):
@@ -409,7 +890,7 @@
 
     own_units = [flat(cut) for cut in side_units(side)]
     sent_units = [links.swap_side(flat(cut)) for cut in side_units(1 - side)]
-    out_full = links.gather_dp(after(w_out.astype(BF16), qkv_full))
+    out_full = lax.all_gather(w_out.astype(BF16), "dp", axis=0, tiled=True)
     down_low = w_down.astype(BF16)
     gate_up_full, down_full = [], []
     for j in range(SLICES):
@@ -417,8 +898,14 @@
         rows_pair = jnp.where(
             side == 0, jnp.concatenate([mine, theirs], 0), jnp.concatenate([theirs, mine], 0)
         )
-        gate_up_full.append(links.gather_line(after(rows_pair, out_full)))
-        down_full.append(links.gather_line(after(down_low[j * piece : (j + 1) * piece], out_full)))
+        gate_up_full.append(links.gather_line(rows_pair))
+        down_full.append(links.gather_line(down_low[j * piece : (j + 1) * piece]))
+    gains_low = norm_gains.astype(BF16).astype(F32)
+    gains_rows = jnp.concatenate([gains_low, jnp.zeros((6, gains_low.shape[1]), F32)], 0)
+    qkv_full, gains_shards = call_gather_weights(
+        dp_size, interleave(w_query, w_key, w_value).astype(BF16), gains_rows
+    )
+    gains_full = jnp.transpose(gains_shards, (1, 0, 2)).reshape(8, width)
 
     grad_own = links.to_slots(cotangent)
     quarter = grad_own.shape[0] // 4
@@ -435,12 +922,10 @@
     qkv = jnp.dot(normed_one, qkv_full, preferred_element_type=F32)
     mixed, rotated, lse, peaks = attention_forward(qkv, cosine, sine, segment_ids, group, kvs)
     mixed_slots = links.to_slots(mixed)
-    attended = links.sum_far(links.sum_core(jnp.dot(mixed_slots, out_full, preferred_element_type=F32)))
-    inputs_own = links.own_quarter(tokens).astype(F32)
-    middle = inputs_own + attended
-    scale_two = inverse_rms(middle)
-    normed_two = (middle * scale_two * gains_full[1]).astype(BF16)
-    rows_two = links.gather_pair(normed_two)
+    tokens_own = links.own_quarter(tokens)
+    rows_two, middle = call_spread_forward(
+        jnp.dot(mixed_slots, out_full, preferred_element_type=F32).astype(BF16), tokens_own, gains_full[1:2]
+    )
 
     output_part = grad_normed_part = None
     grad_gate_up_parts, grad_down_parts = [], []
@@ -460,19 +945,19 @@
         grad_normed_part = back if grad_normed_part is None else grad_normed_part + back
         forth = jnp.dot(hidden, down_full[j], preferred_element_type=F32)
         output_part = forth if output_part is None else output_part + forth
-    grad_normed_two = links.sum_pair(grad_normed_part)
-
-    back_two, gain_two = norm_pull(middle, scale_two, gains_full[1], grad_normed_two)
-    grad_middle = links.own_quarter(cotangent).astype(F32) + back_two
-    grad_middle_slots = links.gather_mp(grad_middle.astype(BF16))
+    grad_middle_slots, grad_middle, gain_two = call_spread_backward(
+        grad_normed_part.astype(BF16), middle, links.own_quarter(cotangent), gains_full[1:2]
+    )
     grad_mixed = links.from_slots(dot_nt(grad_middle_slots, out_full).astype(BF16))
     grad_out_part = dot_tn(mixed_slots, grad_middle_slots).astype(BF16)
 
     grad_qkv = attention_backward(rotated, grad_mixed, lse, cosine, sine, segment_ids, group, kvs)
     grad_qkv_part = dot_tn(normed_one, grad_qkv).astype(BF16)
-    grad_normed_one = links.sum_far(links.sum_core(dot_nt(links.to_slots(grad_qkv), qkv_full)))
-    back_one, gain_one = norm_pull(inputs_own, inverse_rms(inputs_own), gains_full[0], grad_normed_one)
-    input_grad = links.from_slots(links.gather_mp((grad_middle + back_one).astype(BF16))).astype(F32)
+    grad_normed_one = dot_nt(links.to_slots(grad_qkv), qkv_full).astype(BF16)
+    input_slots, gain_one, grad_qkv_own = call_finish(
+        dp_size, grad_normed_one, tokens_own, grad_middle, gains_full[0:1], grad_qkv_part
+    )
+    input_grad = links.from_slots(input_slots).astype(F32)
 
     output_own = middle + links.sum_pair(output_part)
     block_output = links.from_slots(links.gather_mp(output_own.astype(BF16)))
@@ -480,26 +965,22 @@
     gate_up_pieces, down_pieces = [], []
     for j in range(SLICES):
         gate_up_part, down_part = grad_gate_up_parts[j], grad_down_parts[j]
-        pair_rows = 2 * shard
-        summed = links.sum_line(
-            lambda place: lax.dynamic_slice_in_dim(gate_up_part, place * pair_rows, pair_rows, 0)
-        )
-        mine = lax.dynamic_slice_in_dim(summed, side * shard, shard, 0)
-        theirs = links.swap_side(lax.dynamic_slice_in_dim(summed, (1 - side) * shard, shard, 0).astype(BF16))
+        summed = links.sum_line(gate_up_part)
+        mine = lax.dynamic_slice_in_dim(summed, side * shard, shard, 0).astype(F32)
+        theirs = links.swap_side(lax.dynamic_slice_in_dim(summed, (1 - side) * shard, shard, 0))
         theirs = theirs.astype(F32)
         gate_up_pieces.append(
             jnp.stack(
                 [jnp.where(side == 0, mine, theirs), jnp.where(side == 0, theirs, mine)], 0
             ).reshape(2, shard, 2, line, piece)
         )
-        down_pieces.append(
-            links.sum_line(lambda place: lax.dynamic_slice_in_dim(down_part, place * piece, piece, 0))
-        )
+        down_pieces.append(links.sum_line(down_part).astype(F32))
     grad_gate_up = jnp.transpose(jnp.stack(gate_up_pieces, 4), (2, 1, 3, 0, 4, 5)).reshape(w_gate_up.shape)
     grad_down = jnp.concatenate(down_pieces, 0)
-    grad_out = links.sum_dp(grad_out_part)
-    grad_query, grad_key, grad_value = untangle(links.sum_dp(grad_qkv_part))
-    gain_terms = lax.psum(jnp.stack([gain_one, gain_two]), ("dp", "mp"))
+    grad_out = lax.psum_scatter(grad_out_part, "dp", scatter_dimension=0, tiled=True).astype(F32)
+    grad_query, grad_key, grad_value = untangle(grad_qkv_own)
+    gain_terms = jnp.concatenate([gain_one[:1].reshape(-1, HEAD), gain_two[:1].reshape(-1, HEAD)], 0)
+    gain_terms = call_combine_all(dp_size, gain_terms, gain_terms.shape[0], 5).reshape(2, width)
     gain_width = norm_gains.shape[1]
     grad_gains = lax.dynamic_slice_in_dim(gain_terms, links.index * gain_width, gain_width, 1)
 
@@ -508,7 +989,6 @@
     peak_vector = lax.dynamic_update_slice(
         jnp.full((HEADS,), MASKED, F32), local_peak, (links.rank * heads,)
     )
-    peak_all = lax.pmax(peak_vector, ("dp", "mp"))
 
     reduced = (grad_query, grad_key, grad_value, grad_out, grad_gate_up, grad_down, grad_gains)
     masters = (w_query, w_key, w_value, w_out, w_gate_up, w_down, norm_gains)
@@ -533,8 +1013,14 @@
         directions.append(direction)
         weight_sq.append(jnp.sum(master * master) * share)
         update_sq.append(jnp.sum(direction * direction) * share)
-    totals = lax.psum(jnp.stack(weight_sq + update_sq), ("dp", "mp"))
-    weight_norm, update_norm = jnp.sqrt(totals[:7]), jnp.sqrt(totals[7:])
+    sums = jnp.stack(weight_sq + update_sq)
+    pad = lambda vector, fill: jnp.pad(vector, (0, HEAD - vector.shape[0]), constant_values=fill)
+    packed = jnp.concatenate(
+        [jnp.broadcast_to(pad(sums, 0.0), (8, HEAD)), jnp.broadcast_to(pad(peak_vector, MASKED), (8, HEAD))], 0
+    )
+    packed = call_combine_all(dp_size, packed, 8, 6)
+    peak_all = packed[8, :HEADS]
+    weight_norm, update_norm = jnp.sqrt(packed[0, :7]), jnp.sqrt(packed[0, 7:14])
     ratio = weight_norm / (update_norm + STEP_EPS)
     stepped = [masters[number] - RATE * ratio[number] * directions[number] for number in range(7)]
     gamma = CLIP / jnp.maximum(peak_all, CLIP)

time: 1380 us -> 903 us (0.65)
  Pallas kernels: 24.4 us -> 419 us
  starting transfers between devices: 295 us -> 11.3 us
  waiting for transfers between devices: 316 us -> 52.1 us
  blocking collectives: 165 us -> 0 us
  local copies, waits for them, and re-layouts: 182 us -> 93.6 us
  other arithmetic: 184 us -> 98 us
  matrix products: 184 us -> 201 us
    pallas_call x0 -> x6, Pallas kernels: none -> 394 us  [the longest x1 118 us: call_gather_weights(): pl.pallas_call(functools.partial(gather_weights, line), in_specs=[hbm] *...]
    ppermute x111 -> x6, starting transfers between devices: 282 us -> 9.25 us  [swap_side(): return lax.ppermute(value, 'dp', [(i, i ^ 1) for i in range(self.dp)])]
    ppermute x111 -> x6, waiting for transfers between devices: 287 us -> 34.7 us  [swap_side(): return lax.ppermute(value, 'dp', [(i, i ^ 1) for i in range(self.dp)])]
    psum x2 -> x0, blocking collectives: 103 us -> none  [the longest x1 55.5 us: body(): totals = lax.psum(jnp.stack(weight_sq + update_sq), ('dp', 'mp'))]
    unnamed x261 -> x125, local copies, waits for them, and re-layouts: 71.8 us -> 32.9 us
    pmax x1 -> x0, blocking collectives: 38.5 us -> none  [body(): peak_all = lax.pmax(peak_vector, ('dp', 'mp'))]
    concatenate x9 -> x4, other arithmetic: 34.7 us -> 4.23 us  [the longest x1 2.41 us: sum_pair(): picked = lambda ks: jnp.concatenate([cut(slots, k) for k in ks], 0)]
    slice x24 -> x6, local copies, waits for them, and re-layouts: 34 us -> 4.41 us  [the longest x1 1.46 us: sum_pair(): mine[2 * rows:]]
  transfers between devices with their start and end apart: 131 -> 21, of which waited for: 31 -> 6; matrix products, arithmetic and copies ran while one was open for 32% -> 42% of each run, Pallas kernels for 2% -> 47%
where the time goes in v2:
time: 903 us; the launch traced here: 896 us
  Pallas kernels  419 us (46%)
  matrix products  201 us (22%)
  other arithmetic  98 us (11%)
  local copies, waits for them, and re-layouts  93.6 us (10%)
  waiting for transfers between devices  52.1 us (6%)
  between operations  21.2 us (2%)
  starting transfers between devices  11.3 us (1%)
    pallas_call x1, Pallas kernels, call_gather_weights(): pl.pallas_call(functools.partial(gather_weights, line), in_specs=[hbm] *...  118 us
    pallas_call x1, Pallas kernels, call_finish(): pl.pallas_call(functools.partial(finish, line), in_specs=[WHOLE] * 5, out...  95.6 us
    pallas_call x1, Pallas kernels, call_spread_forward(): pl.pallas_call(spread_forward, in_specs=[WHOLE] * 3, out_specs=[WHOLE] *...  77.8 us
    pallas_call x1, Pallas kernels, call_spread_backward(): pl.pallas_call(spread_backward, in_specs=[WHOLE] * 4, out_specs=[WHOLE] *...  72.1 us
    dot_general x6, matrix products, dot_nt(): lax.dot_general(left, right, (((1,), (1,)), ((), ())), preferred_element_...  70.9 us
    dot_general x6, matrix products, dot_tn(): lax.dot_general(left, right, (((0,), (0,)), ((), ())), preferred_element_...  57.8 us
    ppermute x6, waiting for transfers between devices, swap_side(): return lax.ppermute(value, 'dp', [(i, i ^ 1) for i in range(self.dp)])  34.7 us
    unnamed x125, local copies, waits for them, and re-layouts  32.9 us
  transfers between devices with their start and end apart: 21, of which 6 were waited for; matrix products, arithmetic and copies ran while one was open for 42% of the time, Pallas kernels for 47%

profile of v2, /device:TPU:0, one launch (start us, length us, event | category | flops | bytes accessed | tf_op | source)
XLA Modules:
  0.0 896.2 jit_solution(12044202696303329274)
XLA Ops:
  24.5 11.5 %collective-permute-done = bf16[256,1024]{0,1:T(8,128)(2,1)} collective-permute-done((bf16[256,1024]{0,1:T(8,128)(2,1)}, bf16[256,1024]{0,1:T(8,128)(2,1)}, u32[]{:S(2)}, u32[]{:S(2)}) %collective-permute-start) | collective-permute-done | bytes 524320 | tf_op jit(solution)/shard_map/ppermute | solution.py:787
  43.2 22.3 %collective-permute-done.1 = bf16[256,1024]{0,1:T(8,128)(2,1)S(1)} collective-permute-done((bf16[256,1024]{0,1:T(8,128)(2,1)S(1)}, bf16[256,1024]{0,1:T(8,128)(2,1)S(1)}, u32[]{:S(2)}, u32[]{:S(2)}) %collective-permute-start.1) | collective-permute-done | bytes 524320 | tf_op jit(solution)/shard_map/ppermute | solution.py:787
  85.2 117.9 %gather_weights.1 = (bf16[2048,1024]{1,0:T(8,128)(2,1)}, f32[8,8,256]{2,1,0:T(8,128)}) custom-call(bf16[256,1024]{1,0:T(8,128)(2,1)} %slice_dynamic-update-slice_fusion.6.own_ref, f32[8,256]{1,0:T(8,128)} %pad_convert_fusion.gains_ref), custom_call_target="tpu_custom_call" | custom-call | tf_op jit(solution)/shard_map/gather_weights/pallas_call | solution.py:710
  218.3 11.9 %attention_forward.1 = (bf16[1024,512]{1,0:T(8,128)(2,1)S(1)}, bf16[1024,1024]{1,0:T(8,128)(2,1)S(1)}, f32[1024,512]{1,0:T(8,128)}, f32[2,8,128]{2,1,0:T(8,128)S(1)}) custom-call(f32[1024,1024]{1,0:T(8,128)} %fusion.21.qkv_ref, f32[1024,128]{1,0:T(8,128)S(1)} %get-tuple-element.195.cos_ref, f32[1024,128]{1,0:T(8,128)S(1)} %get-tuple-element.196.sin_ref, ...), custom_call_target="tpu_custom_call" | custom-call | tf_op jit(solution)/shard_map/attention_forward/pallas_call | solution.py:136
  241.6 77.8 %spread_forward.1 = (bf16[2048,2048]{1,0:T(8,128)(2,1)}, f32[256,2048]{1,0:T(8,128)S(1)}) custom-call(bf16[1024,2048]{1,0:T(8,128)(2,1)} %convolution_convert_fusion.part_ref, bf16[256,2048]{1,0:T(8,128)(2,1)S(1)} %constant_dynamic-slice_fusion.9.tokens_ref, f32[1,2048]{1,0:T(1,128)S(1)} %bitcast.121), custom_call_target="tpu_custom_call" | custom-call | tf_op jit(solution)/shard_map/spread_forward/pallas_call | solution.py:265
  326.6 15.0 %fusion.78 = f32[2048,1024]{0,1:T(8,128)} fusion(bf16[2048,2048]{1,0:T(8,128)(2,1)} %get-tuple-element.50, bf16[2048,1024]{0,1:T(8,128)(2,1)} %all-gather.8.cloned.1.call-done), kind=kOutput, calls=%fused_computation.217 | convolution fusion | flops 8589934592 | bytes 20971520 | tf_op jit(solution)/shard_map/dot_general | solution.py:934
  341.7 14.4 %multiply_convert_fusion.3 = (bf16[2048,512]{0,1:T(8,128)(2,1)}, bf16[2048,512]{0,1:T(8,128)(2,1)}, bf16[2048,512]{0,1:T(8,128)(2,1)S(1)}) fusion(f32[2048,1024]{0,1:T(8,128)} %fusion.78, bf16[2048,2048]{1,0:T(8,128)(2,1)} %slice_dynamic-update-slice_fusion, bf16[512,2048]{1,0:T(8,128)(2,1)} %all-gather.10.cloned.1.call-done), kind=kOutput, calls=%fused_computation.26 | convolution fusion | flops 4311744512 | bytes 25165824 | tf_op jit(solution)/shard_map/dot_general | solution.py:50
  356.1 9.8 %convolution_convert_fusion.7 = bf16[512,2048]{1,0:T(8,128)(2,1)} fusion(bf16[2048,512]{0,1:T(8,128)(2,1)S(1)} %get-tuple-element.117, bf16[2048,2048]{1,0:T(8,128)(2,1)} %slice_dynamic-update-slice_fusion), kind=kOutput, calls=%fused_computation.41 | convolution fusion | flops 4296015872 | bytes 12582912 | tf_op jit(solution)/shard_map/dot_general | solution.py:58
  366.0 14.8 %fusion.80 = f32[2048,1024]{0,1:T(8,128)} fusion(bf16[2048,2048]{1,0:T(8,128)(2,1)} %get-tuple-element.50, bf16[2048,1024]{0,1:T(8,128)(2,1)} %all-gather.12.cloned.1.call-done), kind=kOutput, calls=%fused_computation.219 | convolution fusion | flops 8589934592 | bytes 20971520 | tf_op jit(solution)/shard_map/dot_general | solution.py:934
  380.8 14.4 %multiply_convert_fusion.1 = (bf16[2048,512]{0,1:T(8,128)(2,1)}, bf16[2048,512]{0,1:T(8,128)(2,1)}, bf16[2048,512]{0,1:T(8,128)(2,1)S(1)}) fusion(f32[2048,1024]{0,1:T(8,128)} %fusion.80, bf16[2048,2048]{1,0:T(8,128)(2,1)} %slice_dynamic-update-slice_fusion, bf16[512,2048]{1,0:T(8,128)(2,1)} %all-gather.14.cloned.1.call-done), kind=kOutput, calls=%fused_computation.24 | convolution fusion | flops 4311744512 | bytes 25165824 | tf_op jit(solution)/shard_map/dot_general | solution.py:50
  395.2 9.1 %convolution_convert_fusion.6 = bf16[512,2048]{1,0:T(8,128)(2,1)} fusion(bf16[2048,512]{0,1:T(8,128)(2,1)S(1)} %get-tuple-element.118, bf16[2048,2048]{1,0:T(8,128)(2,1)} %slice_dynamic-update-slice_fusion), kind=kOutput, calls=%fused_computation.40 | convolution fusion | flops 4296015872 | bytes 12582912 | tf_op jit(solution)/shard_map/dot_general | solution.py:58
  404.4 14.2 %convolution_convert_fusion.4 = bf16[2048,1024]{1,0:T(8,128)(2,1)} fusion(bf16[2048,2048]{1,0:T(8,128)(2,1)} %get-tuple-element.50, bf16[2048,512]{0,1:T(8,128)(2,1)} %get-tuple-element.114, bf16[2048,512]{0,1:T(8,128)(2,1)} %get-tuple-element.113), kind=kOutput, calls=%fused_computation.36 | convolution fusion | flops 8600420352 | bytes 16777216 | tf_op jit(solution)/shard_map/dot_general | solution.py:58
  420.3 15.5 %fusion.7 = f32[2048,2048]{1,0:T(8,128)} fusion(bf16[2048,1024]{0,1:T(8,128)(2,1)} %all-gather.12.cloned.1.call-done, bf16[2048,512]{0,1:T(8,128)(2,1)} %get-tuple-element.116, bf16[2048,512]{0,1:T(8,128)(2,1)} %get-tuple-element.115), kind=kOutput, calls=%fused_computation.42 | convolution fusion | flops 8598323200 | bytes 25165824 | tf_op jit(solution)/shard_map/dot_general | solution.py:50
  435.8 15.8 %add_convert_fusion.part_ref = bf16[2048,2048]{1,0:T(8,128)(2,1)} fusion(f32[2048,2048]{1,0:T(8,128)} %fusion.7, bf16[2048,1024]{0,1:T(8,128)(2,1)S(1)} %copy-done.47, bf16[2048,512]{0,1:T(8,128)(2,1)} %get-tuple-element.114, bf16[2048,512]{0,1:T(8,128)(2,1)S(1)} %copy-done.51), kind=kOutput, calls=%fused_computation | convolution fusion | flops 8606711808 | bytes 33554432 | tf_op jit(solution)/shard_map/dot_general | solution.py:50
  451.7 72.1 %spread_backward.1 = (bf16[1024,2048]{1,0:T(8,128)(2,1)}, f32[256,2048]{1,0:T(8,128)}, f32[8,2048]{1,0:T(8,128)}) custom-call(bf16[2048,2048]{1,0:T(8,128)(2,1)} %add_convert_fusion.part_ref, f32[256,2048]{1,0:T(8,128)} %copy-done, bf16[256,2048]{1,0:T(8,128)(2,1)} %copy-done.22, f32[1,2048]{1,0:T(1,128)} %bitcast.122), custom_call_target="tpu_custom_call" | custom-call | tf_op jit(solution)/shard_map/spread_backward/pallas_call | solution.py:355
  529.8 12.8 %fusion.79 = f32[2048,2048]{1,0:T(8,128)} fusion(bf16[2048,512]{0,1:T(8,128)(2,1)} %copy-done.50, bf16[512,2048]{1,0:T(8,128)(2,1)} %all-gather.10.cloned.1.call-done), kind=kOutput, calls=%fused_computation.218 | convolution fusion | flops 4294967296 | bytes 20971520 | tf_op jit(solution)/shard_map/dot_general | solution.py:946
  542.7 14.6 %fusion.77 = (bf16[2048,2048]{1,0:T(8,128)(2,1)}, f32[2048,2048]{1,0:T(8,128)}) fusion(f32[2048,2048]{1,0:T(8,128)} %fusion.79, bf16[2048,512]{0,1:T(8,128)(2,1)S(1)} %get-tuple-element.118, bf16[512,2048]{1,0:T(8,128)(2,1)S(1)} %copy-done.32), kind=kOutput, calls=%fused_computation.216 | convolution fusion | flops 4303355904 | bytes 46137344 | tf_op jit(solution)/shard_map/dot_general | solution.py:946
  566.1 12.0 %convolution_convert_fusion.3 = bf16[2048,1024]{1,0:T(8,128)(2,1)} fusion(bf16[2048,2048]{1,0:T(8,128)(2,1)S(1)} %bitcast.145, bf16[2048,512]{0,1:T(8,128)(2,1)S(1)} %copy-done.53, bf16[2048,512]{0,1:T(8,128)(2,1)S(1)} %copy-done.52), kind=kOutput, calls=%fused_computation.35 | convolution fusion | flops 8600420352 | bytes 16777216 | tf_op jit(solution)/shard_map/dot_general | solution.py:58
  585.7 13.1 %attention_backward.1 = bf16[1024,1024]{1,0:T(8,128)(2,1)S(1)} custom-call(bf16[1024,1024]{1,0:T(8,128)(2,1)} %copy-done.8, bf16[1024,512]{1,0:T(8,128)(2,1)S(1)} %pad_maximum_fusion.11.grad_ref, f32[1024,512]{1,0:T(8,128)} %get-tuple-element.53.lse_ref, f32[1024,128]{1,0:T(8,128)S(1)} %copy-done.3, f32[1024,128]{1,0:T(8,128)S(1)} %copy-done.5, ...), custom_call_target="tpu_custom_call" | custom-call | tf_op jit(solution)/shard_map/attention_backward/pallas_call | solution.py:161
  625.1 95.6 %finish.1 = (bf16[1024,2048]{1,0:T(8,128)(2,1)}, f32[8,2048]{1,0:T(8,128)S(1)}, f32[256,1024]{1,0:T(8,128)S(1)}) custom-call(bf16[1024,2048]{1,0:T(8,128)(2,1)} %convolution_convert_fusion.2.part_ref, bf16[256,2048]{1,0:T(8,128)(2,1)S(1)} %constant_dynamic-slice_fusion.9.tokens_ref, f32[256,2048]{1,0:T(8,128)} %get-tuple-element.54.total_ref, ...), custom_call_target="tpu_custom_call" | custom-call | tf_op jit(solution)/shard_map/finish/pallas_call | solution.py:554
  721.4 15.6 %combine_all.2 = f32[32,128]{1,0:T(8,128)} custom-call(f32[32,128]{1,0:T(8,128)} %pad_maximum_fusion.21.value_ref), custom_call_target="tpu_custom_call" | custom-call | tf_op jit(solution)/shard_map/combine_all/pallas_call | solution.py:760
  758.1 12.4 %collective-permute-done.4 = bf16[256,2048]{1,0:T(8,128)(2,1)} collective-permute-done((bf16[256,2048]{1,0:T(8,128)(2,1)S(1)}, bf16[256,2048]{1,0:T(8,128)(2,1)}, u32[]{:S(2)}, u32[]{:S(2)}) %collective-permute-start.4) | collective-permute-done | bytes 1048608 | tf_op jit(solution)/shard_map/ppermute | solution.py:784
  827.4 10.2 %multiply_reduce_fusion = (f32[]{:T(128)}, f32[2,256,2048]{2,1,0:T(8,128)}, f32[2,256,2048]{2,1,0:T(8,128)}, f32[]{:T(128)}) fusion(f32[2,256,2048]{2,1,0:T(8,128)} %param.24, f32[2,256,2048]{2,1,0:T(8,128)} %reshape.208, f32[2,2,256,2048]{3,2,1,0:T(8,128)} %param.31), kind=kLoop, calls=%fused_computation.21 | loop fusion | flops 14680062 | bytes 25165832 | tf_op jit(solution)/shard_map/reduce_sum | solution.py:1015
  846.0 15.1 %combine_all.3 = f32[16,128]{1,0:T(8,128)} custom-call(f32[16,128]{1,0:T(8,128)} %pad_maximum_fusion.22.value_ref), custom_call_target="tpu_custom_call" | custom-call | tf_op jit(solution)/shard_map/combine_all/pallas_call | solution.py:760
  (284 shorter events, 236.9 us)
Async XLA Ops:
  7.2 227.9 %all-gather.6.cloned.1.call-start = ((), (), s32[]{:S(2)}) async-start(), calls=%async_computation.5 | async-start | bytes 2359296 | tf_op jit(solution)/shard_map/all_gather | solution.py:893
  9.8 316.8 %all-gather.8.cloned.1.call-start = ((), (), s32[]{:S(2)}) async-start(), calls=%async_computation.6 | async-start | bytes 5242880 | tf_op jit(solution)/shard_map/all_gather | solution.py:790
  18.0 18.0 %collective-permute-start = (bf16[256,1024]{0,1:T(8,128)(2,1)}, bf16[256,1024]{0,1:T(8,128)(2,1)}, u32[]{:S(2)}, u32[]{:S(2)}) collective-permute-start(bf16[256,1024]{0,1:T(8,128)(2,1)} %pad_maximum_fusion.14), channel_id=1, source_target_pairs={{0,4},{4,0},{8,12},{12,8},{16,20},{20,16},{24,28},{28,24},{1,5},{5... | collective-permute-start | bytes 1572872 | tf_op jit(solution)/shard_map/ppermute | solution.py:787
  38.5 303.2 %all-gather.10.cloned.1.call-start = ((), (), s32[]{:S(2)}) async-start(), calls=%async_computation.7 | async-start | bytes 2621440 | tf_op jit(solution)/shard_map/all_gather | solution.py:790
  40.7 325.3 %all-gather.12.cloned.1.call-start = ((), (), s32[]{:S(2)}) async-start(), calls=%async_computation.8 | async-start | bytes 5242880 | tf_op jit(solution)/shard_map/all_gather | solution.py:790
  41.1 24.4 %collective-permute-start.1 = (bf16[256,1024]{0,1:T(8,128)(2,1)S(1)}, bf16[256,1024]{0,1:T(8,128)(2,1)S(1)}, u32[]{:S(2)}, u32[]{:S(2)}) collective-permute-start(bf16[256,1024]{0,1:T(8,128)(2,1)S(1)} %pad_maximum_fusion.15), channel_id=1, source_target_pairs={{0,4},{4,0},{8,12},{12,8},{16,20},{20,16},{24,28},{28,24},{1,5},{5... | collective-permute-start | bytes 1572872 | tf_op jit(solution)/shard_map/ppermute | solution.py:787
  66.8 314.0 %all-gather.14.cloned.1.call-start = ((), (), s32[]{:S(2)}) async-start(), calls=%async_computation.9 | async-start | bytes 2621440 | tf_op jit(solution)/shard_map/all_gather | solution.py:790
  75.9 139.9 %collective-permute-start.7 = (bf16[512,2048]{1,0:T(8,128)(2,1)}, bf16[512,2048]{1,0:T(8,128)(2,1)S(1)}, u32[]{:S(2)}, u32[]{:S(2)}) collective-permute-start(bf16[512,2048]{1,0:T(8,128)(2,1)} %pad_maximum_fusion.9), channel_id=1, source_target_pairs={{0,4},{4,0},{8,12},{12,8},{16,20},{20,16},{24,28},{28,24},{1,5},{5... | collective-permute-start | bytes 6291464 | tf_op jit(solution)/shard_map/ppermute | solution.py:787
  77.7 695.1 %reduce-scatter.12.cloned.1.call-start = ((), (), s32[]{:S(2)}) async-start(), calls=%async_computation.13 | async-start | bytes 2621440 | tf_op jit(solution)/shard_map/reduce_scatter | solution.py:793
  81.3 137.0 %copy-start.6 = (s32[1024,1]{1,0:T(8,128)}, s32[1024,1]{1,0:T(8,128)S(1)}, u32[]{:S(2)}) copy-start(s32[1024,1]{1,0:T(8,128)S(1)} %copy.53.seg_col_ref) | copy-start | bytes 12292
  215.8 104.9 %collective-permute-start.8 = (bf16[512,2048]{1,0:T(8,128)(2,1)S(1)}, bf16[512,2048]{1,0:T(8,128)(2,1)}, u32[]{:S(2)}, u32[]{:S(2)}) collective-permute-start(bf16[512,2048]{1,0:T(8,128)(2,1)S(1)} %collective-permute-done.7), channel_id=1, source_target_pairs={{0,1},{1,0},{2,3},{3,2},{4,5},{5,4},{6,7},{7,6},{8,9},{9,8},{10,11... | collective-permute-start | bytes 6291464 | tf_op jit(solution)/shard_map/ppermute | solution.py:784
  365.9 406.9 %reduce-scatter.14.cloned.1.call-start = ((), (), s32[]{:S(2)}) async-start(), calls=%async_computation.14 | async-start | bytes 2621440 | tf_op jit(solution)/shard_map/reduce_scatter | solution.py:793
  404.4 375.0 %reduce-scatter.8.cloned.1.call-start = ((), (), s32[]{:S(2)}) async-start(), calls=%async_computation.11 | async-start | bytes 5242880 | tf_op jit(solution)/shard_map/reduce_scatter | solution.py:793
  418.6 363.4 %reduce-scatter.6.cloned.1.call-start = ((), (), s32[]{:S(2)}) async-start(), calls=%async_computation.10 | async-start | bytes 2359296 | tf_op jit(solution)/shard_map/reduce_scatter | solution.py:980
  451.6 72.2 %copy-start.38 = (bf16[256,512]{1,0:T(8,128)(2,1)S(1)}, bf16[256,512]{1,0:T(8,128)(2,1)}, u32[]{:S(2)}) copy-start(bf16[256,512]{1,0:T(8,128)(2,1)} %get-tuple-element.165) | copy-start | bytes 786436
  529.8 255.6 %reduce-scatter.10.cloned.1.call-start = ((), (), s32[]{:S(2)}) async-start(), calls=%async_computation.12 | async-start | bytes 5242880 | tf_op jit(solution)/shard_map/reduce_scatter | solution.py:793
  563.5 47.1 %collective-permute-start.2 = (bf16[1024,2048]{1,0:T(8,128)(2,1)}, bf16[1024,2048]{1,0:T(8,128)(2,1)}, u32[]{:S(2)}, u32[]{:S(2)}) collective-permute-start(bf16[1024,2048]{1,0:T(8,128)(2,1)} %pad_maximum_fusion), channel_id=1, source_target_pairs={{0,1},{1,0},{2,3},{3,2},{4,5},{5,4},{6,7},{7,6},{8,9},{9,8},{10,11... | collective-permute-start | bytes 12582920 | tf_op jit(solution)/shard_map/ppermute | solution.py:784
  616.0 127.9 %collective-permute-start.3 = (bf16[512,2048]{1,0:T(8,128)(2,1)}, bf16[512,2048]{1,0:T(8,128)(2,1)}, u32[]{:S(2)}, u32[]{:S(2)}) collective-permute-start(bf16[512,2048]{1,0:T(8,128)(2,1)} %slice.395), channel_id=1, source_target_pairs={{0,4},{4,0},{8,12},{12,8},{16,20},{20,16},{24,28},{28,24},{1,5},{5... | collective-permute-start | bytes 6291464 | tf_op jit(solution)/shard_map/ppermute | solution.py:787
  625.1 112.7 %copy-start.29 = (f32[256,256]{1,0:T(8,128)S(1)}, f32[256,256]{1,0:T(8,128)}, u32[]{:S(2)}) copy-start(f32[256,256]{1,0:T(8,128)} %param.22) | copy-start | bytes 786436
  748.5 22.0 %collective-permute-start.4 = (bf16[256,2048]{1,0:T(8,128)(2,1)S(1)}, bf16[256,2048]{1,0:T(8,128)(2,1)}, u32[]{:S(2)}, u32[]{:S(2)}) collective-permute-start(bf16[256,2048]{1,0:T(8,128)(2,1)S(1)} %slice.560), channel_id=1, source_target_pairs={{0,2},{1,3},{2,0},{3,1},{4,6},{5,7},{6,4},{7,5},{8,10},{9,11},{10,... | collective-permute-start | bytes 3145736 | tf_op jit(solution)/shard_map/ppermute | solution.py:784
  772.2 21.1 %collective-permute-start.5 = (bf16[256,2048]{1,0:T(8,128)(2,1)S(1)}, bf16[256,2048]{1,0:T(8,128)(2,1)}, u32[]{:S(2)}, u32[]{:S(2)}) collective-permute-start(bf16[256,2048]{1,0:T(8,128)(2,1)S(1)} %fusion.12), channel_id=1, source_target_pairs={{0,2},{1,3},{2,0},{3,1},{4,6},{5,7},{6,4},{7,5},{8,10},{9,11},{10,... | collective-permute-start | bytes 3145736 | tf_op jit(solution)/shard_map/ppermute | solution.py:784
  781.2 15.1 %collective-permute-start.9 = (bf16[256,1024]{1,0:T(8,128)(2,1)}, bf16[256,1024]{1,0:T(8,128)(2,1)}, u32[]{:S(2)}, u32[]{:S(2)}) collective-permute-start(bf16[256,1024]{1,0:T(8,128)(2,1)} %constant_dynamic-slice_fusion.2), channel_id=1, source_target_pairs={{0,4},{4,0},{8,12},{12,8},{16,20},{20,16},{24,28},{28,24},{1,5},{5... | collective-permute-start | bytes 1572872 | tf_op jit(solution)/shard_map/ppermute | solution.py:787
  787.3 15.0 %collective-permute-start.10 = (bf16[256,1024]{1,0:T(8,128)(2,1)}, bf16[256,1024]{1,0:T(8,128)(2,1)}, u32[]{:S(2)}, u32[]{:S(2)}) collective-permute-start(bf16[256,1024]{1,0:T(8,128)(2,1)} %constant_dynamic-slice_fusion.1), channel_id=1, source_target_pairs={{0,4},{4,0},{8,12},{12,8},{16,20},{20,16},{24,28},{28,24},{1,5},{5... | collective-permute-start | bytes 1572872 | tf_op jit(solution)/shard_map/ppermute | solution.py:787
  796.0 88.6 %collective-permute-start.6 = (bf16[512,2048]{1,0:T(8,128)(2,1)}, bf16[512,2048]{1,0:T(8,128)(2,1)}, u32[]{:S(2)}, u32[]{:S(2)}) collective-permute-start(bf16[512,2048]{1,0:T(8,128)(2,1)} %pad_maximum_fusion.8), channel_id=1, source_target_pairs={{0,1},{1,0},{2,3},{3,2},{4,5},{5,4},{6,7},{7,6},{8,9},{9,8},{10,11... | collective-permute-start | bytes 6291464 | tf_op jit(solution)/shard_map/ppermute | solution.py:784
  (53 other events, 594.9 us)
Sparse Core Ops, SparseCore 0:
  10.7 64.2 all-gather.5
  77.1 102.7 all-gather.7
  182.1 46.8 all-gather.9
  230.9 79.4 all-gather.11
  312.4 44.4 all-gather.13
  366.0 41.3 reduce-scatter.11
  409.8 43.1 reduce-scatter.13
  455.2 76.0 reduce-scatter.7
  535.3 68.0 reduce-scatter.5
  606.2 78.7 reduce-scatter.9

commit v3 on v2

v3 whole, which is shorter than its diff:
```python
import functools
import math

import jax
import jax.numpy as jnp
from jax import lax
from jax.experimental import pallas as pl
from jax.experimental.pallas import tpu as pltpu
from jax.sharding import PartitionSpec as P

HEADS = 16
HEAD = 128
BLOCK = 512
CLIP = 10
TILE = 256

NORM_EPS = 1e-05
ROPE_BASE = 1000000.0
RATE = 0.4
DECAY = 0.5
WEIGHT_DECAY = 0.01
STEP_EPS = 1e-06
MASKED = -1e30

F32 = jnp.float32
BF16 = jnp.bfloat16


def rope_tables(length):
    positions = jnp.arange(length, dtype=F32)
    frequency = ROPE_BASE ** (-(jnp.arange(HEAD // 2, dtype=F32) * 2.0) / HEAD)
    angles = positions[:, None] * frequency[None, :]
    cosine, sine = jnp.cos(angles), jnp.sin(angles)
    return jnp.concatenate([cosine, cosine], 1), jnp.concatenate([-sine, sine], 1)


def lasting(microseconds):
    return pl.CostEstimate(flops=0, bytes_accessed=int(microseconds * 3e6), transcendentals=0)


def turn(values, cosine, sine):
    return values * cosine + pltpu.roll(values, HEAD // 2, 1) * sine


def allowed_mask(seg_row_ref, seg_col_ref, row_start, low, high):
    query_pos = row_start + lax.broadcasted_iota(jnp.int32, (TILE, high - low), 0)
    key_pos = low + lax.broadcasted_iota(jnp.int32, (TILE, high - low), 1)
    same = seg_col_ref[row_start : row_start + TILE, :] == seg_row_ref[0, :, low:high]
    return (key_pos <= query_pos) & same


def dot_nt(left, right):
    return lax.dot_general(left, right, (((1,), (1,)), ((), ())), preferred_element_type=F32)


def dot_nn(left, right):
    return lax.dot_general(left, right, (((1,), (0,)), ((), ())), preferred_element_type=F32)


def dot_tn(left, right):
    return lax.dot_general(left, right, (((0,), (0,)), ((), ())), preferred_element_type=F32)


def slot_rows(rank_ref, start):
    return pl.ds(pl.multiple_of(((start // TILE) ^ rank_ref[0]) * TILE, TILE), TILE)


def attend_forward(group, rank_ref, qkv_ref, cos_ref, sin_ref, seg_row_ref, seg_col_ref, out_ref, rot_ref, lse_ref, peak_ref):
    length = qkv_ref.shape[0]
    scale = 1.0 / math.sqrt(HEAD)
    for part in range(group + 1):
        columns = slice(part * HEAD, (part + 1) * HEAD)
        rot_ref[:, columns] = turn(qkv_ref[:, columns], cos_ref[...], sin_ref[...]).astype(BF16)
    value_columns = slice((group + 1) * HEAD, (group + 2) * HEAD)
    rot_ref[:, value_columns] = qkv_ref[:, value_columns].astype(BF16)
    key_columns = slice(group * HEAD, (group + 1) * HEAD)
    peak_ref[...] = jnp.full(peak_ref.shape, MASKED, F32)
    peaks = [None] * group
    for start in range(0, length, TILE):
        low, high = max(0, start - BLOCK), start + TILE
        rows = slice(start, start + TILE)
        mask = allowed_mask(seg_row_ref, seg_col_ref, start, low, high)
        keys = rot_ref[low:high, key_columns]
        values = rot_ref[low:high, value_columns]
        for head in range(group):
            columns = slice(head * HEAD, (head + 1) * HEAD)
            scores = jnp.where(mask, dot_nt(rot_ref[rows, columns], keys) * scale, MASKED)
            top = jnp.max(scores, 1, keepdims=True)
            exponent = jnp.exp(scores - top)
            total = jnp.sum(exponent, 1, keepdims=True)
            probs = (exponent * (1.0 / total)).astype(BF16)
            out_ref[slot_rows(rank_ref, start), columns] = dot_nn(probs, values).astype(BF16)
            lse_ref[rows, columns] = jnp.broadcast_to(top + jnp.log(total), (TILE, HEAD))
            peak = jnp.max(top, 0, keepdims=True)
            peaks[head] = peak if peaks[head] is None else jnp.maximum(peaks[head], peak)
    for head in range(group):
        peak_ref[0, head : head + 1, :] = jnp.broadcast_to(peaks[head], (1, HEAD))


def attend_backward(group, rank_ref, rot_ref, grad_ref, lse_ref, cos_ref, sin_ref, seg_row_ref, seg_col_ref, out_ref, dk_ref, dv_ref):
    length = rot_ref.shape[0]
    scale = 1.0 / math.sqrt(HEAD)
    key_columns = slice(group * HEAD, (group + 1) * HEAD)
    value_columns = slice((group + 1) * HEAD, (group + 2) * HEAD)
    dk_ref[...] = jnp.zeros(dk_ref.shape, F32)
    dv_ref[...] = jnp.zeros(dv_ref.shape, F32)
    for start in range(0, length, TILE):
        low, high = max(0, start - BLOCK), start + TILE
        rows = slice(start, start + TILE)
        mask = allowed_mask(seg_row_ref, seg_col_ref, start, low, high)
        keys = rot_ref[low:high, key_columns]
        values = rot_ref[low:high, value_columns]
        for head in range(group):
            columns = slice(head * HEAD, (head + 1) * HEAD)
            queries = rot_ref[rows, columns]
            grads = grad_ref[slot_rows(rank_ref, start), columns]
            scores = dot_nt(queries, keys) * scale
            probs = jnp.exp(jnp.where(mask, scores - lse_ref[rows, columns][:, :1], MASKED))
            grad_probs = dot_nt(grads, values)
            inner = jnp.sum(probs * grad_probs, 1, keepdims=True)
            grad_scores = (probs * (grad_probs - inner)).astype(BF16)
            dv_ref[low:high, :] += dot_tn(probs.astype(BF16), grads)
            dk_ref[low:high, :] += dot_tn(grad_scores, queries)
            grad_query = dot_nn(grad_scores, keys) * scale
            turned = turn(grad_query, cos_ref[rows, :], -sin_ref[rows, :])
            out_ref[slot_rows(rank_ref, start), columns] = turned.astype(BF16)
    for start in range(0, length, TILE):
        rows = slice(start, start + TILE)
        turned = turn(dk_ref[rows, :] * scale, cos_ref[rows, :], -sin_ref[rows, :])
        out_ref[slot_rows(rank_ref, start), key_columns] = turned.astype(BF16)
        out_ref[slot_rows(rank_ref, start), value_columns] = dv_ref[rows, :].astype(BF16)


def attention_specs(length, group):
    wide = pl.BlockSpec((length, (group + 2) * HEAD), lambda kv, rank: (0, kv))
    narrow = pl.BlockSpec((length, group * HEAD), lambda kv, rank: (0, kv))
    table = pl.BlockSpec((length, HEAD), lambda kv, rank: (0, 0))
    seg_row = pl.BlockSpec((1, 1, length), lambda kv, rank: (0, 0, 0))
    seg_col = pl.BlockSpec((length, 1), lambda kv, rank: (0, 0))
    return wide, narrow, table, seg_row, seg_col


def attention_forward(rank, qkv, cosine, sine, segments, group, kv_count):
    length = segments.shape[1]
    wide, narrow, table, seg_row, seg_col = attention_specs(length, group)
    return pl.pallas_call(
        functools.partial(attend_forward, group),
        grid_spec=pltpu.PrefetchScalarGridSpec(
            num_scalar_prefetch=1,
            grid=(kv_count,),
            in_specs=[wide, table, table, seg_row, seg_col],
            out_specs=[narrow, wide, narrow, pl.BlockSpec((1, 8, HEAD), lambda kv, rank: (kv, 0, 0))],
        ),
        out_shape=[
            jax.ShapeDtypeStruct((length, kv_count * group * HEAD), BF16),
            jax.ShapeDtypeStruct((length, kv_count * (group + 2) * HEAD), BF16),
            jax.ShapeDtypeStruct((length, kv_count * group * HEAD), F32),
            jax.ShapeDtypeStruct((kv_count, 8, HEAD), F32),
        ],
        compiler_params=pltpu.CompilerParams(vmem_limit_bytes=48 * 2**20),
        cost_estimate=lasting(12),
        name="attention_forward",
    )(rank, qkv, cosine, sine, segments.reshape(1, 1, length), segments.reshape(length, 1))


def attention_backward(rank, rotated, grads, lse, cosine, sine, segments, group, kv_count):
    length = segments.shape[1]
    wide, narrow, table, seg_row, seg_col = attention_specs(length, group)
    return pl.pallas_call(
        functools.partial(attend_backward, group),
        grid_spec=pltpu.PrefetchScalarGridSpec(
            num_scalar_prefetch=1,
            grid=(kv_count,),
            in_specs=[wide, narrow, narrow, table, table, seg_row, seg_col],
            out_specs=wide,
            scratch_shapes=[pltpu.VMEM((length, HEAD), F32), pltpu.VMEM((length, HEAD), F32)],
        ),
        out_shape=jax.ShapeDtypeStruct((length, kv_count * (group + 2) * HEAD), BF16),
        compiler_params=pltpu.CompilerParams(vmem_limit_bytes=48 * 2**20),
        cost_estimate=lasting(13),
        name="attention_backward",
    )(rank, rotated, grads, lse, cosine, sine, segments.reshape(1, 1, length), segments.reshape(length, 1))


def lamb_direction(master, first, second, grad):
    first_moment = DECAY * first + (1.0 - DECAY) * grad
    second_moment = DECAY * second + (1.0 - DECAY) * grad * grad
    return second_moment, first_moment / (jnp.sqrt(second_moment) + STEP_EPS) + WEIGHT_DECAY * master


def gate_up_step(side_ref, master_ref, moment_ref, *refs):
    (gate_mine, up_mine, gate_theirs, up_theirs), (grad_ref, second_ref, direction_ref, sums_ref) = refs[:4], refs[4:]
    part, place, which = pl.program_id(0), pl.program_id(1), pl.program_id(2)
    mine = jnp.where(part == 0, gate_mine[...], up_mine[...])
    theirs = jnp.where(part == 0, gate_theirs[...], up_theirs[...])
    grad = jnp.where(which == side_ref[0], mine, theirs).astype(F32)
    second, direction = lamb_direction(master_ref[0], moment_ref[0, 0], moment_ref[1, 0], grad)
    grad_ref[0], second_ref[0], direction_ref[0] = grad, second, direction

    @pl.when((part == 0) & (place == 0) & (which == 0))
    def _():
        sums_ref[...] = jnp.zeros(sums_ref.shape, F32)

    sums_ref[...] += jnp.sum((direction * direction).reshape(-1, 8, direction.shape[1]), 0)


def call_gate_up_step(line, side, master, moments, summed, theirs):
    _, shard, units = master.shape
    block = units // (2 * line)
    whole = pl.BlockSpec((1, shard, block), lambda g, p, w, side: (g, 0, p * 2 + w))
    shape = jax.ShapeDtypeStruct(master.shape, F32)
    gate_place = lambda g, p: jnp.where(g == 0, p, line - 1)
    up_place = lambda g, p: jnp.where(g == 1, p, 0)
    return pl.pallas_call(
        gate_up_step,
        grid_spec=pltpu.PrefetchScalarGridSpec(
            num_scalar_prefetch=1,
            grid=(2, line, 2),
            in_specs=[
                whole,
                pl.BlockSpec((2, 1, shard, block), lambda g, p, w, side: (0, g, 0, p * 2 + w)),
                pl.BlockSpec((shard, block), lambda g, p, w, side: (side[0], gate_place(g, p))),
                pl.BlockSpec((shard, block), lambda g, p, w, side: (side[0], up_place(g, p))),
                pl.BlockSpec((shard, block), lambda g, p, w, side: (0, gate_place(g, p))),
                pl.BlockSpec((shard, block), lambda g, p, w, side: (0, up_place(g, p))),
            ],
            out_specs=[whole, whole, whole, pl.BlockSpec((8, block), lambda g, p, w, side: (0, 0))],
        ),
        out_shape=[shape, shape, shape, jax.ShapeDtypeStruct((8, block), F32)],
        cost_estimate=lasting(16),
        name="gate_up_step",
    )(side, master, moments, *summed, *theirs)


VMEM_ALL = pl.BlockSpec(memory_space=pltpu.VMEM)
SMALL = 5


def small_step(group, kvs, owner_ref, grad_qkv_ref, grad_out_ref, grad_gains_ref, *refs):
    masters, moments, refs = refs[:SMALL], refs[SMALL : 2 * SMALL], refs[2 * SMALL :]
    grads, seconds, directions, sums_ref = refs[:3], refs[3:8], refs[8:13], refs[13]
    step = (group + 2) * HEAD
    for kv in range(kvs):
        low = kv * step
        for ref, start, columns in ((grads[0], 0, group * HEAD), (grads[1], group * HEAD, HEAD), (grads[2], (group + 1) * HEAD, HEAD)):
            ref[:, kv * columns : (kv + 1) * columns] = grad_qkv_ref[:, low + start : low + start + columns]
    sums_ref[...] = jnp.zeros(sums_ref.shape, F32)
    for number in range(SMALL):
        grad = (grads[0], grads[1], grads[2], grad_out_ref, grad_gains_ref)[number][...]
        moment = moments[number]
        second, direction = lamb_direction(masters[number][...], moment[0], moment[1], grad)
        seconds[number][...] = second
        directions[number][...] = direction
        total = jnp.sum(jnp.sum(direction * direction, 0, keepdims=True), 1, keepdims=True)
        row = jnp.broadcast_to(total, (1, HEAD))
        sums_ref[number : number + 1, :] = row * owner_ref[...] if number == SMALL - 1 else row


def call_small_step(group, kvs, owner, grad_qkv, grad_out, grad_gains, masters, moments):
    like = lambda arrays: [jax.ShapeDtypeStruct(array.shape, F32) for array in arrays]
    return pl.pallas_call(
        functools.partial(small_step, group, kvs),
        in_specs=[VMEM_ALL] * (4 + 2 * SMALL),
        out_specs=[VMEM_ALL] * 14,
        out_shape=[*like(masters[:3]), *like(masters), *like(masters), jax.ShapeDtypeStruct((8, HEAD), F32)],
        compiler_params=pltpu.CompilerParams(vmem_limit_bytes=40 * 2**20),
        cost_estimate=lasting(6),
        name="small_step",
    )(owner, grad_qkv, grad_out, grad_gains, *masters, *moments)


def pick_lane(row, lane):
    lanes = lax.broadcasted_iota(jnp.int32, row.shape, 1)
    return jnp.sum(jnp.where(lanes == lane, row, 0.0), 1, keepdims=True)


def rate_of(packed_ref, number):
    squares = packed_ref[0:1, :]
    weight, update = jnp.sqrt(pick_lane(squares, number)), jnp.sqrt(pick_lane(squares, 7 + number))
    return RATE * (weight / (update + STEP_EPS))


def small_update(group, kvs, rank_ref, packed_ref, *refs):
    masters, directions, news, copies = (refs[k * SMALL : (k + 1) * SMALL] for k in range(4))
    gamma = CLIP / jnp.maximum(packed_ref[8:9, :], float(CLIP))
    heads = [pick_lane(gamma, rank_ref[0] * (group * kvs) + head) for head in range(group * kvs)]
    for place, number in enumerate((0, 1, 2, 3, 6)):
        rate = rate_of(packed_ref, number)
        if place > 1:
            stepped = masters[place][...] - rate * directions[place][...]
            news[place][...] = stepped
            copies[place][...] = stepped.astype(BF16)
            continue
        for head in range(group * kvs if place == 0 else kvs):
            scale = heads[head]
            if place == 1:
                scale = functools.reduce(jnp.minimum, heads[head * group : (head + 1) * group])
            columns = slice(head * HEAD, (head + 1) * HEAD)
            stepped = masters[place][:, columns] - rate * directions[place][:, columns]
            stepped = stepped * jnp.sqrt(scale)
            news[place][:, columns] = stepped
            copies[place][:, columns] = stepped.astype(BF16)


def call_small_update(group, kvs, rank, packed, masters, directions):
    like = lambda kind: [jax.ShapeDtypeStruct(array.shape, kind) for array in masters]
    return pl.pallas_call(
        functools.partial(small_update, group, kvs),
        in_specs=[pl.BlockSpec(memory_space=pltpu.SMEM), *[VMEM_ALL] * (1 + 2 * SMALL)],
        out_specs=[VMEM_ALL] * (2 * SMALL),
        out_shape=[*like(F32), *like(BF16)],
        compiler_params=pltpu.CompilerParams(vmem_limit_bytes=40 * 2**20),
        cost_estimate=lasting(5),
        name="small_update",
    )(rank, packed, *masters, *directions)


def large_update(number, packed_ref, master_ref, direction_ref, new_ref, copy_ref):
    stepped = master_ref[...] - rate_of(packed_ref, number) * direction_ref[...]
    new_ref[...] = stepped
    copy_ref[...] = stepped.astype(BF16)


def call_large_update(number, packed, master, direction):
    rows, columns = master.shape
    tile = min(rows, 128)
    blocks = pl.BlockSpec((tile, columns), lambda i: (i, 0))
    return pl.pallas_call(
        functools.partial(large_update, number),
        grid=(rows // tile,),
        in_specs=[pl.BlockSpec((16, HEAD), lambda i: (0, 0)), blocks, blocks],
        out_specs=[blocks, blocks],
        out_shape=[jax.ShapeDtypeStruct(master.shape, F32), jax.ShapeDtypeStruct(master.shape, BF16)],
        cost_estimate=lasting(4),
        name="large_update",
    )(packed, master, direction)


MESH = pl.DeviceIdType.MESH
WHOLE = pl.BlockSpec(memory_space=pltpu.VMEM)
CHUNKS = 8
AHEAD = 1


def greet(partners):
    barrier = pltpu.get_barrier_semaphore()
    for partner in partners:
        pl.semaphore_signal(barrier, inc=1, device_id=partner, device_id_type=MESH)
    pl.semaphore_wait(barrier, len(partners))


def sender(send_sems, recv_sems, log):
    def copy(kind, chunk, source, target, device):
        made = pltpu.make_async_remote_copy(
            src_ref=source,
            dst_ref=target,
            send_sem=send_sems.at[kind, chunk],
            recv_sem=recv_sems.at[kind, chunk],
            device_id=device,
            device_id_type=MESH,
        )
        log.append(made)
        return made

    return copy


def partners_of():
    rank, index = lax.axis_index("mp"), lax.axis_index("dp")
    return {"mp": rank ^ 1}, {"mp": rank ^ 2}, {"dp": index ^ 1}


class Everyone:
    def __init__(self, line, near_ref, line_ref, near_send, near_recv, line_send, line_recv):
        self.line, self.near_ref, self.line_ref = line, near_ref, line_ref
        self.near_send, self.near_recv, self.line_send, self.line_recv = near_send, near_recv, line_send, line_recv
        self.index, self.rank = lax.axis_index("dp"), lax.axis_index("mp")
        self.place, self.side = self.index // 2, self.index % 2
        self.code = self.side * 4 + self.rank

    @staticmethod
    def scratch(line, shape):
        return [
            pltpu.VMEM((8, *shape), F32),
            pltpu.VMEM((line, *shape), F32),
            pltpu.SemaphoreType.DMA((8,)),
            pltpu.SemaphoreType.DMA((8,)),
            pltpu.SemaphoreType.DMA((line,)),
            pltpu.SemaphoreType.DMA((line,)),
        ]

    def peer(self, k):
        return {"dp": self.index ^ (k // 4), "mp": self.rank ^ (k % 4)}

    def along(self, k):
        return {"dp": ((self.place + k) % self.line) * 2 + self.side}

    def partners(self):
        return [self.peer(k) for k in range(1, 8)] + [self.along(k) for k in range(1, self.line)]

    @staticmethod
    def add(left, right):
        return left + right

    def near_copy(self, k, slot):
        return pltpu.make_async_remote_copy(
            src_ref=self.near_ref.at[self.code],
            dst_ref=self.near_ref.at[slot],
            send_sem=self.near_send.at[k],
            recv_sem=self.near_recv.at[slot],
            device_id=self.peer(k),
            device_id_type=MESH,
        )

    def line_copy(self, k, slot):
        return pltpu.make_async_remote_copy(
            src_ref=self.line_ref.at[self.place],
            dst_ref=self.line_ref.at[slot],
            send_sem=self.line_send.at[k],
            recv_sem=self.line_recv.at[slot],
            device_id=self.along(k),
            device_id_type=MESH,
        )

    @staticmethod
    def total(ref, count, fold):
        value = ref[0]
        for k in range(1, count):
            value = fold(value, ref[k])
        return value

    def send_near(self):
        for k in range(1, 8):
            self.near_copy(k, self.code).start()

    def send_line(self, fold):
        for k in range(1, 8):
            self.near_copy(k, self.code ^ k).wait_recv()
        self.line_ref[self.place] = self.total(self.near_ref, 8, fold)
        for k in range(1, self.line):
            self.line_copy(k, self.place).start()

    def result(self, fold):
        for k in range(1, self.line):
            self.line_copy(k, (self.place + k) % self.line).wait_recv()
        value = self.total(self.line_ref, self.line, fold)
        for k in range(1, 8):
            self.near_copy(k, self.code).wait_send()
        for k in range(1, self.line):
            self.line_copy(k, self.place).wait_send()
        return value


def spread_forward(part_ref, tokens_ref, gain_ref, rows_ref, middle_ref, near_ref, out_ref, far_ref, send_sems, recv_sems):
    core, far, pair = partners_of()
    quarter, _ = tokens_ref.shape
    size = quarter // CHUNKS
    at = lambda slot, i: pl.ds(slot * quarter + i * size, size)
    greet([core, far, pair])
    log = []
    copy = sender(send_sems, recv_sems, log)
    near = {}
    for i in range(CHUNKS):
        for k in range(2):
            near[k, i] = copy(k, i, part_ref.at[at(2 * k + 1, i)], near_ref.at[at(k, i)], core)
            near[k, i].start()
    sums = {}

    def send_sum(i):
        near[1, i].wait_recv()
        total = part_ref[at(2, i), :].astype(F32) + near_ref[at(1, i), :].astype(F32)
        out_ref[at(0, i), :] = total.astype(BF16)
        sums[i] = copy(2, i, out_ref.at[at(0, i)], far_ref.at[at(0, i)], far)
        sums[i].start()

    for i in range(AHEAD):
        send_sum(i)
    moves = {}
    for i in range(CHUNKS + 2):
        if i + AHEAD < CHUNKS:
            send_sum(i + AHEAD)
        if i < CHUNKS:
            near[0, i].wait_recv()
            sums[i].wait_recv()
            middle = tokens_ref[at(0, i), :].astype(F32) + (
                part_ref[at(0, i), :].astype(F32)
                + near_ref[at(0, i), :].astype(F32)
                + far_ref[at(0, i), :].astype(F32)
            )
            middle_ref[at(0, i), :] = middle
            rows_ref[at(0, i), :] = (middle * inverse_rms(middle) * gain_ref[0:1, :]).astype(BF16)
            own = rows_ref.at[at(0, i)]
            for kind, slot, device in ((3, 2, far), (4, 4, pair), (6, 1, core)):
                moves[kind, i] = copy(kind, i, own, rows_ref.at[at(slot, i)], device)
                moves[kind, i].start()
        j = i - 1
        if 0 <= j < CHUNKS:
            moves[3, j].wait_recv()
            for kind, slot, device in ((5, 6, pair), (7, 3, core)):
                moves[kind, j] = copy(kind, j, rows_ref.at[at(2, j)], rows_ref.at[at(slot, j)], device)
                moves[kind, j].start()
            moves[4, j].wait_recv()
            moves[8, j] = copy(8, j, rows_ref.at[at(4, j)], rows_ref.at[at(5, j)], core)
            moves[8, j].start()
        j = i - 2
        if 0 <= j < CHUNKS:
            moves[5, j].wait_recv()
            moves[9, j] = copy(9, j, rows_ref.at[at(6, j)], rows_ref.at[at(7, j)], core)
            moves[9, j].start()
    for i in range(CHUNKS):
        for kind in (6, 7, 8, 9):
            moves[kind, i].wait_recv()
    for made in log:
        made.wait_send()


def call_spread_forward(part, tokens_own, gain):
    quarter, width = tokens_own.shape
    return pl.pallas_call(
        spread_forward,
        in_specs=[WHOLE] * 3,
        out_specs=[WHOLE] * 2,
        out_shape=[
            jax.ShapeDtypeStruct((8 * quarter, width), BF16),
            jax.ShapeDtypeStruct((quarter, width), F32),
        ],
        scratch_shapes=[
            pltpu.VMEM((2 * quarter, width), BF16),
            pltpu.VMEM((quarter, width), BF16),
            pltpu.VMEM((quarter, width), BF16),
            pltpu.SemaphoreType.DMA((10, CHUNKS)),
            pltpu.SemaphoreType.DMA((10, CHUNKS)),
        ],
        compiler_params=pltpu.CompilerParams(
            collective_id=1, has_side_effects=True, vmem_limit_bytes=50 * 2**20
        ),
        cost_estimate=lasting(64),
        name="spread_forward",
    )(part, tokens_own, gain)


def pull_chunk(values, scale_gain, grad):
    scale = inverse_rms(values)
    turned = grad * scale_gain
    inner = jnp.mean(turned * values, -1, keepdims=True)
    return scale * turned - (scale * scale * scale) * values * inner, grad * values * scale


def spread_backward(part_ref, middle_ref, grad_ref, gain_ref, rows_ref, total_ref, gain_out_ref, near_ref, side_out_ref, side_in_ref, far_out_ref, far_in_ref, send_sems, recv_sems):
    core, far, pair = partners_of()
    quarter, width = middle_ref.shape
    size = quarter // CHUNKS
    at = lambda slot, i: pl.ds(slot * quarter + i * size, size)
    greet([core, far, pair])
    log = []
    copy = sender(send_sems, recv_sems, log)
    near, side, sums, moves = {}, {}, {}, {}
    for i in range(CHUNKS):
        for k in (2, 3, 0, 1):
            near[k, i] = copy(k, i, part_ref.at[at(2 * k + 1, i)], near_ref.at[at(k, i)], core)
            near[k, i].start()

    def pairs(k, i):
        return part_ref[at(2 * k, i), :].astype(F32) + near_ref[at(k, i), :].astype(F32)

    def send_side(i):
        for k in (1, 0):
            near[2 + k, i].wait_recv()
            side_out_ref[at(k, i), :] = pairs(2 + k, i).astype(BF16)
            side[k, i] = copy(4 + k, i, side_out_ref.at[at(k, i)], side_in_ref.at[at(k, i)], pair)
            side[k, i].start()

    for i in range(AHEAD):
        send_side(i)
    gain_sum = jnp.zeros((1, width), F32)
    for i in range(CHUNKS + 2):
        if i + AHEAD < CHUNKS:
            send_side(i + AHEAD)
        if i < CHUNKS:
            near[1, i].wait_recv()
            side[1, i].wait_recv()
            far_out_ref[at(0, i), :] = (pairs(1, i) + side_in_ref[at(1, i), :].astype(F32)).astype(BF16)
            sums[i] = copy(6, i, far_out_ref.at[at(0, i)], far_in_ref.at[at(0, i)], far)
            sums[i].start()
        j = i - 1
        if 0 <= j < CHUNKS:
            near[0, j].wait_recv()
            side[0, j].wait_recv()
            sums[j].wait_recv()
            grad = pairs(0, j) + side_in_ref[at(0, j), :].astype(F32) + far_in_ref[at(0, j), :].astype(F32)
            back, gain_part = pull_chunk(middle_ref[at(0, j), :], gain_ref[0:1, :], grad)
            gain_sum = gain_sum + jnp.sum(gain_part, 0, keepdims=True)
            total = grad_ref[at(0, j), :].astype(F32) + back
            total_ref[at(0, j), :] = total
            rows_ref[at(0, j), :] = total.astype(BF16)
            own = rows_ref.at[at(0, j)]
            for kind, slot, device in ((7, 2, far), (8, 1, core)):
                moves[kind, j] = copy(kind, j, own, rows_ref.at[at(slot, j)], device)
                moves[kind, j].start()
        j = i - 2
        if 0 <= j < CHUNKS:
            moves[7, j].wait_recv()
            moves[9, j] = copy(9, j, rows_ref.at[at(2, j)], rows_ref.at[at(3, j)], core)
            moves[9, j].start()
    gain_out_ref[...] = jnp.broadcast_to(gain_sum, gain_out_ref.shape)
    for i in range(CHUNKS):
        for kind in (8, 9):
            moves[kind, i].wait_recv()
    for made in log:
        made.wait_send()


def call_spread_backward(part, middle, grad_own, gain):
    quarter, width = middle.shape
    return pl.pallas_call(
        spread_backward,
        in_specs=[WHOLE] * 4,
        out_specs=[WHOLE] * 3,
        out_shape=[
            jax.ShapeDtypeStruct((4 * quarter, width), BF16),
            jax.ShapeDtypeStruct((quarter, width), F32),
            jax.ShapeDtypeStruct((8, width), F32),
        ],
        scratch_shapes=[
            pltpu.VMEM((4 * quarter, width), BF16),
            pltpu.VMEM((2 * quarter, width), BF16),
            pltpu.VMEM((2 * quarter, width), BF16),
            pltpu.VMEM((quarter, width), BF16),
            pltpu.VMEM((quarter, width), BF16),
            pltpu.SemaphoreType.DMA((10, CHUNKS)),
            pltpu.SemaphoreType.DMA((10, CHUNKS)),
        ],
        compiler_params=pltpu.CompilerParams(
            collective_id=2, has_side_effects=True, vmem_limit_bytes=56 * 2**20
        ),
        cost_estimate=lasting(68),
        name="spread_backward",
    )(part, middle, grad_own, gain)


def finish(line, part_ref, tokens_ref, total_ref, gain_ref, *refs):
    gain_two_ref, grads_refs, refs = refs[0], refs[1:3], refs[3:]
    rows_ref, gain_out_ref, *owned_refs = refs[:4]
    near_ref, far_out_ref, far_in_ref = refs[4:7]
    side_in_refs, up_out_refs, up_in_refs, down_out_refs, down_in_refs = (refs[k : k + 2] for k in range(7, 17, 2))
    send_sems, recv_sems, side_send, side_recv, line_send, line_recv, *exchange = refs[17:]
    core, far, pair = partners_of()
    index = lax.axis_index("dp")
    place, side = index // 2, index % 2
    above, below = {"dp": index + 2}, {"dp": index - 2}
    quarter, width = tokens_ref.shape
    size = quarter // CHUNKS
    last = line - 1
    at = lambda slot, i: pl.ds(slot * quarter + i * size, size)

    def block(w, where, which):
        rows = owned_refs[w].shape[0]
        return pl.ds((where * 2 + which) * rows, rows)


    everyone = Everyone(line, *exchange)
    greet(everyone.partners())
    log = []
    copy = sender(send_sems, recv_sems, log)
    near, sums, moves = {}, {}, {}
    for i in range(CHUNKS):
        for k in (1, 0):
            near[k, i] = copy(k, i, part_ref.at[at(2 * k + 1, i)], near_ref.at[at(k, i)], core)
            near[k, i].start()

    def side_copy(w, where):
        return pltpu.make_async_remote_copy(
            src_ref=grads_refs[w].at[block(w, where, 1 - side)],
            dst_ref=side_in_refs[w].at[where],
            send_sem=side_send.at[w, where],
            recv_sem=side_recv.at[w, where],
            device_id=pair,
            device_id_type=MESH,
        )

    def line_copy(w, upward, step):
        out_ref, in_ref = (up_out_refs[w], up_in_refs[w]) if upward else (down_out_refs[w], down_in_refs[w])
        way = 0 if upward else 1
        return pltpu.make_async_remote_copy(
            src_ref=out_ref.at[step - 1],
            dst_ref=in_ref.at[step - 1],
            send_sem=line_send.at[w, way, step - 1],
            recv_sem=line_recv.at[w, way, step - 1],
            device_id=above if upward else below,
            device_id_type=MESH,
        )

    for step in range(last, 0, -1):

        @pl.when(place + step <= last)
        def _(step=step):
            for w in range(2):
                side_copy(w, place + step).start()

        @pl.when(place - step >= 0)
        def _(step=step):
            for w in range(2):
                side_copy(w, place - step).start()

    for w in range(2):
        side_copy(w, place).start()

    for i in range(CHUNKS):
        near[1, i].wait_recv()
        summed = part_ref[at(2, i), :].astype(F32) + near_ref[at(1, i), :].astype(F32)
        far_out_ref[at(0, i), :] = summed.astype(BF16)
        sums[i] = copy(2, i, far_out_ref.at[at(0, i)], far_in_ref.at[at(0, i)], far)
        sums[i].start()

    def term(w, where):
        return grads_refs[w][block(w, where, side), :].astype(F32) + side_in_refs[w][where].astype(F32)

    def line_step(step):
        for w in range(2):

            @pl.when(place + step <= last)
            def _(w=w):
                side_copy(w, place + step).wait_recv()
                value = term(w, place + step)
                up_out_refs[w][step - 1] = value.astype(BF16)
                if step < last:

                    @pl.when(place > 0)
                    def _():
                        line_copy(w, True, step + 1).wait_recv()
                        up_out_refs[w][step - 1] = (value + up_in_refs[w][step].astype(F32)).astype(BF16)

                line_copy(w, True, step).start()

            @pl.when(place - step >= 0)
            def _(w=w):
                side_copy(w, place - step).wait_recv()
                value = term(w, place - step)
                down_out_refs[w][step - 1] = value.astype(BF16)
                if step < last:

                    @pl.when(place < last)
                    def _():
                        line_copy(w, False, step + 1).wait_recv()
                        down_out_refs[w][step - 1] = (value + down_in_refs[w][step].astype(F32)).astype(BF16)

                line_copy(w, False, step).start()

    gain_sum = jnp.zeros((1, width), F32)
    steps = list(range(last, 0, -1))
    for i in range(CHUNKS + 1):
        if i < CHUNKS:
            near[0, i].wait_recv()
            sums[i].wait_recv()
            grad = (
                part_ref[at(0, i), :].astype(F32)
                + near_ref[at(0, i), :].astype(F32)
                + far_in_ref[at(0, i), :].astype(F32)
            )
            back, gain_part = pull_chunk(tokens_ref[at(0, i), :].astype(F32), gain_ref[0:1, :], grad)
            gain_sum = gain_sum + jnp.sum(gain_part, 0, keepdims=True)
            rows_ref[at(0, i), :] = (total_ref[at(0, i), :] + back).astype(BF16)
            own = rows_ref.at[at(0, i)]
            for kind, slot, device in ((3, 2, far), (4, 1, core)):
                moves[kind, i] = copy(kind, i, own, rows_ref.at[at(slot, i)], device)
                moves[kind, i].start()
        if steps:
            line_step(steps.pop(0))
        j = i - 1
        if 0 <= j < CHUNKS:
            moves[3, j].wait_recv()
            moves[5, j] = copy(5, j, rows_ref.at[at(2, j)], rows_ref.at[at(3, j)], core)
            moves[5, j].start()
    while steps:
        line_step(steps.pop(0))
    columns = gain_out_ref.shape[1]
    for r in range(4):
        cut = slice(r * columns, (r + 1) * columns)
        everyone.near_ref[everyone.code, r : r + 1, :] = gain_sum[:, cut]
        everyone.near_ref[everyone.code, r + 4 : r + 5, :] = gain_two_ref[0:1, cut]
    everyone.send_near()
    everyone.send_line(everyone.add)
    for w in range(2):
        side_copy(w, place).wait_recv()
        owned_refs[w][...] = term(w, place)

        @pl.when(place > 0)
        def _(w=w):
            line_copy(w, True, 1).wait_recv()
            owned_refs[w][...] += up_in_refs[w][0].astype(F32)

        @pl.when(place < last)
        def _(w=w):
            line_copy(w, False, 1).wait_recv()
            owned_refs[w][...] += down_in_refs[w][0].astype(F32)

    gain_out_ref[...] = everyone.result(everyone.add)
    for i in range(CHUNKS):
        for kind in (4, 5):
            moves[kind, i].wait_recv()
    for made in log:
        made.wait_send()
    for w in range(2):
        for where in range(line):
            side_copy(w, where).wait_send()
        for step in range(last, 0, -1):

            @pl.when(place + step <= last)
            def _(w=w, step=step):
                line_copy(w, True, step).wait_send()

            @pl.when(place - step >= 0)
            def _(w=w, step=step):
                line_copy(w, False, step).wait_send()


def call_finish(dp_size, part, tokens_own, total, gain, gain_two, *grads):
    quarter, width = tokens_own.shape
    line = dp_size // 2
    owned = [(grad.shape[0] // dp_size, grad.shape[1]) for grad in grads]
    stacks = lambda count: [pltpu.VMEM((count, *shape), BF16) for shape in owned]
    return pl.pallas_call(
        functools.partial(finish, line),
        in_specs=[WHOLE] * 7,
        out_specs=[WHOLE] * 4,
        out_shape=[
            jax.ShapeDtypeStruct((4 * quarter, width), BF16),
            jax.ShapeDtypeStruct((8, width // 4), F32),
            *[jax.ShapeDtypeStruct(shape, F32) for shape in owned],
        ],
        scratch_shapes=[
            pltpu.VMEM((2 * quarter, width), BF16),
            pltpu.VMEM((quarter, width), BF16),
            pltpu.VMEM((quarter, width), BF16),
            *stacks(line),
            *stacks(line - 1),
            *stacks(line - 1),
            *stacks(line - 1),
            *stacks(line - 1),
            pltpu.SemaphoreType.DMA((6, CHUNKS)),
            pltpu.SemaphoreType.DMA((6, CHUNKS)),
            pltpu.SemaphoreType.DMA((2, line)),
            pltpu.SemaphoreType.DMA((2, line)),
            pltpu.SemaphoreType.DMA((2, 2, line)),
            pltpu.SemaphoreType.DMA((2, 2, line)),
            *Everyone.scratch(line, (8, width // 4)),
        ],
        compiler_params=pltpu.CompilerParams(
            collective_id=3, has_side_effects=True, vmem_limit_bytes=56 * 2**20
        ),
        cost_estimate=lasting(85),
        name="finish",
    )(part, tokens_own, total, gain, gain_two, *grads)


def gather_weights(line, own_ref, out_ref, gains_ref, grad_ref, full_ref, out_full_ref, gains_full_ref, rows_ref, local_sems, side_send, side_recv, line_send, line_recv, rows_send, rows_recv, staged_ref):
    index = lax.axis_index("dp")
    place, side = index // 2, index % 2
    pair, above, below = {"dp": index ^ 1}, {"dp": index + 2}, {"dp": index - 2}
    rank = lax.axis_index("mp")
    core, far = {"mp": rank ^ 1}, {"mp": rank ^ 2}
    quarter = grad_ref.shape[0] // 4
    slot_of = lambda k: rows_ref.at[pl.ds(k * quarter, quarter)]
    quarter_of = lambda k: grad_ref.at[pl.ds((rank ^ k) * quarter, quarter)]
    last = line - 1
    owns, fulls = (own_ref, out_ref, gains_ref), (full_ref, out_full_ref, gains_full_ref)
    all_three = range(3)

    barrier = pltpu.get_barrier_semaphore()
    pl.semaphore_signal(barrier, inc=1, device_id=pair, device_id_type=MESH)
    pl.semaphore_signal(barrier, inc=1, device_id=core, device_id_type=MESH)
    pl.semaphore_signal(barrier, inc=1, device_id=far, device_id_type=MESH)

    @pl.when(place < last)
    def _():
        pl.semaphore_signal(barrier, inc=1, device_id=above, device_id_type=MESH)

    @pl.when(place > 0)
    def _():
        pl.semaphore_signal(barrier, inc=1, device_id=below, device_id_type=MESH)

    pl.semaphore_wait(barrier, 3 + (place < last).astype(jnp.int32) + (place > 0).astype(jnp.int32))

    def slot(which, where, side):
        rows = owns[which].shape[0]
        return fulls[which].at[pl.ds((where * 2 + side) * rows, rows)]

    def views(which, where):
        return slot(which, where, side)

    def source(which, where, first):
        return owns[which] if first else views(which, where)

    def line_copy(which, upward, where, first=False):
        way = 0 if upward else 1
        return pltpu.make_async_remote_copy(
            src_ref=source(which, where, first),
            dst_ref=views(which, where),
            send_sem=line_send.at[which, way, where],
            recv_sem=line_recv.at[which, way, where],
            device_id=above if upward else below,
            device_id_type=MESH,
        )

    def side_copy(which, where, first=False):
        return pltpu.make_async_remote_copy(
            src_ref=source(which, where, first),
            dst_ref=views(which, where),
            send_sem=side_send.at[which, where],
            recv_sem=side_recv.at[which, where],
            device_id=pair,
            device_id_type=MESH,
        )

    def side_arrival(which, where):
        target = slot(which, where, 1 - side)
        return pltpu.make_async_remote_copy(
            src_ref=target,
            dst_ref=target,
            send_sem=side_send.at[which, where],
            recv_sem=side_recv.at[which, where],
            device_id=pair,
            device_id_type=MESH,
        )

    @pl.when(place < last)
    def _():
        for which in all_three:
            line_copy(which, True, place, True).start()

    @pl.when(place > 0)
    def _():
        for which in all_three:
            line_copy(which, False, place, True).start()

    for which in all_three:
        side_copy(which, place, True).start()
    here = [pltpu.make_async_copy(source(w, place, True), views(w, place), local_sems.at[w]) for w in all_three]
    for made in here:
        made.start()
    staged_of = lambda k: staged_ref.at[pl.ds(k * quarter, quarter)]
    fetches = [pltpu.make_async_copy(quarter_of(k), staged_of(k), local_sems.at[3 + k]) for k in range(4)]
    stores = [pltpu.make_async_copy(staged_of(k), slot_of(k), local_sems.at[7 + k]) for k in range(4)]
    for made in fetches:
        made.start()

    def rows_copy(number, source, target, device):
        return pltpu.make_async_remote_copy(
            src_ref=source,
            dst_ref=target,
            send_sem=rows_send.at[number],
            recv_sem=rows_recv.at[number],
            device_id=device,
            device_id_type=MESH,
        )

    over = rows_copy(0, quarter_of(0), slot_of(4), pair)
    across = rows_copy(1, slot_of(4), slot_of(6), far)
    near = [rows_copy(2 + k, slot_of(4 + 2 * k), slot_of(5 + 2 * k), core) for k in range(2)]
    over.start()

    for step in range(1, line):

        @pl.when(place - step >= 0)
        def _(step=step):
            where = place - step
            for which in all_three:
                line_copy(which, True, where).wait_recv()

                @pl.when(place < last)
                def _(which=which):
                    line_copy(which, True, where).start()

                side_copy(which, where).start()

        @pl.when(place + step <= last)
        def _(step=step):
            where = place + step
            for which in all_three:
                line_copy(which, False, where).wait_recv()

                @pl.when(place > 0)
                def _(which=which):
                    line_copy(which, False, where).start()

                side_copy(which, where).start()

        if step == 1:
            for fetch, store in zip(fetches, stores):
                fetch.wait()
                store.start()
            over.wait_recv()
            across.start()
            near[0].start()

    across.wait_recv()
    near[1].start()
    for made in here + stores:
        made.wait()
    for where in range(line):
        for which in all_three:
            side_arrival(which, where).wait_recv()
            side_copy(which, where).wait_send()

            @pl.when((where <= place) & (place < last))
            def _(which=which, where=where):
                line_copy(which, True, where).wait_send()

            @pl.when((where >= place) & (place > 0))
            def _(which=which, where=where):
                line_copy(which, False, where).wait_send()

    for k in range(2):
        near[k].wait_recv()
        near[k].wait_send()
    over.wait_send()
    across.wait_send()


def call_gather_weights(dp_size, grads, *owns):
    line = dp_size // 2
    hbm = pl.BlockSpec(memory_space=pl.ANY)
    return pl.pallas_call(
        functools.partial(gather_weights, line),
        in_specs=[hbm] * 4,
        out_specs=[hbm] * 4,
        out_shape=[
            *[jax.ShapeDtypeStruct((dp_size * own.shape[0], own.shape[1]), own.dtype) for own in owns],
            jax.ShapeDtypeStruct((2 * grads.shape[0], grads.shape[1]), grads.dtype),
        ],
        scratch_shapes=[
            pltpu.SemaphoreType.DMA((11,)),
            pltpu.SemaphoreType.DMA((3, line)),
            pltpu.SemaphoreType.DMA((3, line)),
            pltpu.SemaphoreType.DMA((3, 2, line)),
            pltpu.SemaphoreType.DMA((3, 2, line)),
            pltpu.SemaphoreType.DMA((4,)),
            pltpu.SemaphoreType.DMA((4,)),
            pltpu.VMEM(grads.shape, grads.dtype),
        ],
        compiler_params=pltpu.CompilerParams(
            collective_id=4, has_side_effects=True, vmem_limit_bytes=16 * 2**20
        ),
        cost_estimate=lasting(120),
        name="gather_weights",
    )(*owns, grads)


def combine_all(line, early_ref, small_ref, gate_up_ref, out_ref, *exchange):
    everyone = Everyone(line, *exchange)
    greet(everyone.partners())
    lanes = lax.broadcasted_iota(jnp.int32, early_ref.shape, 1)
    adds = lax.broadcasted_iota(jnp.int32, early_ref.shape, 0) < 8
    fold = lambda left, right: jnp.where(adds, left + right, jnp.maximum(left, right))
    value = early_ref[...]
    gate_up = jnp.sum(jnp.sum(gate_up_ref[...], 0, keepdims=True), 1, keepdims=True)
    terms = [small_ref[k : k + 1, :] for k in range(SMALL)] + [jnp.broadcast_to(gate_up, (1, HEAD))]
    for term, number in zip(terms, (0, 1, 2, 3, 6, 4)):
        value = jnp.where(adds & (lanes == 7 + number), term, value)
    everyone.near_ref[everyone.code] = value
    everyone.send_near()
    everyone.send_line(fold)
    out_ref[...] = everyone.result(fold)


def call_combine_all(dp_size, early, small, gate_up):
    line = dp_size // 2
    return pl.pallas_call(
        functools.partial(combine_all, line),
        in_specs=[WHOLE] * 3,
        out_specs=WHOLE,
        out_shape=jax.ShapeDtypeStruct(early.shape, F32),
        scratch_shapes=Everyone.scratch(line, early.shape),
        compiler_params=pltpu.CompilerParams(collective_id=6, has_side_effects=True),
        cost_estimate=lasting(10),
        name="combine_all",
    )(early, small, gate_up)


class Links:
    def __init__(self, dp_size, mp_size):
        self.dp, self.mp, self.line = dp_size, mp_size, dp_size // 2
        self.index = lax.axis_index("dp")
        self.place, self.side, self.rank = self.index // 2, self.index % 2, lax.axis_index("mp")
        self.lines = [[place * 2 + side for place in range(self.line)] for side in range(2)]

    def swap_mp(self, value, bit):
        return lax.ppermute(value, "mp", [(i, i ^ bit) for i in range(self.mp)])

    def swap_side(self, value):
        return lax.ppermute(value, "dp", [(i, i ^ 1) for i in range(self.dp)])

    def gather_line(self, own):
        return lax.all_gather(own, "dp", axis=0, tiled=True, axis_index_groups=self.lines)

    def sum_line(self, parts):
        return lax.psum_scatter(parts, "dp", scatter_dimension=0, tiled=True, axis_index_groups=self.lines)


    def to_slots(self, values):
        rows = values.shape[0] // self.mp
        return jnp.concatenate(
            [lax.dynamic_slice_in_dim(values, (self.rank ^ k) * rows, rows, 0) for k in range(self.mp)], 0
        )

    def from_slots(self, values):
        rows = values.shape[0] // self.mp
        cuts = [values[k * rows : (k + 1) * rows] for k in range(self.mp)]
        odd = (self.rank & 1) == 1
        high = (self.rank & 2) == 2
        cuts = [jnp.where(odd, cuts[k ^ 1], cuts[k]) for k in range(self.mp)]
        cuts = [jnp.where(high, cuts[k ^ 2], cuts[k]) for k in range(self.mp)]
        return jnp.concatenate(cuts, 0)

    def own_quarter(self, values):
        rows = values.shape[0] // self.mp
        return lax.dynamic_slice_in_dim(values, self.rank * rows, rows, 0)

    def gather_core(self, quarter, far):
        rows = quarter.shape[0]
        near = self.swap_mp(jnp.concatenate([quarter, far], 0), 1)
        return jnp.concatenate([quarter, near[:rows], far, near[rows:]], 0)

    def swap_core(self, slots):
        rows = slots.shape[0] // 8
        picked = lambda ks: jnp.concatenate([slots[k * rows : (k + 1) * rows] for k in ks], 0)
        return slots, self.swap_mp(picked((1, 3, 5, 7)), 1)

    def sum_core(self, slots, near):
        rows = slots.shape[0] // 8
        add = lambda ks, low: jnp.concatenate(
            [
                slots[k * rows : (k + 1) * rows].astype(F32) + near[i * rows : (i + 1) * rows].astype(F32)
                for i, k in enumerate(ks, low)
            ],
            0,
        ).astype(BF16)
        return add((0, 2), 0), add((4, 6), 2)


def after(value, *others):
    return lax.optimization_barrier((value, *others))[0]


def inverse_rms(values):
    return lax.rsqrt(jnp.mean(values * values, -1, keepdims=True) + NORM_EPS)


def body(
    dp_size,
    mp_size,
    tokens,
    cotangent,
    segment_ids,
    w_query,
    w_key,
    w_value,
    w_out,
    w_gate_up,
    w_down,
    norm_gains,
    query_moments,
    key_moments,
    value_moments,
    out_moments,
    gate_up_moments,
    down_moments,
    gains_moments,
):
    links = Links(dp_size, mp_size)
    line, side = links.line, links.side
    heads = w_query.shape[1] // HEAD
    kvs = w_key.shape[1] // HEAD
    group = heads // kvs
    width = tokens.shape[1]
    shard = w_query.shape[0]
    units = w_gate_up.shape[2]
    block = units // (line * 2)

    def interleave(query, key, value):
        parts = []
        for kv in range(kvs):
            parts.append(query[..., kv * group * HEAD : (kv + 1) * group * HEAD])
            parts.append(key[..., kv * HEAD : (kv + 1) * HEAD])
            parts.append(value[..., kv * HEAD : (kv + 1) * HEAD])
        return jnp.concatenate(parts, -1)

    by_side = w_gate_up.reshape(2, shard, line, 2, block)

    def side_units(which):
        cut = lax.dynamic_index_in_dim(by_side, which, 3, keepdims=False).astype(BF16)
        return jnp.concatenate([cut[0].reshape(shard, -1), cut[1].reshape(shard, -1)], 1)

    inputs = tokens.astype(F32)
    scale_one = inverse_rms(inputs)
    down_full = links.gather_line(w_down.astype(BF16))
    own_units = side_units(side)
    sent_units = links.swap_side(side_units(1 - side))
    rows_pair = jnp.zeros((2 * shard, own_units.shape[1]), BF16)
    rows_pair = lax.dynamic_update_slice(rows_pair, own_units, (side * shard, 0))
    rows_pair = lax.dynamic_update_slice(rows_pair, sent_units, ((1 - side) * shard, 0))
    gate_up_full = after(links.gather_line(rows_pair), down_full)
    gains_low = norm_gains.astype(BF16).astype(F32)
    gains_rows = jnp.concatenate([gains_low, jnp.zeros((6, gains_low.shape[1]), F32)], 0)
    qkv_full, out_full, gains_shards, grad_rows = call_gather_weights(
        dp_size,
        cotangent,
        after(interleave(w_query, w_key, w_value).astype(BF16), rows_pair, scale_one),
        w_out.astype(BF16),
        gains_rows,
    )
    gains_full = jnp.transpose(gains_shards.reshape(dp_size, 8, -1), (1, 0, 2)).reshape(8, width)

    quarter = tokens.shape[0] // 4

    cosine, sine = rope_tables(segment_ids.shape[1])
    normed_one = (inputs * scale_one * gains_full[0]).astype(BF16)
    qkv = jnp.dot(normed_one, qkv_full, preferred_element_type=F32)
    rank_ref = links.rank.astype(jnp.int32).reshape(1)
    mixed_slots, rotated, lse, peaks = attention_forward(rank_ref, qkv, cosine, sine, segment_ids, group, kvs)
    tokens_own = links.own_quarter(tokens)
    rows_two, middle = call_spread_forward(
        jnp.dot(mixed_slots, out_full, preferred_element_type=F32).astype(BF16), tokens_own, gains_full[1:2]
    )

    columns = line * block
    grad_hidden = dot_nt(grad_rows, down_full)
    grad_hidden, gate_up_full = lax.optimization_barrier((grad_hidden, gate_up_full))
    both = jnp.dot(rows_two, gate_up_full, preferred_element_type=F32)
    gate, up = both[:, :columns], both[:, columns:]
    sigmoid = jax.nn.sigmoid(gate)
    hidden = (gate * sigmoid * up).astype(BF16)
    grad_gate = (grad_hidden * up * sigmoid * (1.0 + gate * (1.0 - sigmoid))).astype(BF16)
    grad_up = (grad_hidden * gate * sigmoid).astype(BF16)
    output_part = jnp.dot(hidden, down_full, preferred_element_type=F32).astype(BF16)
    output_part, output_near = links.swap_core(output_part)
    grad_down_part = dot_tn(after(hidden, output_part), grad_rows).astype(BF16)
    grad_gate_part = dot_tn(after(rows_two, grad_down_part), grad_gate).astype(BF16)
    grad_both = after(jnp.concatenate([grad_gate, grad_up], 1), grad_gate_part)
    back = dot_nt(grad_both, gate_up_full).astype(BF16)
    grad_middle_slots, grad_middle, gain_two = call_spread_backward(
        after(back, output_near), middle, links.own_quarter(cotangent), gains_full[1:2]
    )
    output_mine, output_theirs = links.sum_core(output_part, after(output_near, grad_middle_slots))
    grad_down_low = links.sum_line(grad_down_part)
    grad_up_part = dot_tn(after(rows_two, output_theirs, grad_down_low), grad_up).astype(BF16)
    gate_sum = after(links.sum_line(grad_gate_part), grad_down_low)
    up_sum = after(links.sum_line(grad_up_part), gate_sum)
    grad_middle_slots = after(grad_middle_slots, grad_up_part)
    grad_mixed = dot_nt(grad_middle_slots, out_full).astype(BF16)

    grad_down = grad_down_low.astype(F32)
    down_second, down_direction = lamb_direction(w_down, down_moments[0], down_moments[1], grad_down)
    down_sum = jnp.sum(down_direction * down_direction)

    local_peak = peaks[:, :group, 0].reshape(heads)
    peak_vector = lax.dynamic_update_slice(
        jnp.full((HEADS,), MASKED, F32), local_peak, (links.rank * heads,)
    )
    owner = (links.rank == 0).astype(F32)
    lanes = lax.broadcasted_iota(jnp.int32, (16, HEAD), 1)
    lower = lax.broadcasted_iota(jnp.int32, (16, HEAD), 0) < 8
    early = jnp.broadcast_to(jnp.pad(peak_vector, (0, HEAD - HEADS), constant_values=MASKED), (16, HEAD))
    early = jnp.where(lower, 0.0, early)
    masters = (w_query, w_key, w_value, w_out, w_gate_up, w_down, norm_gains)
    for number, master in enumerate(masters):
        square = jnp.sum(master * master) * (owner if number == 6 else 1.0)
        early = jnp.where(lower & (lanes == number), square, early)
    early = jnp.where(lower & (lanes == 12), down_sum, early)

    grad_qkv = attention_backward(rank_ref, rotated, grad_mixed, lse, cosine, sine, segment_ids, group, kvs)
    grad_qkv_part = dot_tn(links.to_slots(normed_one), grad_qkv).astype(BF16)
    grad_out_part = dot_tn(mixed_slots, grad_middle_slots).astype(BF16)
    grad_normed_one = dot_nt(grad_qkv, qkv_full).astype(BF16)
    output_theirs = links.swap_side(output_theirs)
    output_pair = output_mine.astype(F32) + after(output_theirs, grad_qkv_part, grad_normed_one).astype(F32)
    output_far = links.swap_mp(output_pair[quarter:].astype(BF16), 2).astype(F32)
    input_slots, gain_terms, grad_qkv_own, grad_out = call_finish(
        dp_size,
        after(grad_normed_one, gate_sum, output_pair),
        tokens_own,
        grad_middle,
        gains_full[0:1],
        gain_two,
        grad_qkv_part,
        grad_out_part,
    )
    input_grad = links.from_slots(input_slots).astype(F32)
    output_low = (middle + output_pair[:quarter] + after(output_far, input_slots)).astype(BF16)
    output_far = links.swap_mp(output_low, 2)

    other_side = lambda value: lax.dynamic_slice_in_dim(value, (1 - side) * shard, shard, 0)
    summed = [gate_sum, up_sum]
    theirs = [links.swap_side(other_side(value)) for value in summed]
    grad_qkv_own = after(grad_qkv_own, theirs[0], other_side(up_sum))
    gain_terms = gain_terms.reshape(2, width)
    gain_width = norm_gains.shape[1]
    grad_gains = lax.dynamic_slice_in_dim(gain_terms, links.index * gain_width, gain_width, 1)

    small = (w_query, w_key, w_value, w_out, norm_gains)
    small_moments = (query_moments, key_moments, value_moments, out_moments, gains_moments)
    grad_query, grad_key, grad_value, *rest = call_small_step(
        group, kvs, jnp.full((1, HEAD), owner), grad_qkv_own, grad_out, grad_gains, small, small_moments
    )
    small_seconds, small_directions, small_sums = rest[:SMALL], rest[SMALL : 2 * SMALL], rest[2 * SMALL]
    if block % HEAD == 0:
        grad_gate_up, gate_up_second, gate_up_direction, gate_up_sums = call_gate_up_step(
            line, side.astype(jnp.int32).reshape(1), w_gate_up, gate_up_moments, summed, theirs
        )
    else:
        parts = []
        for j in range(2):
            mine = lax.dynamic_slice_in_dim(summed[j], side * shard, shard, 0)
            sides = [jnp.where(side == 0, mine, theirs[j]), jnp.where(side == 0, theirs[j], mine)]
            parts.append(jnp.stack([value.reshape(shard, line, block) for value in sides], 2))
        grad_gate_up = jnp.stack(parts, 0).reshape(w_gate_up.shape)
        grad_gate_up = grad_gate_up.astype(F32)
        gate_up_second, gate_up_direction = lamb_direction(
            w_gate_up, gate_up_moments[0], gate_up_moments[1], grad_gate_up
        )
        gate_up_sums = jnp.sum((gate_up_direction * gate_up_direction).reshape(-1, 8, 2 * HEAD), 0)
    output_far = after(output_far, gate_up_sums)
    block_output = links.from_slots(links.gather_core(output_low, output_far))
    packed = call_combine_all(dp_size, early, small_sums, gate_up_sums)
    updated = call_small_update(
        group, kvs, links.rank.astype(jnp.int32).reshape(1), packed, small, small_directions
    )
    flat_rows = lambda value: value.reshape(2 * shard, units)
    new_gate_up, copy_gate_up = (
        value.reshape(w_gate_up.shape)
        for value in call_large_update(4, packed, flat_rows(w_gate_up), flat_rows(gate_up_direction))
    )
    new_down, copy_down = call_large_update(5, packed, w_down, down_direction)
    grads = (grad_query, grad_key, grad_value, grad_out, grad_gate_up, grad_down, grad_gains)
    place_large = lambda values, gate_up, down: (*values[:4], gate_up, down, values[4])
    norms = jnp.sqrt(jnp.stack([packed[0, :7], packed[0, 7:14]]))
    return (
        block_output,
        input_grad,
        *grads,
        *place_large(small_seconds, gate_up_second, down_second),
        *place_large(updated[:SMALL], new_gate_up, new_down),
        *place_large(updated[SMALL:], copy_gate_up, copy_down),
        norms,
        packed[8, :HEADS],
    )


def solution(mesh):
    column = P("dp", "mp")
    row = P(("mp", "dp"), None)
    gate_up = P(None, "dp", "mp")
    gains = P(None, "dp")
    params = (column, column, column, row, gate_up, row, gains)
    moments = (
        P(None, "dp", "mp"),
        P(None, "dp", "mp"),
        P(None, "dp", "mp"),
        P(None, ("mp", "dp"), None),
        P(None, None, "dp", "mp"),
        P(None, ("mp", "dp"), None),
        P(None, None, "dp"),
    )
    tokens = P("dp", None)
    return jax.shard_map(
        functools.partial(body, mesh.shape["dp"], mesh.shape["mp"]),
        mesh=mesh,
        in_specs=(tokens, tokens, tokens, *params, *moments),
        out_specs=(tokens, tokens, *params, *params, *params, *params, P(), P()),
        check_vma=False,
    )
```

time: 903 us -> 778 us (0.86)
  local copies, waits for them, and re-layouts: 93.6 us -> 36.9 us
  matrix products: 201 us -> 145 us
  other arithmetic: 98 us -> 74.3 us
  Pallas kernels: 419 us -> 437 us
    pallas_call x1, Pallas kernels: 118 us -> 145 us  [call_gather_weights(): pl.pallas_call(functools.partial(gather_weights, line), in_specs=[hbm] *...]
    dot_general x6 -> x4, matrix products: 70.9 us -> 46.8 us  [dot_nt(): lax.dot_general(left, right, (((1,), (1,)), ((), ())), preferred_element_...]
    ppermute x6 -> x4, waiting for transfers between devices: 34.7 us -> 56.4 us  [swap_side(): return lax.ppermute(value, 'dp', [(i, i ^ 1) for i in range(self.dp)])]
    dot_general x4 -> x2, matrix products: 57.2 us -> 36 us  [the longest x1 21.7 us: body(): both = jnp.dot(rows_two, gate_up_full, preferred_element_type=F32)]
    reduce_sum x13 -> x6, other arithmetic: 33.8 us -> 12.9 us  [the longest x5 6.63 us: body(): square = jnp.sum(master * master) * (owner if number == 6 else 1.0)]
    another operation x6 -> x2, local copies, waits for them, and re-layouts: 18.4 us -> 0.09 us  [the longest x1 0.08 us: body(): local_peak = peaks[:, :group, 0].reshape(heads)]
    ppermute x5 -> x4, waiting for transfers between devices: 17.2 us -> 0.01 us  [swap_mp(): return lax.ppermute(value, 'mp', [(i, i ^ bit) for i in range(self.mp)])]
    pallas_call x1, Pallas kernels: 77.8 us -> 61.7 us  [call_spread_forward(): pl.pallas_call(spread_forward, in_specs=[WHOLE] * 3, out_specs=[WHOLE] *...]
  transfers between devices with their start and end apart: 21 -> 13, of which waited for: 6 -> 4; matrix products, arithmetic and copies ran while one was open for 42% -> 22% of each run, Pallas kernels for 47% -> 57%
where the time goes in v3:
time: 778 us; the launch traced here: 773 us
  Pallas kernels  437 us (56%)
  matrix products  145 us (19%)
  other arithmetic  74.3 us (10%)
  waiting for transfers between devices  56.5 us (7%)
  local copies, waits for them, and re-layouts  36.9 us (5%)
  between operations  15.9 us (2%)
    pallas_call x1, Pallas kernels, call_gather_weights(): pl.pallas_call(functools.partial(gather_weights, line), in_specs=[hbm] *...  145 us
    pallas_call x1, Pallas kernels, call_finish(): pl.pallas_call(functools.partial(finish, line), in_specs=[WHOLE] * 7, out...  96.6 us
    pallas_call x1, Pallas kernels, call_spread_backward(): pl.pallas_call(spread_backward, in_specs=[WHOLE] * 4, out_specs=[WHOLE] *...  67.2 us
    pallas_call x1, Pallas kernels, call_spread_forward(): pl.pallas_call(spread_forward, in_specs=[WHOLE] * 3, out_specs=[WHOLE] *...  61.7 us
    ppermute x4, waiting for transfers between devices, swap_side(): return lax.ppermute(value, 'dp', [(i, i ^ 1) for i in range(self.dp)])  56.4 us
    dot_general x5, matrix products, dot_tn(): lax.dot_general(left, right, (((0,), (0,)), ((), ())), preferred_element_...  51.6 us
    dot_general x4, matrix products, dot_nt(): lax.dot_general(left, right, (((1,), (1,)), ((), ())), preferred_element_...  46.8 us
    dot_general x1, matrix products, body(): both = jnp.dot(rows_two, gate_up_full, preferred_element_type=F32)  21.7 us
  transfers between devices with their start and end apart: 13, of which 4 were waited for; matrix products, arithmetic and copies ran while one was open for 22% of the time, Pallas kernels for 57%

profile of v3, /device:TPU:0, one launch (start us, length us, event | category | flops | bytes accessed | tf_op | source)
XLA Modules:
  0.0 772.7 jit_solution(4684151146713851903)
XLA Ops:
  18.0 23.2 %collective-permute-done = bf16[256,2048]{0,1:T(8,128)(2,1)} collective-permute-done((bf16[256,2048]{0,1:T(8,128)(2,1)}, bf16[256,2048]{0,1:T(8,128)(2,1)}, u32[]{:S(2)}, u32[]{:S(2)}) %collective-permute-start) | collective-permute-done | bytes 1048608 | tf_op jit(solution)/shard_map/ppermute | solution.py:1091
  50.6 144.7 %gather_weights.1 = (bf16[2048,1024]{1,0:T(8,128)(2,1)S(1)}, bf16[512,2048]{1,0:T(8,128)(2,1)S(1)}, f32[64,256]{1,0:T(8,128)S(1)}, bf16[2048,2048]{1,0:T(8,128)(2,1)S(1)}) custom-call(bf16[256,1024]{1,0:T(8,128)(2,1)S(1)} %slice_dynamic-update-slice_fusion.2.own_ref, bf16[64,2048]{1,0:T(8,128)(2,1)S(1)} %get-tuple-element.201.out_ref, ...), custom_call_target="tpu_custom_call" | custom-call | bytes 360000000 | tf_op jit(solution)/shard_map/gather_weights/pallas_call | solution.py:1023
  210.1 11.4 %attention_forward.1 = (bf16[1024,512]{1,0:T(8,128)(2,1)S(1)}, bf16[1024,1024]{1,0:T(8,128)(2,1)S(1)}, f32[1024,512]{1,0:T(8,128)}, f32[2,8,128]{2,1,0:T(8,128)S(1)}) custom-call(s32[1]{0:T(128)} %bitcast.rank_ref, f32[1024,1024]{1,0:T(8,128)} %fusion.29.qkv_ref, f32[1024,128]{1,0:T(8,128)S(1)} %get-tuple-element.220.cos_ref, ...), custom_call_target="tpu_custom_call" | custom-call | bytes 36000000 | tf_op jit(solution)/shard_map/attention_forward/pallas_call | solution.py:146
  225.9 61.7 %spread_forward.1 = (bf16[2048,2048]{1,0:T(8,128)(2,1)}, f32[256,2048]{1,0:T(8,128)S(1)}) custom-call(bf16[1024,2048]{1,0:T(8,128)(2,1)} %convolution_convert_fusion.3.part_ref, bf16[256,2048]{1,0:T(8,128)(2,1)S(1)} %constant_dynamic-slice_fusion.8.tokens_ref, f32[1,2048]{1,0:T(1,128)S(1)} %bitcast.59), custom_call_target="tpu_custom_call" | custom-call | bytes 192000000 | tf_op jit(solution)/shard_map/spread_forward/pallas_call | solution.py:519
  288.9 14.7 %fusion.30 = f32[2048,1024]{1,0:T(8,128)} fusion(bf16[2048,2048]{1,0:T(8,128)(2,1)} %copy-done.33, bf16[1024,2048]{1,0:T(8,128)(2,1)} %all-gather.3.cloned.1.call-done), kind=kOutput, calls=%fused_computation.123 | convolution fusion | flops 8589934592 | bytes 20971520 | tf_op jit(solution)/shard_map/dot_general | solution.py:53
  303.7 21.7 %fusion.31 = f32[2048,2048]{1,0:T(8,128)S(1)} fusion(bf16[2048,2048]{1,0:T(8,128)(2,1)} %get-tuple-element.117, bf16[2048,2048]{0,1:T(8,128)(2,1)} %all-gather.5.cloned.1.call-done), kind=kOutput, calls=%fused_computation.124 | convolution fusion | flops 17179869184 | bytes 33554432 | tf_op jit(solution)/shard_map/dot_general | solution.py:1229
  325.3 11.6 %multiply_convert_fusion.1 = (bf16[2048,1024]{1,0:T(8,128)(2,1)}, bf16[2048,1024]{1,0:T(8,128)(2,1)}, bf16[2048,1024]{1,0:T(8,128)(2,1)}) fusion(f32[2048,1024]{1,0:T(8,128)} %fusion.30, f32[2048,2048]{1,0:T(8,128)S(1)} %fusion.31), kind=kLoop, calls=%fused_computation.7 | loop fusion | flops 33554432 | bytes 37748736 | tf_op jit(solution)/shard_map/convert_element_type | solution.py:1233
  336.9 14.3 %convolution_convert_fusion.1 = bf16[2048,2048]{1,0:T(8,128)(2,1)} fusion(bf16[2048,1024]{1,0:T(8,128)(2,1)} %get-tuple-element.110, bf16[1024,2048]{1,0:T(8,128)(2,1)} %all-gather.3.cloned.1.call-done), kind=kOutput, calls=%fused_computation.11 | convolution fusion | flops 8594128896 | bytes 16777216 | tf_op jit(solution)/shard_map/dot_general | solution.py:1235
  351.3 11.1 %convolution_convert_fusion.2 = bf16[1024,2048]{1,0:T(8,128)(2,1)} fusion(bf16[2048,1024]{1,0:T(8,128)(2,1)S(1)} %copy-done.47, bf16[2048,2048]{1,0:T(8,128)(2,1)S(1)} %bitcast.66), kind=kOutput, calls=%fused_computation.26 | convolution fusion | flops 8592031744 | bytes 16777216 | tf_op jit(solution)/shard_map/dot_general | solution.py:61
  362.4 14.0 %convolution_convert_fusion.6 = bf16[2048,1024]{1,0:T(8,128)(2,1)} fusion(bf16[2048,2048]{1,0:T(8,128)(2,1)} %get-tuple-element.117, bf16[2048,1024]{1,0:T(8,128)(2,1)} %get-tuple-element.170), kind=kOutput, calls=%fused_computation.30 | convolution fusion | flops 8592031744 | bytes 16777216 | tf_op jit(solution)/shard_map/dot_general | solution.py:61
  384.7 8.4 %pad_maximum_fusion = bf16[2048,2048]{1,0:T(8,128)(2,1)} fusion(bf16[2048,1024]{1,0:T(8,128)(2,1)} %get-tuple-element.171, bf16[2048,1024]{1,0:T(8,128)(2,1)} %get-tuple-element.170), kind=kLoop, calls=%fused_computation.5 | loop fusion | flops 16777216 | bytes 16777216 | tf_op jit(solution)/shard_map/concatenate | solution.py:1239
  393.1 23.6 %convolution_convert_fusion.part_ref = bf16[2048,2048]{1,0:T(8,128)(2,1)} fusion(bf16[2048,2048]{1,0:T(8,128)(2,1)} %pad_maximum_fusion, bf16[2048,2048]{0,1:T(8,128)(2,1)} %all-gather.5.cloned.1.call-done), kind=kOutput, calls=%fused_computation.10 | convolution fusion | flops 17184063488 | bytes 25165824 | tf_op jit(solution)/shard_map/dot_general | solution.py:53
  416.7 67.2 %spread_backward.1 = (bf16[1024,2048]{1,0:T(8,128)(2,1)}, f32[256,2048]{1,0:T(8,128)}, f32[8,2048]{1,0:T(8,128)}) custom-call(bf16[2048,2048]{1,0:T(8,128)(2,1)} %convolution_convert_fusion.part_ref, f32[256,2048]{1,0:T(8,128)} %copy-done.1, bf16[256,2048]{1,0:T(8,128)(2,1)} %constant_dynamic-slice_fusion.7.grad_ref, f32[1,2048]{1,0:T(1,128)} %bitcast.60), custom_call_target="tpu_custom_call" | custom-call | bytes 204000000 | tf_op jit(solution)/shard_map/spread_backward/pallas_call | solution.py:615
  489.8 14.2 %convolution_convert_fusion.5 = bf16[2048,1024]{1,0:T(8,128)(2,1)} fusion(bf16[2048,2048]{1,0:T(8,128)(2,1)} %get-tuple-element.117, bf16[2048,1024]{1,0:T(8,128)(2,1)} %get-tuple-element.171), kind=kOutput, calls=%fused_computation.29 | convolution fusion | flops 8592031744 | bytes 16777216 | tf_op jit(solution)/shard_map/dot_general | solution.py:61
  512.7 13.6 %attention_backward.1 = bf16[1024,1024]{1,0:T(8,128)(2,1)S(1)} custom-call(s32[1]{0:T(128)} %bitcast.rank_ref, bf16[1024,1024]{1,0:T(8,128)(2,1)} %copy-done.17, bf16[1024,512]{1,0:T(8,128)(2,1)S(1)} %convolution_convert_fusion.8.grad_ref, f32[1024,512]{1,0:T(8,128)} %get-tuple-element.119.lse_ref, f32[1024,128]{1,0:T(8,128)S(1)} %copy-done.9, ...), custom_call_target="tpu_custom_call" | custom-call | bytes 39000000 | tf_op jit(solution)/shard_map/attention_backward/pallas_call | solution.py:169
  526.4 6.1 convolution_convert_fusion.4.part_ref
  532.5 6.4 fusion.11.refs_1_
  538.9 17.8 %collective-permute-done.2 = bf16[512,2048]{1,0:T(8,128)(2,1)S(1)} collective-permute-done((bf16[512,2048]{1,0:T(8,128)(2,1)S(1)}, bf16[512,2048]{1,0:T(8,128)(2,1)S(1)}, u32[]{:S(2)}, u32[]{:S(2)}) %collective-permute-start.2) | collective-permute-done | bytes 2097184 | tf_op jit(solution)/shard_map/ppermute | solution.py:1091
  567.0 96.6 %finish.1 = (bf16[1024,2048]{1,0:T(8,128)(2,1)}, f32[8,512]{1,0:T(8,128)}, f32[256,1024]{1,0:T(8,128)}, f32[64,2048]{1,0:T(8,128)}) custom-call(bf16[1024,2048]{1,0:T(8,128)(2,1)} %convolution_convert_fusion.4.part_ref, bf16[256,2048]{1,0:T(8,128)(2,1)} %copy-done, f32[256,2048]{1,0:T(8,128)} %get-tuple-element.123.total_ref, f32[1,2048]{1,0:T(1,128)} %bitcast.75, ...), custom_call_target="tpu_custom_call" | custom-call | bytes 255000000 | tf_op jit(solution)/shard_map/finish/pallas_call | solution.py:822
  682.1 9.4 %collective-permute-done.6.refs_3_ = bf16[256,1024]{1,0:T(8,128)(2,1)S(1)} collective-permute-done((bf16[256,1024]{1,0:T(8,128)(2,1)}, bf16[256,1024]{1,0:T(8,128)(2,1)S(1)}, u32[]{:S(2)}, u32[]{:S(2)}) %collective-permute-start.6) | collective-permute-done | bytes 524320 | tf_op jit(solution)/shard_map/ppermute | solution.py:1091
  692.2 16.5 %gate_up_step.1 = (f32[2,256,2048]{2,1,0:T(8,128)}, f32[2,256,2048]{2,1,0:T(8,128)}, f32[2,256,2048]{2,1,0:T(8,128)}, f32[8,256]{1,0:T(8,128)}) custom-call(s32[1]{0:T(128)} %bitcast.10.side_ref, f32[2,256,2048]{2,1,0:T(8,128)} %master_ref.2, f32[2,2,256,2048]{3,2,1,0:T(8,128)} %moment_ref.1, bf16[512,1024]{1,0:T(8,128)(2,1)} %reduce-scatter.6.cloned.1.call-done.refs_0_, ...), custom_call_target="tpu_custom_call" | custom-call | bytes 48000000 | tf_op jit(solution)/shard_map/gate_up_step/pallas_call | solution.py:214
  711.7 6.3 multiply_reduce_fusion.2
  735.2 10.5 %combine_all.1.packed_ref = f32[16,128]{1,0:T(8,128)} custom-call(f32[16,128]{1,0:T(8,128)} %select_select_fusion.early_ref, f32[8,128]{1,0:T(8,128)} %copy-done.32, f32[8,256]{1,0:T(8,128)} %get-tuple-element.128.gate_up_ref), custom_call_target="tpu_custom_call" | custom-call | bytes 30000000 | tf_op jit(solution)/shard_map/combine_all/pallas_call | solution.py:1068
  749.4 7.0 large_update.2
  (230 shorter events, 124.8 us)
Async XLA Ops:
  7.2 281.7 %all-gather.3.cloned.1.call-start = ((), (), s32[]{:S(2)}) async-start(), calls=%async_computation.3 | async-start | bytes 5242880 | tf_op jit(solution)/shard_map/all_gather | solution.py:1094
  10.0 293.7 %all-gather.5.cloned.1.call-start = ((), (), s32[]{:S(2)}) async-start(), calls=%async_computation.4 | async-start | bytes 10485760 | tf_op jit(solution)/shard_map/all_gather | solution.py:1094
  14.8 26.4 %collective-permute-start = (bf16[256,2048]{0,1:T(8,128)(2,1)}, bf16[256,2048]{0,1:T(8,128)(2,1)}, u32[]{:S(2)}, u32[]{:S(2)}) collective-permute-start(bf16[256,2048]{0,1:T(8,128)(2,1)} %pad_maximum_fusion.5), channel_id=1, source_target_pairs={{0,4},{4,0},{8,12},{12,8},{16,20},{20,16},{24,28},{28,24},{1,5},{5... | collective-permute-start | bytes 3145736 | tf_op jit(solution)/shard_map/ppermute | solution.py:1091
  17.7 26.2 %copy-start.27 = (s32[1,1024]{1,0:T(1,128)S(1)}, s32[1,1024]{1,0:T(1,128)}, u32[]{:S(2)}) copy-start(s32[1,1024]{1,0:T(1,128)} %param.19) | copy-start | bytes 12292
  17.7 26.5 %copy-start.28 = (f32[2,256]{1,0:T(2,128)S(1)}, f32[2,256]{1,0:T(2,128)}, u32[]{:S(2)}) copy-start(f32[2,256]{1,0:T(2,128)} %refs_4_.3) | copy-start | bytes 6148
  43.9 445.9 %reduce-scatter.4.cloned.1.call-start = ((), (), s32[]{:S(2)}) async-start(), calls=%async_computation.5 | async-start | bytes 5242880 | tf_op jit(solution)/shard_map/reduce_scatter | solution.py:1097
  47.2 163.0 %copy-start.8 = (f32[1024,128]{1,0:T(8,128)}, f32[1024,128]{1,0:T(8,128)S(1)}, u32[]{:S(2)}) copy-start(f32[1024,128]{1,0:T(8,128)S(1)} %get-tuple-element.220.cos_ref) | copy-start | bytes 1572868
  47.2 163.0 %copy-start.10 = (f32[1024,128]{1,0:T(8,128)}, f32[1024,128]{1,0:T(8,128)S(1)}, u32[]{:S(2)}) copy-start(f32[1024,128]{1,0:T(8,128)S(1)} %get-tuple-element.221.sin_ref) | copy-start | bytes 1572868
  50.5 175.4 %copy-start = (bf16[256,2048]{1,0:T(8,128)(2,1)}, bf16[256,2048]{1,0:T(8,128)(2,1)S(1)}, u32[]{:S(2)}) copy-start(bf16[256,2048]{1,0:T(8,128)(2,1)S(1)} %constant_dynamic-slice_fusion.8.tokens_ref) | copy-start | bytes 3145732
  198.6 22.9 %copy-start.36 = (bf16[512,2048]{1,0:T(8,128)(2,1)}, bf16[512,2048]{1,0:T(8,128)(2,1)S(1)}, u32[]{:S(2)}) copy-start(bf16[512,2048]{1,0:T(8,128)(2,1)S(1)} %get-tuple-element.103) | copy-start | bytes 6291460
  199.3 26.6 %copy-start.26 = (f32[1,1,8,256]{3,1,2,0:T(1,128)}, f32[1,1,8,256]{3,1,2,0:T(1,128)S(1)}, u32[]{:S(2)}) copy-start(f32[1,1,8,256]{3,1,2,0:T(1,128)S(1)} %copy.65) | copy-start | bytes 24580
  325.3 25.9 %slice-start = ((s8[8388608]{0:T(1024)(128)(4,1)}), s8[4194304]{0:T(1024)(128)(4,1)S(1)}, s32[]{:S(2)}) async-start(s8[8388608]{0:T(1024)(128)(4,1)} %bitcast.65), calls=%async_computation.8 | async-start | bytes 8388608
  336.9 14.3 %copy-start.47 = (bf16[2048,1024]{1,0:T(8,128)(2,1)S(1)}, bf16[2048,1024]{1,0:T(8,128)(2,1)}, u32[]{:S(2)}) copy-start(bf16[2048,1024]{1,0:T(8,128)(2,1)} %get-tuple-element.110) | copy-start | bytes 12582916
  362.4 198.7 %reduce-scatter.6.cloned.1.call-start = ((), (), s32[]{:S(2)}) async-start(), calls=%async_computation.6 | async-start | bytes 5242880 | tf_op jit(solution)/shard_map/reduce_scatter | solution.py:1097
  376.5 291.2 %reduce-scatter.8.cloned.1.call-start = ((), (), s32[]{:S(2)}) async-start(), calls=%async_computation.7 | async-start | bytes 5242880 | tf_op jit(solution)/shard_map/reduce_scatter | solution.py:1097
  382.0 34.7 %collective-permute-start.1 = (bf16[1024,2048]{1,0:T(8,128)(2,1)}, bf16[1024,2048]{1,0:T(8,128)(2,1)}, u32[]{:S(2)}, u32[]{:S(2)}) collective-permute-start(bf16[1024,2048]{1,0:T(8,128)(2,1)} %pad_maximum_fusion.1), channel_id=1, source_target_pairs={{0,1},{1,0},{2,3},{3,2},{4,5},{5,4},{6,7},{7,6},{8,9},{9,8},{10,11... | collective-permute-start | bytes 12582920 | tf_op jit(solution)/shard_map/ppermute | solution.py:1088
  508.7 48.0 %collective-permute-start.2 = (bf16[512,2048]{1,0:T(8,128)(2,1)S(1)}, bf16[512,2048]{1,0:T(8,128)(2,1)S(1)}, u32[]{:S(2)}, u32[]{:S(2)}) collective-permute-start(bf16[512,2048]{1,0:T(8,128)(2,1)S(1)} %copy-done.50), channel_id=1, source_target_pairs={{0,4},{4,0},{8,12},{12,8},{16,20},{20,16},{24,28},{28,24},{1,5},{5... | collective-permute-start | bytes 6291464 | tf_op jit(solution)/shard_map/ppermute | solution.py:1091
  559.6 104.0 %collective-permute-start.3 = (bf16[256,2048]{1,0:T(8,128)(2,1)S(1)}, bf16[256,2048]{1,0:T(8,128)(2,1)S(1)}, u32[]{:S(2)}, u32[]{:S(2)}) collective-permute-start(bf16[256,2048]{1,0:T(8,128)(2,1)S(1)} %slice.299), channel_id=1, source_target_pairs={{0,2},{1,3},{2,0},{3,1},{4,6},{5,7},{6,4},{7,5},{8,10},{9,11},{10,... | collective-permute-start | bytes 3145736 | tf_op jit(solution)/shard_map/ppermute | solution.py:1088
  567.0 96.9 %copy-start.44 = (f32[512,2048]{1,0:T(8,128)S(1)}, f32[512,2048]{1,0:T(8,128)}, u32[]{:S(2)}) copy-start(f32[512,2048]{1,0:T(8,128)} %copy-done.43) | copy-start | bytes 12582916
  665.8 43.0 %copy-start.45 = (bf16[256,2048]{1,0:T(8,128)(2,1)}, bf16[256,2048]{1,0:T(8,128)(2,1)S(1)}, u32[]{:S(2)}) copy-start(bf16[256,2048]{1,0:T(8,128)(2,1)S(1)} %fusion.18) | copy-start | bytes 3145732
  665.8 42.9 %collective-permute-start.4 = (bf16[256,2048]{1,0:T(8,128)(2,1)S(1)}, bf16[256,2048]{1,0:T(8,128)(2,1)S(1)}, u32[]{:S(2)}, u32[]{:S(2)}) collective-permute-start(bf16[256,2048]{1,0:T(8,128)(2,1)S(1)} %fusion.18), channel_id=1, source_target_pairs={{0,2},{1,3},{2,0},{3,1},{4,6},{5,7},{6,4},{7,5},{8,10},{9,11},{10,... | collective-permute-start | bytes 3145736 | tf_op jit(solution)/shard_map/ppermute | solution.py:1088
  667.0 15.1 %collective-permute-start.5 = (bf16[256,1024]{1,0:T(8,128)(2,1)}, bf16[256,1024]{1,0:T(8,128)(2,1)S(1)}, u32[]{:S(2)}, u32[]{:S(2)}) collective-permute-start(bf16[256,1024]{1,0:T(8,128)(2,1)} %constant_dynamic-slice_fusion.2), channel_id=1, source_target_pairs={{0,4},{4,0},{8,12},{12,8},{16,20},{20,16},{24,28},{28,24},{1,5},{5... | collective-permute-start | bytes 1572872 | tf_op jit(solution)/shard_map/ppermute | solution.py:1091
  669.6 21.9 %collective-permute-start.6 = (bf16[256,1024]{1,0:T(8,128)(2,1)}, bf16[256,1024]{1,0:T(8,128)(2,1)S(1)}, u32[]{:S(2)}, u32[]{:S(2)}) collective-permute-start(bf16[256,1024]{1,0:T(8,128)(2,1)} %constant_dynamic-slice_fusion.1), channel_id=1, source_target_pairs={{0,4},{4,0},{8,12},{12,8},{16,20},{20,16},{24,28},{28,24},{1,5},{5... | collective-permute-start | bytes 1572872 | tf_op jit(solution)/shard_map/ppermute | solution.py:1091
  710.4 49.7 %collective-permute-start.7 = (bf16[512,2048]{1,0:T(8,128)(2,1)}, bf16[512,2048]{1,0:T(8,128)(2,1)}, u32[]{:S(2)}, u32[]{:S(2)}) collective-permute-start(bf16[512,2048]{1,0:T(8,128)(2,1)} %pad_maximum_fusion.4), channel_id=1, source_target_pairs={{0,1},{1,0},{2,3},{3,2},{4,5},{5,4},{6,7},{7,6},{8,9},{9,8},{10,11... | collective-permute-start | bytes 6291464 | tf_op jit(solution)/shard_map/ppermute | solution.py:1088
  (52 other events, 248.3 us)
Sparse Core Ops, SparseCore 0:
  10.2 102.1 all-gather.2
  114.5 163.0 all-gather.4
  362.5 78.8 reduce-scatter.3
  443.7 77.2 reduce-scatter.5
  523.7 83.7 reduce-scatter.7

commit v4 on v3

--- a/solution.py
+++ b/solution.py
@@ -68,11 +68,14 @@
 def attend_forward(group, rank_ref, qkv_ref, cos_ref, sin_ref, seg_row_ref, seg_col_ref, out_ref, rot_ref, lse_ref, peak_ref):
     length = qkv_ref.shape[0]
     scale = 1.0 / math.sqrt(HEAD)
-    for part in range(group + 1):
-        columns = slice(part * HEAD, (part + 1) * HEAD)
-        rot_ref[:, columns] = turn(qkv_ref[:, columns], cos_ref[...], sin_ref[...]).astype(BF16)
     value_columns = slice((group + 1) * HEAD, (group + 2) * HEAD)
-    rot_ref[:, value_columns] = qkv_ref[:, value_columns].astype(BF16)
+    for start in range(0, length, TILE):
+        rows, source = slice(start, start + TILE), slot_rows(rank_ref, start)
+        for part in range(group + 1):
+            columns = slice(part * HEAD, (part + 1) * HEAD)
+            turned = turn(qkv_ref[source, columns], cos_ref[rows, :], sin_ref[rows, :])
+            rot_ref[rows, columns] = turned.astype(BF16)
+        rot_ref[rows, value_columns] = qkv_ref[source, value_columns].astype(BF16)
     key_columns = slice(group * HEAD, (group + 1) * HEAD)
     peak_ref[...] = jnp.full(peak_ref.shape, MASKED, F32)
     peaks = [None] * group
@@ -182,6 +185,30 @@
     )(rank, rotated, grads, lse, cosine, sine, segments.reshape(1, 1, length), segments.reshape(length, 1))
 
 
+def gate_rows(both_ref, grad_ref, hidden_ref, grad_both_ref):
+    columns = grad_ref.shape[1]
+    gate, up, grad = both_ref[:, :columns], both_ref[:, columns:], grad_ref[...]
+    sigmoid = 1.0 / (1.0 + jnp.exp(-gate))
+    silu = gate * sigmoid
+    hidden_ref[...] = (silu * up).astype(BF16)
+    grad_both_ref[:, :columns] = (grad * up * (sigmoid * (1.0 + gate * (1.0 - sigmoid)))).astype(BF16)
+    grad_both_ref[:, columns:] = (grad * silu).astype(BF16)
+
+
+def call_gate_rows(both, grad):
+    rows, columns = grad.shape
+    tile = lambda width: pl.BlockSpec((TILE, width), lambda i: (i, 0))
+    return pl.pallas_call(
+        gate_rows,
+        grid=(rows // TILE,),
+        in_specs=[tile(2 * columns), tile(columns)],
+        out_specs=[tile(columns), tile(2 * columns)],
+        out_shape=[jax.ShapeDtypeStruct((rows, columns), BF16), jax.ShapeDtypeStruct((rows, 2 * columns), BF16)],
+        cost_estimate=lasting(10),
+        name="gate_rows",
+    )(both, grad)
+
+
 def lamb_direction(master, first, second, grad):
     first_moment = DECAY * first + (1.0 - DECAY) * grad
     second_moment = DECAY * second + (1.0 - DECAY) * grad * grad
@@ -370,6 +397,29 @@
     return {"mp": rank ^ 1}, {"mp": rank ^ 2}, {"dp": index ^ 1}
 
 
+def pick_rows(side_ref, rows_ref, _, out_ref):
+    out_ref[...] = rows_ref[...]
+
+
+def call_pick_rows(side, values, ready):
+    rows, columns = values.shape[0] // 2, values.shape[1]
+    return pl.pallas_call(
+        pick_rows,
+        grid_spec=pltpu.PrefetchScalarGridSpec(
+            num_scalar_prefetch=1,
+            grid=(1,),
+            in_specs=[
+                pl.BlockSpec((rows, columns), lambda i, side: (1 - side[0], 0)),
+                pl.BlockSpec(memory_space=pl.ANY),
+            ],
+            out_specs=pl.BlockSpec((rows, columns), lambda i, side: (0, 0)),
+        ),
+        out_shape=jax.ShapeDtypeStruct((rows, columns), values.dtype),
+        cost_estimate=lasting(2),
+        name="pick_rows",
+    )(side, values, ready)
+
+
 class Everyone:
     def __init__(self, line, near_ref, line_ref, near_send, near_recv, line_send, line_recv):
         self.line, self.near_ref, self.line_ref = line, near_ref, line_ref
@@ -451,7 +501,22 @@
         return value
 
 
-def spread_forward(part_ref, tokens_ref, gain_ref, rows_ref, middle_ref, near_ref, out_ref, far_ref, send_sems, recv_sems):
+def spread_forward(part_ref, tokens_ref, gain_ref, grad_ref, down_ref, rows_ref, middle_ref, hidden_ref, near_ref, out_ref, far_ref, grad_in_ref, down_in_ref, hidden_out_ref, send_sems, recv_sems, fetch_sems, store_sems):
+    fetches = [
+        pltpu.make_async_copy(source, target, fetch_sems.at[k])
+        for k, (source, target) in enumerate(((grad_ref, grad_in_ref), (down_ref, down_in_ref)))
+    ]
+    for fetch in fetches:
+        fetch.start()
+    band = hidden_out_ref.shape[0] // CHUNKS
+    stores = []
+
+    def multiply(i):
+        rows = pl.ds(i * band, band)
+        hidden_out_ref[rows, :] = dot_nt(grad_in_ref[rows, :], down_in_ref[...])
+        stores.append(pltpu.make_async_copy(hidden_out_ref.at[rows], hidden_ref.at[rows], store_sems.at[i]))
+        stores[-1].start()
+
     core, far, pair = partners_of()
     quarter, _ = tokens_ref.shape
     size = quarter // CHUNKS
@@ -507,36 +572,51 @@
             moves[5, j].wait_recv()
             moves[9, j] = copy(9, j, rows_ref.at[at(6, j)], rows_ref.at[at(7, j)], core)
             moves[9, j].start()
+        if i == 0:
+            for fetch in fetches:
+                fetch.wait()
+        if i < CHUNKS:
+            multiply(i)
     for i in range(CHUNKS):
         for kind in (6, 7, 8, 9):
             moves[kind, i].wait_recv()
     for made in log:
         made.wait_send()
-
-
-def call_spread_forward(part, tokens_own, gain):
+    for store in stores:
+        store.wait()
+
+
+def call_spread_forward(part, tokens_own, gain, grad_rows, down):
     quarter, width = tokens_own.shape
+    hidden = (grad_rows.shape[0], down.shape[0])
+    hbm = pl.BlockSpec(memory_space=pl.ANY)
     return pl.pallas_call(
         spread_forward,
-        in_specs=[WHOLE] * 3,
-        out_specs=[WHOLE] * 2,
+        in_specs=[*[WHOLE] * 3, hbm, hbm],
+        out_specs=[WHOLE, WHOLE, hbm],
         out_shape=[
             jax.ShapeDtypeStruct((8 * quarter, width), BF16),
             jax.ShapeDtypeStruct((quarter, width), F32),
+            jax.ShapeDtypeStruct(hidden, F32),
         ],
         scratch_shapes=[
             pltpu.VMEM((2 * quarter, width), BF16),
             pltpu.VMEM((quarter, width), BF16),
             pltpu.VMEM((quarter, width), BF16),
+            pltpu.VMEM(grad_rows.shape, BF16),
+            pltpu.VMEM(down.shape, BF16),
+            pltpu.VMEM(hidden, F32),
             pltpu.SemaphoreType.DMA((10, CHUNKS)),
             pltpu.SemaphoreType.DMA((10, CHUNKS)),
+            pltpu.SemaphoreType.DMA((2,)),
+            pltpu.SemaphoreType.DMA((CHUNKS,)),
         ],
         compiler_params=pltpu.CompilerParams(
-            collective_id=1, has_side_effects=True, vmem_limit_bytes=50 * 2**20
+            collective_id=1, has_side_effects=True, vmem_limit_bytes=54 * 2**20
         ),
         cost_estimate=lasting(64),
         name="spread_forward",
-    )(part, tokens_own, gain)
+    )(part, tokens_own, gain, grad_rows, down)
 
 
 def pull_chunk(values, scale_gain, grad):
@@ -546,7 +626,23 @@
     return scale * turned - (scale * scale * scale) * values * inner, grad * values * scale
 
 
-def spread_backward(part_ref, middle_ref, grad_ref, gain_ref, rows_ref, total_ref, gain_out_ref, near_ref, side_out_ref, side_in_ref, far_out_ref, far_in_ref, send_sems, recv_sems):
+def spread_backward(part_ref, middle_ref, grad_ref, gain_ref, left_ref, both_ref, _, rows_ref, total_ref, gain_out_ref, up_ref, near_ref, side_out_ref, side_in_ref, far_out_ref, far_in_ref, left_in_ref, right_in_ref, up_out_ref, send_sems, recv_sems, fetch_sems, store_sems):
+    units = right_in_ref.shape[1]
+    fetches = [
+        pltpu.make_async_copy(left_ref, left_in_ref, fetch_sems.at[0]),
+        pltpu.make_async_copy(both_ref.at[:, pl.ds(units, units)], right_in_ref, fetch_sems.at[1]),
+    ]
+    for fetch in fetches:
+        fetch.start()
+    band = up_out_ref.shape[0] // CHUNKS
+    stores = []
+
+    def multiply(i):
+        rows = pl.ds(i * band, band)
+        up_out_ref[rows, :] = dot_tn(left_in_ref[:, rows], right_in_ref[...]).astype(BF16)
+        stores.append(pltpu.make_async_copy(up_out_ref.at[rows], up_ref.at[rows], store_sems.at[i]))
+        stores[-1].start()
+
     core, far, pair = partners_of()
     quarter, width = middle_ref.shape
     size = quarter // CHUNKS
@@ -602,24 +698,34 @@
             moves[7, j].wait_recv()
             moves[9, j] = copy(9, j, rows_ref.at[at(2, j)], rows_ref.at[at(3, j)], core)
             moves[9, j].start()
+        if i == 0:
+            for fetch in fetches:
+                fetch.wait()
+        if i < CHUNKS:
+            multiply(i)
     gain_out_ref[...] = jnp.broadcast_to(gain_sum, gain_out_ref.shape)
     for i in range(CHUNKS):
         for kind in (8, 9):
             moves[kind, i].wait_recv()
     for made in log:
         made.wait_send()
-
-
-def call_spread_backward(part, middle, grad_own, gain):
+    for store in stores:
+        store.wait()
+
+
+def call_spread_backward(part, middle, grad_own, gain, left, both, ready):
     quarter, width = middle.shape
+    units = both.shape[1] // 2
+    hbm = pl.BlockSpec(memory_space=pl.ANY)
     return pl.pallas_call(
         spread_backward,
-        in_specs=[WHOLE] * 4,
-        out_specs=[WHOLE] * 3,
+        in_specs=[*[WHOLE] * 4, hbm, hbm, hbm],
+        out_specs=[*[WHOLE] * 3, hbm],
         out_shape=[
             jax.ShapeDtypeStruct((4 * quarter, width), BF16),
             jax.ShapeDtypeStruct((quarter, width), F32),
             jax.ShapeDtypeStruct((8, width), F32),
+            jax.ShapeDtypeStruct((width, units), BF16),
         ],
         scratch_shapes=[
             pltpu.VMEM((4 * quarter, width), BF16),
@@ -627,21 +733,26 @@
             pltpu.VMEM((2 * quarter, width), BF16),
             pltpu.VMEM((quarter, width), BF16),
             pltpu.VMEM((quarter, width), BF16),
+            pltpu.VMEM(left.shape, BF16),
+            pltpu.VMEM((left.shape[0], units), BF16),
+            pltpu.VMEM((width, units), BF16),
             pltpu.SemaphoreType.DMA((10, CHUNKS)),
             pltpu.SemaphoreType.DMA((10, CHUNKS)),
+            pltpu.SemaphoreType.DMA((2,)),
+            pltpu.SemaphoreType.DMA((CHUNKS,)),
         ],
         compiler_params=pltpu.CompilerParams(
             collective_id=2, has_side_effects=True, vmem_limit_bytes=56 * 2**20
         ),
         cost_estimate=lasting(68),
         name="spread_backward",
-    )(part, middle, grad_own, gain)
+    )(part, middle, grad_own, gain, left, both, ready)
 
 
 def finish(line, part_ref, tokens_ref, total_ref, gain_ref, *refs):
-    gain_two_ref, grads_refs, refs = refs[0], refs[1:3], refs[3:]
-    rows_ref, gain_out_ref, *owned_refs = refs[:4]
-    near_ref, far_out_ref, far_in_ref = refs[4:7]
+    gain_two_ref, grads_refs, refs = refs[0], refs[1:3], refs[4:]
+    input_ref, gain_out_ref, *owned_refs = refs[:4]
+    rows_ref, near_ref, far_out_ref, far_in_ref, refs = *refs[4:8], refs[1:]
     side_in_refs, up_out_refs, up_in_refs, down_out_refs, down_in_refs = (refs[k : k + 2] for k in range(7, 17, 2))
     send_sems, recv_sems, side_send, side_recv, line_send, line_recv, *exchange = refs[17:]
     core, far, pair = partners_of()
@@ -745,6 +856,10 @@
                         down_out_refs[w][step - 1] = (value + down_in_refs[w][step].astype(F32)).astype(BF16)
 
                 line_copy(w, False, step).start()
+
+    def settle(slot, i):
+        start = pl.multiple_of((lax.axis_index("mp") ^ slot) * quarter + i * size, size)
+        input_ref[pl.ds(start, size), :] = rows_ref[at(slot, i), :].astype(F32)
 
     gain_sum = jnp.zeros((1, width), F32)
     steps = list(range(last, 0, -1))
@@ -760,6 +875,7 @@
             back, gain_part = pull_chunk(tokens_ref[at(0, i), :].astype(F32), gain_ref[0:1, :], grad)
             gain_sum = gain_sum + jnp.sum(gain_part, 0, keepdims=True)
             rows_ref[at(0, i), :] = (total_ref[at(0, i), :] + back).astype(BF16)
+            settle(0, i)
             own = rows_ref.at[at(0, i)]
             for kind, slot, device in ((3, 2, far), (4, 1, core)):
                 moves[kind, i] = copy(kind, i, own, rows_ref.at[at(slot, i)], device)
@@ -769,6 +885,7 @@
         j = i - 1
         if 0 <= j < CHUNKS:
             moves[3, j].wait_recv()
+            settle(2, j)
             moves[5, j] = copy(5, j, rows_ref.at[at(2, j)], rows_ref.at[at(3, j)], core)
             moves[5, j].start()
     while steps:
@@ -796,8 +913,9 @@
 
     gain_out_ref[...] = everyone.result(everyone.add)
     for i in range(CHUNKS):
-        for kind in (4, 5):
+        for kind, slot in ((4, 1), (5, 3)):
             moves[kind, i].wait_recv()
+            settle(slot, i)
     for made in log:
         made.wait_send()
     for w in range(2):
@@ -814,21 +932,22 @@
                 line_copy(w, False, step).wait_send()
 
 
-def call_finish(dp_size, part, tokens_own, total, gain, gain_two, *grads):
+def call_finish(dp_size, part, tokens_own, total, gain, gain_two, ready, *grads):
     quarter, width = tokens_own.shape
     line = dp_size // 2
     owned = [(grad.shape[0] // dp_size, grad.shape[1]) for grad in grads]
     stacks = lambda count: [pltpu.VMEM((count, *shape), BF16) for shape in owned]
     return pl.pallas_call(
         functools.partial(finish, line),
-        in_specs=[WHOLE] * 7,
+        in_specs=[*[WHOLE] * 7, pl.BlockSpec(memory_space=pl.ANY)],
         out_specs=[WHOLE] * 4,
         out_shape=[
-            jax.ShapeDtypeStruct((4 * quarter, width), BF16),
+            jax.ShapeDtypeStruct((4 * quarter, width), F32),
             jax.ShapeDtypeStruct((8, width // 4), F32),
             *[jax.ShapeDtypeStruct(shape, F32) for shape in owned],
         ],
         scratch_shapes=[
+            pltpu.VMEM((4 * quarter, width), BF16),
             pltpu.VMEM((2 * quarter, width), BF16),
             pltpu.VMEM((quarter, width), BF16),
             pltpu.VMEM((quarter, width), BF16),
@@ -850,7 +969,7 @@
         ),
         cost_estimate=lasting(85),
         name="finish",
-    )(part, tokens_own, total, gain, gain_two, *grads)
+    )(part, tokens_own, total, gain, gain_two, *grads, ready)
 
 
 def gather_weights(line, own_ref, out_ref, gains_ref, grad_ref, full_ref, out_full_ref, gains_full_ref, rows_ref, local_sems, side_send, side_recv, line_send, line_recv, rows_send, rows_recv, staged_ref):
@@ -1112,10 +1231,6 @@
         cuts = [jnp.where(high, cuts[k ^ 2], cuts[k]) for k in range(self.mp)]
         return jnp.concatenate(cuts, 0)
 
-    def own_quarter(self, values):
-        rows = values.shape[0] // self.mp
-        return lax.dynamic_slice_in_dim(values, self.rank * rows, rows, 0)
-
     def gather_core(self, quarter, far):
         rows = quarter.shape[0]
         near = self.swap_mp(jnp.concatenate([quarter, far], 0), 1)
@@ -1135,7 +1250,7 @@
             ],
             0,
         ).astype(BF16)
-        return add((0, 2), 0), add((4, 6), 2)
+        return add((0, 2), 0), add((4,), 2), add((6,), 3)
 
 
 def after(value, *others):
@@ -1191,7 +1306,8 @@
         cut = lax.dynamic_index_in_dim(by_side, which, 3, keepdims=False).astype(BF16)
         return jnp.concatenate([cut[0].reshape(shard, -1), cut[1].reshape(shard, -1)], 1)
 
-    inputs = tokens.astype(F32)
+    token_slots = links.to_slots(tokens)
+    inputs = token_slots.astype(F32)
     scale_one = inverse_rms(inputs)
     down_full = links.gather_line(w_down.astype(BF16))
     own_units = side_units(side)
@@ -1205,7 +1321,7 @@
     qkv_full, out_full, gains_shards, grad_rows = call_gather_weights(
         dp_size,
         cotangent,
-        after(interleave(w_query, w_key, w_value).astype(BF16), rows_pair, scale_one),
+        after(interleave(w_query, w_key, w_value).astype(BF16), rows_pair, scale_one, token_slots),
         w_out.astype(BF16),
         gains_rows,
     )
@@ -1218,35 +1334,34 @@
     qkv = jnp.dot(normed_one, qkv_full, preferred_element_type=F32)
     rank_ref = links.rank.astype(jnp.int32).reshape(1)
     mixed_slots, rotated, lse, peaks = attention_forward(rank_ref, qkv, cosine, sine, segment_ids, group, kvs)
-    tokens_own = links.own_quarter(tokens)
-    rows_two, middle = call_spread_forward(
-        jnp.dot(mixed_slots, out_full, preferred_element_type=F32).astype(BF16), tokens_own, gains_full[1:2]
+    tokens_own = token_slots[:quarter]
+    rows_two, middle, grad_hidden = call_spread_forward(
+        jnp.dot(mixed_slots, out_full, preferred_element_type=F32).astype(BF16),
+        tokens_own,
+        gains_full[1:2],
+        grad_rows,
+        down_full,
     )
 
     columns = line * block
-    grad_hidden = dot_nt(grad_rows, down_full)
-    grad_hidden, gate_up_full = lax.optimization_barrier((grad_hidden, gate_up_full))
     both = jnp.dot(rows_two, gate_up_full, preferred_element_type=F32)
-    gate, up = both[:, :columns], both[:, columns:]
-    sigmoid = jax.nn.sigmoid(gate)
-    hidden = (gate * sigmoid * up).astype(BF16)
-    grad_gate = (grad_hidden * up * sigmoid * (1.0 + gate * (1.0 - sigmoid))).astype(BF16)
-    grad_up = (grad_hidden * gate * sigmoid).astype(BF16)
-    output_part = jnp.dot(hidden, down_full, preferred_element_type=F32).astype(BF16)
+    hidden, grad_both = call_gate_rows(both, grad_hidden)
+    grad_down_part = dot_tn(hidden, grad_rows).astype(BF16)
+    output_part = jnp.dot(after(hidden, grad_down_part), down_full, preferred_element_type=F32).astype(BF16)
     output_part, output_near = links.swap_core(output_part)
-    grad_down_part = dot_tn(after(hidden, output_part), grad_rows).astype(BF16)
-    grad_gate_part = dot_tn(after(rows_two, grad_down_part), grad_gate).astype(BF16)
-    grad_both = after(jnp.concatenate([grad_gate, grad_up], 1), grad_gate_part)
-    back = dot_nt(grad_both, gate_up_full).astype(BF16)
-    grad_middle_slots, grad_middle, gain_two = call_spread_backward(
-        after(back, output_near), middle, links.own_quarter(cotangent), gains_full[1:2]
+    output_mine, output_other, output_theirs = links.sum_core(output_part, after(output_near, grad_down_part))
+    output_second = links.swap_side(output_theirs)
+    grad_gate_part = dot_tn(rows_two, grad_both[:, :columns]).astype(BF16)
+    output_first = links.swap_side(output_other)
+    back = dot_nt(after(grad_both, grad_gate_part), gate_up_full).astype(BF16)
+    grad_middle_slots, grad_middle, gain_two, grad_up_part = call_spread_backward(
+        back, middle, grad_rows[:quarter], gains_full[1:2], rows_two, grad_both, output_second
     )
-    output_mine, output_theirs = links.sum_core(output_part, after(output_near, grad_middle_slots))
+    output_second = output_mine[quarter:].astype(F32) + after(output_second, back).astype(F32)
+    output_far = links.swap_mp(after(output_second.astype(BF16), grad_middle_slots), 2)
     grad_down_low = links.sum_line(grad_down_part)
-    grad_up_part = dot_tn(after(rows_two, output_theirs, grad_down_low), grad_up).astype(BF16)
     gate_sum = after(links.sum_line(grad_gate_part), grad_down_low)
     up_sum = after(links.sum_line(grad_up_part), gate_sum)
-    grad_middle_slots = after(grad_middle_slots, grad_up_part)
     grad_mixed = dot_nt(grad_middle_slots, out_full).astype(BF16)
 
     grad_down = grad_down_low.astype(F32)
@@ -1269,30 +1384,30 @@
     early = jnp.where(lower & (lanes == 12), down_sum, early)
 
     grad_qkv = attention_backward(rank_ref, rotated, grad_mixed, lse, cosine, sine, segment_ids, group, kvs)
-    grad_qkv_part = dot_tn(links.to_slots(normed_one), grad_qkv).astype(BF16)
+    grad_qkv_part = dot_tn(normed_one, grad_qkv).astype(BF16)
     grad_out_part = dot_tn(mixed_slots, grad_middle_slots).astype(BF16)
     grad_normed_one = dot_nt(grad_qkv, qkv_full).astype(BF16)
-    output_theirs = links.swap_side(output_theirs)
-    output_pair = output_mine.astype(F32) + after(output_theirs, grad_qkv_part, grad_normed_one).astype(F32)
-    output_far = links.swap_mp(output_pair[quarter:].astype(BF16), 2).astype(F32)
-    input_slots, gain_terms, grad_qkv_own, grad_out = call_finish(
+    input_grad, gain_terms, grad_qkv_own, grad_out = call_finish(
         dp_size,
-        after(grad_normed_one, gate_sum, output_pair),
+        after(grad_normed_one, gate_sum),
         tokens_own,
         grad_middle,
         gains_full[0:1],
         gain_two,
+        output_first,
         grad_qkv_part,
         grad_out_part,
     )
-    input_grad = links.from_slots(input_slots).astype(F32)
-    output_low = (middle + output_pair[:quarter] + after(output_far, input_slots)).astype(BF16)
+    output_far = after(output_far, input_grad).astype(F32)
+    output_low = (middle + output_mine[:quarter].astype(F32) + output_first.astype(F32) + output_far).astype(BF16)
     output_far = links.swap_mp(output_low, 2)
 
-    other_side = lambda value: lax.dynamic_slice_in_dim(value, (1 - side) * shard, shard, 0)
     summed = [gate_sum, up_sum]
-    theirs = [links.swap_side(other_side(value)) for value in summed]
-    grad_qkv_own = after(grad_qkv_own, theirs[0], other_side(up_sum))
+    side_ref = side.astype(jnp.int32).reshape(1)
+    theirs = [
+        links.swap_side(call_pick_rows(side_ref, value, ready))
+        for value, ready in ((gate_sum, grad_qkv), (up_sum, gain_terms))
+    ]
     gain_terms = gain_terms.reshape(2, width)
     gain_width = norm_gains.shape[1]
     grad_gains = lax.dynamic_slice_in_dim(gain_terms, links.index * gain_width, gain_width, 1)
@@ -1302,6 +1417,7 @@
     grad_query, grad_key, grad_value, *rest = call_small_step(
         group, kvs, jnp.full((1, HEAD), owner), grad_qkv_own, grad_out, grad_gains, small, small_moments
     )
+    theirs = [after(value, grad_query, down_direction, early, output_low) for value in theirs]
     small_seconds, small_directions, small_sums = rest[:SMALL], rest[SMALL : 2 * SMALL], rest[2 * SMALL]
     if block % HEAD == 0:
         grad_gate_up, gate_up_second, gate_up_direction, gate_up_sums = call_gate_up_step(

time: 778 us -> 742 us (0.954)
  Pallas kernels: 437 us -> 482 us
  other arithmetic: 74.3 us -> 43.5 us
  waiting for transfers between devices: 56.5 us -> 26.8 us
  matrix products: 145 us -> 117 us
    pallas_call x3 -> x6, Pallas kernels: 226 us -> 273 us  [the longest x1 125 us: call_finish(): pl.pallas_call(functools.partial(finish, line), in_specs=[*[WHOLE] * 7, p...]
    ppermute x4 -> x5, waiting for transfers between devices: 56.4 us -> 24.8 us  [swap_side(): return lax.ppermute(value, 'dp', [(i, i ^ 1) for i in range(self.dp)])]
    dot_general x4 -> x3, matrix products: 46.8 us -> 30.9 us  [dot_nt(): lax.dot_general(left, right, (((1,), (1,)), ((), ())), preferred_element_...]
    convert_element_type x5 -> x3, other arithmetic: 21.8 us -> 7.59 us  [the longest x1 3.67 us: body(): (middle + output_mine[:quarter].astype(F32) + output_first.astype(F32) +...]
    dot_general x5 -> x4, matrix products: 51.6 us -> 38.7 us  [dot_tn(): lax.dot_general(left, right, (((0,), (0,)), ((), ())), preferred_element_...]
    unnamed x137 -> x146, local copies, waits for them, and re-layouts: 21 us -> 31.2 us
    concatenate x2 -> x0, other arithmetic: 9.96 us -> none  [the longest x1 8.39 us: body(): grad_both = after(jnp.concatenate([grad_gate, grad_up], 1), grad_gate_part)]
  transfers between devices with their start and end apart: 13 -> 14, of which waited for: 4 -> 3; matrix products, arithmetic and copies ran while one was open for 22% -> 17% of each run, Pallas kernels for 57% -> 63%
where the time goes in v4:
time: 742 us; the launch traced here: 737 us
  Pallas kernels  482 us (65%)
  matrix products  117 us (16%)
  other arithmetic  43.5 us (6%)
  local copies, waits for them, and re-layouts  40.4 us (5%)
  waiting for transfers between devices  26.8 us (4%)
  between operations  15.8 us (2%)
  starting transfers between devices  11.2 us (2%)
    pallas_call x1, Pallas kernels, call_gather_weights(): pl.pallas_call(functools.partial(gather_weights, line), in_specs=[hbm] *...  143 us
    pallas_call x1, Pallas kernels, call_finish(): pl.pallas_call(functools.partial(finish, line), in_specs=[*[WHOLE] * 7, p...  125 us
    pallas_call x1, Pallas kernels, call_spread_backward(): pl.pallas_call(spread_backward, in_specs=[*[WHOLE] * 4, hbm, hbm, hbm], o...  67 us
    pallas_call x1, Pallas kernels, call_spread_forward(): pl.pallas_call(spread_forward, in_specs=[*[WHOLE] * 3, hbm, hbm], out_spe...  62.8 us
    dot_general x4, matrix products, dot_tn(): lax.dot_general(left, right, (((0,), (0,)), ((), ())), preferred_element_...  38.7 us
    unnamed x146, local copies, waits for them, and re-layouts  31.2 us
    dot_general x3, matrix products, dot_nt(): lax.dot_general(left, right, (((1,), (1,)), ((), ())), preferred_element_...  30.9 us
    ppermute x5, waiting for transfers between devices, swap_side(): return lax.ppermute(value, 'dp', [(i, i ^ 1) for i in range(self.dp)])  24.8 us
  transfers between devices with their start and end apart: 14, of which 3 were waited for; matrix products, arithmetic and copies ran while one was open for 17% of the time, Pallas kernels for 63%

profile of v4, /device:TPU:0, one launch (start us, length us, event | category | flops | bytes accessed | tf_op | source)
XLA Modules:
  0.0 736.7 jit_solution(13761604526396762611)
XLA Ops:
  18.0 23.2 %collective-permute-done = bf16[256,2048]{0,1:T(8,128)(2,1)} collective-permute-done((bf16[256,2048]{0,1:T(8,128)(2,1)}, bf16[256,2048]{0,1:T(8,128)(2,1)}, u32[]{:S(2)}, u32[]{:S(2)}) %collective-permute-start) | collective-permute-done | bytes 1048608 | tf_op jit(solution)/shard_map/ppermute | solution.py:1210
  52.4 143.0 %gather_weights.1 = (bf16[2048,1024]{1,0:T(8,128)(2,1)S(1)}, bf16[512,2048]{1,0:T(8,128)(2,1)S(1)}, f32[64,256]{1,0:T(8,128)S(1)}, bf16[2048,2048]{1,0:T(8,128)(2,1)S(1)}) custom-call(bf16[256,1024]{1,0:T(8,128)(2,1)S(1)} %slice_dynamic-update-slice_fusion.2.own_ref, bf16[64,2048]{1,0:T(8,128)(2,1)S(1)} %get-tuple-element.194.out_ref, ...), custom_call_target="tpu_custom_call" | custom-call | bytes 360000000 | tf_op jit(solution)/shard_map/gather_weights/pallas_call | solution.py:1142
  201.9 6.4 fusion.12.qkv_ref
  208.3 12.0 %attention_forward.1 = (bf16[1024,512]{1,0:T(8,128)(2,1)S(1)}, bf16[1024,1024]{1,0:T(8,128)(2,1)S(1)}, f32[1024,512]{1,0:T(8,128)}, f32[2,8,128]{2,1,0:T(8,128)S(1)}) custom-call(s32[1]{0:T(128)} %bitcast.rank_ref, f32[1024,1024]{1,0:T(8,128)} %fusion.12.qkv_ref, f32[1024,128]{1,0:T(8,128)S(1)} %get-tuple-element.213.cos_ref, ...), custom_call_target="tpu_custom_call" | custom-call | bytes 36000000 | tf_op jit(solution)/shard_map/attention_forward/pallas_call | solution.py:149
  222.7 4.4 convolution_convert_fusion.3.part_ref
  227.1 62.8 %spread_forward.1 = (bf16[2048,2048]{1,0:T(8,128)(2,1)}, f32[256,2048]{1,0:T(8,128)}, f32[2048,1024]{1,0:T(8,128)}) custom-call(bf16[1024,2048]{1,0:T(8,128)(2,1)} %convolution_convert_fusion.3.part_ref, bf16[256,2048]{1,0:T(8,128)(2,1)} %copy-done.45, f32[1,2048]{1,0:T(1,128)} %bitcast.69, bf16[2048,2048]{1,0:T(8,128)(2,1)} %copy-done, ...), custom_call_target="tpu_custom_call" | custom-call | bytes 192000000 | tf_op jit(solution)/shard_map/spread_forward/pallas_call | solution.py:593
  289.9 24.5 %fusion.23.both_ref = f32[2048,2048]{1,0:T(8,128)} fusion(bf16[2048,2048]{1,0:T(8,128)(2,1)} %get-tuple-element.106.left_ref, bf16[2048,2048]{0,1:T(8,128)(2,1)} %all-gather.5.cloned.1.call-done), kind=kOutput, calls=%fused_computation.94 | convolution fusion | flops 17179869184 | bytes 33554432 | tf_op jit(solution)/shard_map/dot_general | solution.py:1347
  314.4 14.6 %gate_rows.1 = (bf16[2048,1024]{1,0:T(8,128)(2,1)}, bf16[2048,2048]{1,0:T(8,128)(2,1)}) custom-call(f32[2048,2048]{1,0:T(8,128)} %fusion.23.both_ref, f32[2048,1024]{1,0:T(8,128)} %get-tuple-element.108.grad_ref), custom_call_target="tpu_custom_call" | custom-call | bytes 30000000 | tf_op jit(solution)/shard_map/gate_rows/pallas_call | solution.py:201
  329.0 14.0 %fusion.5 = bf16[2048,1024]{1,0:T(8,128)(2,1)} fusion(bf16[2048,2048]{1,0:T(8,128)(2,1)} %get-tuple-element.106.left_ref, bf16[2048,2048]{1,0:T(8,128)(2,1)} %get-tuple-element.113.both_ref), kind=kOutput, calls=%fused_computation.13 | convolution fusion | flops 8592031744 | bytes 16777216 | tf_op jit(solution)/shard_map/dot_general | solution.py:61
  343.1 14.3 %convolution_convert_fusion.2 = bf16[1024,2048]{1,0:T(8,128)(2,1)} fusion(bf16[2048,1024]{1,0:T(8,128)(2,1)} %get-tuple-element.110, bf16[2048,2048]{1,0:T(8,128)(2,1)} %copy-done), kind=kOutput, calls=%fused_computation.14 | convolution fusion | flops 8592031744 | bytes 16777216 | tf_op jit(solution)/shard_map/dot_general | solution.py:61
  357.4 11.9 %convolution_convert_fusion.1 = bf16[2048,2048]{1,0:T(8,128)(2,1)S(1)} fusion(bf16[2048,1024]{1,0:T(8,128)(2,1)} %get-tuple-element.110, bf16[1024,2048]{1,0:T(8,128)(2,1)} %all-gather.3.cloned.1.call-done.down_ref), kind=kOutput, calls=%fused_computation.6 | convolution fusion | flops 8594128896 | bytes 16777216 | tf_op jit(solution)/shard_map/dot_general | solution.py:1350
  371.0 4.9 slice.154.grad_ref
  380.3 22.2 %convolution_convert_fusion.part_ref = bf16[2048,2048]{1,0:T(8,128)(2,1)} fusion(bf16[2048,2048]{1,0:T(8,128)(2,1)S(1)} %bitcast.62, bf16[2048,2048]{0,1:T(8,128)(2,1)} %all-gather.5.cloned.1.call-done), kind=kOutput, calls=%fused_computation.5 | convolution fusion | flops 17184063488 | bytes 25165824 | tf_op jit(solution)/shard_map/dot_general | solution.py:53
  405.1 67.0 %spread_backward.1 = (bf16[1024,2048]{1,0:T(8,128)(2,1)}, f32[256,2048]{1,0:T(8,128)}, f32[8,2048]{1,0:T(8,128)}, bf16[2048,1024]{1,0:T(8,128)(2,1)}) custom-call(bf16[2048,2048]{1,0:T(8,128)(2,1)} %convolution_convert_fusion.part_ref, f32[256,2048]{1,0:T(8,128)} %get-tuple-element.105.middle_ref, bf16[256,2048]{1,0:T(8,128)(2,1)} %slice.154.grad_ref, ...), custom_call_target="tpu_custom_call" | custom-call | bytes 204000000 | tf_op jit(solution)/shard_map/spread_backward/pallas_call | solution.py:720
  472.9 4.1 multiply_reduce_fusion
  485.6 13.3 %attention_backward.1._ = bf16[1024,1024]{1,0:T(8,128)(2,1)S(1)} custom-call(s32[1]{0:T(128)} %bitcast.rank_ref, bf16[1024,1024]{1,0:T(8,128)(2,1)} %copy-done.18, bf16[1024,512]{1,0:T(8,128)(2,1)S(1)} %convolution_convert_fusion.7.grad_ref, f32[1024,512]{1,0:T(8,128)} %get-tuple-element.118.lse_ref, f32[1024,128]{1,0:T(8,128)S(1)} %copy-done.7, ...), custom_call_target="tpu_custom_call" | custom-call | bytes 39000000 | tf_op jit(solution)/shard_map/attention_backward/pallas_call | solution.py:172
  499.0 6.3 convolution_convert_fusion.5.part_ref
  509.1 6.7 convolution_convert_fusion.4.refs_1_
  516.8 124.6 %finish.1 = (f32[1024,2048]{1,0:T(8,128)}, f32[8,512]{1,0:T(8,128)}, f32[256,1024]{1,0:T(8,128)}, f32[64,2048]{1,0:T(8,128)}) custom-call(bf16[1024,2048]{1,0:T(8,128)(2,1)} %convolution_convert_fusion.5.part_ref, bf16[256,2048]{1,0:T(8,128)(2,1)} %copy-done.45, f32[256,2048]{1,0:T(8,128)} %get-tuple-element.121.total_ref, f32[1,2048]{1,0:T(1,128)} %bitcast.71, ...), custom_call_target="tpu_custom_call" | custom-call | bytes 255000000 | tf_op jit(solution)/shard_map/finish/pallas_call | solution.py:940
  653.2 7.4 %multiply_reduce_fusion.2 = (f32[]{:T(128)}, f32[256,2048]{1,0:T(8,128)}, f32[256,2048]{1,0:T(8,128)}, f32[256,2048]{1,0:T(8,128)}, f32[]{:T(128)}) fusion(f32[256,2048]{1,0:T(8,128)} %master_ref.3, f32[2,256,2048]{2,1,0:T(8,128)} %param.32, bf16[256,2048]{1,0:T(8,128)(2,1)} %reduce-scatter.6.cloned.1.call-done), kind=kLoop, calls=%fused_computation.26 | loop fusion | flops 7864318 | bytes 13631496 | tf_op jit(solution)/shard_map/reduce_sum | solution.py:1369
  670.1 5.2 select_select_fusion.early_ref
  675.3 16.5 %gate_up_step.1 = (f32[2,256,2048]{2,1,0:T(8,128)}, f32[2,256,2048]{2,1,0:T(8,128)}, f32[2,256,2048]{2,1,0:T(8,128)}, f32[8,256]{1,0:T(8,128)}) custom-call(s32[1]{0:T(128)} %bitcast.10.side_ref, f32[2,256,2048]{2,1,0:T(8,128)} %master_ref.2, f32[2,2,256,2048]{3,2,1,0:T(8,128)} %moment_ref.1, ...), custom_call_target="tpu_custom_call" | custom-call | bytes 48000000 | tf_op jit(solution)/shard_map/gate_up_step/pallas_call | solution.py:241
  695.0 10.1 %combine_all.1.packed_ref = f32[16,128]{1,0:T(8,128)} custom-call(f32[16,128]{1,0:T(8,128)} %select_select_fusion.early_ref, f32[8,128]{1,0:T(8,128)} %copy-done.37, f32[8,256]{1,0:T(8,128)} %get-tuple-element.134.gate_up_ref), custom_call_target="tpu_custom_call" | custom-call | bytes 30000000 | tf_op jit(solution)/shard_map/combine_all/pallas_call | solution.py:1187
  708.7 6.7 large_update.2
  (232 shorter events, 94.8 us)
Async XLA Ops:
  7.2 219.9 %all-gather.3.cloned.1.call-start = ((), (), s32[]{:S(2)}) async-start(), calls=%async_computation.3 | async-start | bytes 5242880 | tf_op jit(solution)/shard_map/all_gather | solution.py:1213
  10.0 279.9 %all-gather.5.cloned.1.call-start = ((), (), s32[]{:S(2)}) async-start(), calls=%async_computation.4 | async-start | bytes 10485760 | tf_op jit(solution)/shard_map/all_gather | solution.py:1213
  14.8 26.4 %collective-permute-start = (bf16[256,2048]{0,1:T(8,128)(2,1)}, bf16[256,2048]{0,1:T(8,128)(2,1)}, u32[]{:S(2)}, u32[]{:S(2)}) collective-permute-start(bf16[256,2048]{0,1:T(8,128)(2,1)} %pad_maximum_fusion.4), channel_id=1, source_target_pairs={{0,4},{4,0},{8,12},{12,8},{16,20},{20,16},{24,28},{28,24},{1,5},{5... | collective-permute-start | bytes 3145736 | tf_op jit(solution)/shard_map/ppermute | solution.py:1210
  17.7 26.2 %copy-start.31 = (s32[1,1024]{1,0:T(1,128)S(1)}, s32[1,1024]{1,0:T(1,128)}, u32[]{:S(2)}) copy-start(s32[1,1024]{1,0:T(1,128)} %param.19) | copy-start | bytes 12292
  17.7 26.5 %copy-start.33 = (f32[2,256]{1,0:T(2,128)S(1)}, f32[2,256]{1,0:T(2,128)}, u32[]{:S(2)}) copy-start(f32[2,256]{1,0:T(2,128)} %refs_4_.3) | copy-start | bytes 6148
  43.9 472.0 %reduce-scatter.4.cloned.1.call-start = ((), (), s32[]{:S(2)}) async-start(), calls=%async_computation.5 | async-start | bytes 5242880 | tf_op jit(solution)/shard_map/reduce_scatter | solution.py:1216
  44.2 164.2 %copy-start.10 = (s32[1024,1]{1,0:T(8,128)}, s32[1024,1]{1,0:T(8,128)S(1)}, u32[]{:S(2)}) copy-start(s32[1024,1]{1,0:T(8,128)S(1)} %copy.55.seg_col_ref) | copy-start | bytes 12292
  47.1 161.2 %copy-start.6 = (f32[1024,128]{1,0:T(8,128)}, f32[1024,128]{1,0:T(8,128)S(1)}, u32[]{:S(2)}) copy-start(f32[1024,128]{1,0:T(8,128)S(1)} %get-tuple-element.213.cos_ref) | copy-start | bytes 1572868
  47.2 161.2 %copy-start.8 = (f32[1024,128]{1,0:T(8,128)}, f32[1024,128]{1,0:T(8,128)S(1)}, u32[]{:S(2)}) copy-start(f32[1024,128]{1,0:T(8,128)S(1)} %get-tuple-element.214.sin_ref) | copy-start | bytes 1572868
  48.9 153.1 %copy-start.54 = (bf16[1024,2048]{1,0:T(8,128)(2,1)}, bf16[1024,2048]{1,0:T(8,128)(2,1)S(1)}, u32[]{:S(2)}) copy-start(bf16[1024,2048]{1,0:T(8,128)(2,1)S(1)} %get-tuple-element.171) | copy-start | bytes 12582916
  49.2 152.7 %copy-start.60 = (f32[1024]{0:T(1024)}, f32[1024]{0:T(1024)S(1)}, u32[]{:S(2)}) copy-start(f32[1024]{0:T(1024)S(1)} %add_rsqrt_fusion) | copy-start | bytes 12292
  343.0 172.8 %reduce-scatter.6.cloned.1.call-start = ((), (), s32[]{:S(2)}) async-start(), calls=%async_computation.6 | async-start | bytes 5242880 | tf_op jit(solution)/shard_map/reduce_scatter | solution.py:1216
  357.4 293.1 %reduce-scatter.8.cloned.1.call-start = ((), (), s32[]{:S(2)}) async-start(), calls=%async_computation.7 | async-start | bytes 5242880 | tf_op jit(solution)/shard_map/reduce_scatter | solution.py:1216
  370.5 7.3 collective-permute-start.1
  377.8 24.8 %copy-start.51 = (bf16[1024,2048]{1,0:T(8,128)(2,1)}, bf16[1024,2048]{1,0:T(8,128)(2,1)S(1)}, u32[]{:S(2)}) copy-start(bf16[1024,2048]{1,0:T(8,128)(2,1)S(1)} %collective-permute-done.1) | copy-start | bytes 12582916
  378.6 25.5 %collective-permute-start.3 = (bf16[256,2048]{1,0:T(8,128)(2,1)S(1)}, bf16[256,2048]{1,0:T(8,128)(2,1)S(1)}, u32[]{:S(2)}, u32[]{:S(2)}) collective-permute-start(bf16[256,2048]{1,0:T(8,128)(2,1)S(1)} %get-tuple-element.173), channel_id=1, source_target_pairs={{0,4},{4,0},{8,12},{12,8},{16,20},{20,16},{24,28},{28,24},{1,5},{5... | collective-permute-start | bytes 3145736 | tf_op jit(solution)/shard_map/ppermute | solution.py:1210
  477.6 38.2 %collective-permute-start.2 = (bf16[256,2048]{1,0:T(8,128)(2,1)S(1)}, bf16[256,2048]{1,0:T(8,128)(2,1)S(1)}, u32[]{:S(2)}, u32[]{:S(2)}) collective-permute-start(bf16[256,2048]{1,0:T(8,128)(2,1)S(1)} %get-tuple-element.172), channel_id=1, source_target_pairs={{0,4},{4,0},{8,12},{12,8},{16,20},{20,16},{24,28},{28,24},{1,5},{5... | collective-permute-start | bytes 3145736 | tf_op jit(solution)/shard_map/ppermute | solution.py:1210
  481.9 159.6 %collective-permute-start.4 = (bf16[256,2048]{1,0:T(8,128)(2,1)}, bf16[256,2048]{1,0:T(8,128)(2,1)S(1)}, u32[]{:S(2)}, u32[]{:S(2)}) collective-permute-start(bf16[256,2048]{1,0:T(8,128)(2,1)} %add_convert_fusion.1), channel_id=1, source_target_pairs={{0,2},{1,3},{2,0},{3,1},{4,6},{5,7},{6,4},{7,5},{8,10},{9,11},{10,... | collective-permute-start | bytes 3145736 | tf_op jit(solution)/shard_map/ppermute | solution.py:1207
  516.8 124.7 %copy-start.48 = (f32[256,2048]{1,0:T(8,128)S(1)}, f32[256,2048]{1,0:T(8,128)}, u32[]{:S(2)}) copy-start(f32[256,2048]{1,0:T(8,128)} %get-tuple-element.105.middle_ref) | copy-start | bytes 6291460
  645.1 46.7 %collective-permute-start.5 = (bf16[256,2048]{1,0:T(8,128)(2,1)}, bf16[256,2048]{1,0:T(8,128)(2,1)}, u32[]{:S(2)}, u32[]{:S(2)}) collective-permute-start(bf16[256,2048]{1,0:T(8,128)(2,1)} %add_convert_fusion), channel_id=1, source_target_pairs={{0,2},{1,3},{2,0},{3,1},{4,6},{5,7},{6,4},{7,5},{8,10},{9,11},{10,... | collective-permute-start | bytes 3145736 | tf_op jit(solution)/shard_map/ppermute | solution.py:1207
  649.1 26.2 %collective-permute-start.6 = (bf16[256,1024]{1,0:T(8,128)(2,1)}, bf16[256,1024]{1,0:T(8,128)(2,1)}, u32[]{:S(2)}, u32[]{:S(2)}) collective-permute-start(bf16[256,1024]{1,0:T(8,128)(2,1)} %pick_rows.2), channel_id=1, source_target_pairs={{0,4},{4,0},{8,12},{12,8},{16,20},{20,16},{24,28},{28,24},{1,5},{5... | collective-permute-start | bytes 1572872 | tf_op jit(solution)/shard_map/ppermute | solution.py:1210
  652.4 22.9 %collective-permute-start.7 = (bf16[256,1024]{1,0:T(8,128)(2,1)}, bf16[256,1024]{1,0:T(8,128)(2,1)}, u32[]{:S(2)}, u32[]{:S(2)}) collective-permute-start(bf16[256,1024]{1,0:T(8,128)(2,1)} %pick_rows.3), channel_id=1, source_target_pairs={{0,4},{4,0},{8,12},{12,8},{16,20},{20,16},{24,28},{28,24},{1,5},{5... | collective-permute-start | bytes 1572872 | tf_op jit(solution)/shard_map/ppermute | solution.py:1210
  660.6 31.2 %copy-start.35 = (f32[2,256]{1,0:T(2,128)}, f32[2,256]{1,0:T(2,128)S(1)}, u32[]{:S(2)}) copy-start(f32[2,256]{1,0:T(2,128)S(1)} %constant_dynamic-slice_fusion.grad_gains_ref) | copy-start | bytes 6148
  695.0 24.2 %collective-permute-start.8 = (bf16[512,2048]{1,0:T(8,128)(2,1)}, bf16[512,2048]{1,0:T(8,128)(2,1)}, u32[]{:S(2)}, u32[]{:S(2)}) collective-permute-start(bf16[512,2048]{1,0:T(8,128)(2,1)} %pad_maximum_fusion.3), channel_id=1, source_target_pairs={{0,1},{1,0},{2,3},{3,2},{4,5},{5,4},{6,7},{7,6},{8,9},{9,8},{10,11... | collective-permute-start | bytes 6291464 | tf_op jit(solution)/shard_map/ppermute | solution.py:1207
  (57 other events, 301.1 us)
Sparse Core Ops, SparseCore 0:
  10.2 101.1 all-gather.2
  113.5 164.0 all-gather.4
  343.1 81.3 reduce-scatter.3
  426.8 77.2 reduce-scatter.5
  506.2 113.3 reduce-scatter.7

commit v5 on v4

--- a/solution.py
+++ b/solution.py
@@ -750,7 +750,7 @@
 
 
 def finish(line, part_ref, tokens_ref, total_ref, gain_ref, *refs):
-    gain_two_ref, grads_refs, refs = refs[0], refs[1:3], refs[4:]
+    gain_two_ref, grads_refs, refs = refs[0], refs[1:3], refs[7:]
     input_ref, gain_out_ref, *owned_refs = refs[:4]
     rows_ref, near_ref, far_out_ref, far_in_ref, refs = *refs[4:8], refs[1:]
     side_in_refs, up_out_refs, up_in_refs, down_out_refs, down_in_refs = (refs[k : k + 2] for k in range(7, 17, 2))
@@ -939,7 +939,7 @@
     stacks = lambda count: [pltpu.VMEM((count, *shape), BF16) for shape in owned]
     return pl.pallas_call(
         functools.partial(finish, line),
-        in_specs=[*[WHOLE] * 7, pl.BlockSpec(memory_space=pl.ANY)],
+        in_specs=[*[WHOLE] * 7, *[pl.BlockSpec(memory_space=pl.ANY)] * 4],
         out_specs=[WHOLE] * 4,
         out_shape=[
             jax.ShapeDtypeStruct((4 * quarter, width), F32),
@@ -969,7 +969,7 @@
         ),
         cost_estimate=lasting(85),
         name="finish",
-    )(part, tokens_own, total, gain, gain_two, *grads, ready)
+    )(part, tokens_own, total, gain, gain_two, *grads, *ready)
 
 
 def gather_weights(line, own_ref, out_ref, gains_ref, grad_ref, full_ref, out_full_ref, gains_full_ref, rows_ref, local_sems, side_send, side_recv, line_send, line_recv, rows_send, rows_recv, staged_ref):
@@ -1387,6 +1387,8 @@
     grad_qkv_part = dot_tn(normed_one, grad_qkv).astype(BF16)
     grad_out_part = dot_tn(mixed_slots, grad_middle_slots).astype(BF16)
     grad_normed_one = dot_nt(grad_qkv, qkv_full).astype(BF16)
+    side_ref = side.astype(jnp.int32).reshape(1)
+    gate_theirs = links.swap_side(call_pick_rows(side_ref, gate_sum, grad_qkv))
     input_grad, gain_terms, grad_qkv_own, grad_out = call_finish(
         dp_size,
         after(grad_normed_one, gate_sum),
@@ -1394,7 +1396,7 @@
         grad_middle,
         gains_full[0:1],
         gain_two,
-        output_first,
+        (output_first, down_direction, early, gate_theirs),
         grad_qkv_part,
         grad_out_part,
     )
@@ -1403,11 +1405,7 @@
     output_far = links.swap_mp(output_low, 2)
 
     summed = [gate_sum, up_sum]
-    side_ref = side.astype(jnp.int32).reshape(1)
-    theirs = [
-        links.swap_side(call_pick_rows(side_ref, value, ready))
-        for value, ready in ((gate_sum, grad_qkv), (up_sum, gain_terms))
-    ]
+    theirs = [gate_theirs, links.swap_side(call_pick_rows(side_ref, up_sum, gain_terms))]
     gain_terms = gain_terms.reshape(2, width)
     gain_width = norm_gains.shape[1]
     grad_gains = lax.dynamic_slice_in_dim(gain_terms, links.index * gain_width, gain_width, 1)

time: 742 us -> 733 us (0.988)
  Pallas kernels: 482 us -> 470 us
    pallas_call x1, Pallas kernels: 125 us -> 113 us  [call_finish(): pl.pallas_call(functools.partial(finish, line), in_specs=[*[WHOLE] * 7, *...]
    unnamed x146 -> x148, local copies, waits for them, and re-layouts: 31.2 us -> 29 us
  transfers between devices with their start and end apart: 14 -> 14, of which waited for: 3 -> 5; matrix products, arithmetic and copies ran while one was open for 17% -> 17% of each run, Pallas kernels for 63% -> 63%
where the time goes in v5:
time: 733 us; the launch traced here: 727 us
  Pallas kernels  470 us (64%)
  matrix products  117 us (16%)
  other arithmetic  45 us (6%)
  local copies, waits for them, and re-layouts  38.2 us (5%)
  waiting for transfers between devices  30.5 us (4%)
  between operations  15.7 us (2%)
  starting transfers between devices  10.7 us (1%)
    pallas_call x1, Pallas kernels, call_gather_weights(): pl.pallas_call(functools.partial(gather_weights, line), in_specs=[hbm] *...  143 us
    pallas_call x1, Pallas kernels, call_finish(): pl.pallas_call(functools.partial(finish, line), in_specs=[*[WHOLE] * 7, *...  113 us
    pallas_call x1, Pallas kernels, call_spread_backward(): pl.pallas_call(spread_backward, in_specs=[*[WHOLE] * 4, hbm, hbm, hbm], o...  66.9 us
    pallas_call x1, Pallas kernels, call_spread_forward(): pl.pallas_call(spread_forward, in_specs=[*[WHOLE] * 3, hbm, hbm], out_spe...  62.8 us
    dot_general x4, matrix products, dot_tn(): lax.dot_general(left, right, (((0,), (0,)), ((), ())), preferred_element_...  39.1 us
    dot_general x3, matrix products, dot_nt(): lax.dot_general(left, right, (((1,), (1,)), ((), ())), preferred_element_...  30.7 us
    unnamed x148, local copies, waits for them, and re-layouts  29 us
    ppermute x5, waiting for transfers between devices, swap_side(): return lax.ppermute(value, 'dp', [(i, i ^ 1) for i in range(self.dp)])  28.5 us
  transfers between devices with their start and end apart: 14, of which 5 were waited for; matrix products, arithmetic and copies ran while one was open for 17% of the time, Pallas kernels for 63%

profile of v5, /device:TPU:0, one launch (start us, length us, event | category | flops | bytes accessed | tf_op | source)
XLA Modules:
  0.0 727.1 jit_solution(14757211608331571984)
XLA Ops:
  18.0 23.2 %collective-permute-done = bf16[256,2048]{0,1:T(8,128)(2,1)} collective-permute-done((bf16[256,2048]{0,1:T(8,128)(2,1)}, bf16[256,2048]{0,1:T(8,128)(2,1)}, u32[]{:S(2)}, u32[]{:S(2)}) %collective-permute-start) | collective-permute-done | bytes 1048608 | tf_op jit(solution)/shard_map/ppermute | solution.py:1210
  52.4 143.0 %gather_weights.1 = (bf16[2048,1024]{1,0:T(8,128)(2,1)S(1)}, bf16[512,2048]{1,0:T(8,128)(2,1)S(1)}, f32[64,256]{1,0:T(8,128)S(1)}, bf16[2048,2048]{1,0:T(8,128)(2,1)S(1)}) custom-call(bf16[256,1024]{1,0:T(8,128)(2,1)S(1)} %slice_dynamic-update-slice_fusion.2.own_ref, bf16[64,2048]{1,0:T(8,128)(2,1)S(1)} %get-tuple-element.194.out_ref, ...), custom_call_target="tpu_custom_call" | custom-call | bytes 360000000 | tf_op jit(solution)/shard_map/gather_weights/pallas_call | solution.py:1142
  200.1 6.3 fusion.12.qkv_ref
  206.5 11.8 %attention_forward.1 = (bf16[1024,512]{1,0:T(8,128)(2,1)S(1)}, bf16[1024,1024]{1,0:T(8,128)(2,1)S(1)}, f32[1024,512]{1,0:T(8,128)}, f32[2,8,128]{2,1,0:T(8,128)S(1)}) custom-call(s32[1]{0:T(128)} %bitcast.rank_ref, f32[1024,1024]{1,0:T(8,128)} %fusion.12.qkv_ref, f32[1024,128]{1,0:T(8,128)S(1)} %get-tuple-element.213.cos_ref, ...), custom_call_target="tpu_custom_call" | custom-call | bytes 36000000 | tf_op jit(solution)/shard_map/attention_forward/pallas_call | solution.py:149
  220.7 4.4 convolution_convert_fusion.3.part_ref
  225.0 62.8 %spread_forward.1 = (bf16[2048,2048]{1,0:T(8,128)(2,1)}, f32[256,2048]{1,0:T(8,128)}, f32[2048,1024]{1,0:T(8,128)}) custom-call(bf16[1024,2048]{1,0:T(8,128)(2,1)} %convolution_convert_fusion.3.part_ref, bf16[256,2048]{1,0:T(8,128)(2,1)} %copy-done.45, f32[1,2048]{1,0:T(1,128)} %bitcast.69, bf16[2048,2048]{1,0:T(8,128)(2,1)} %copy-done, ...), custom_call_target="tpu_custom_call" | custom-call | bytes 192000000 | tf_op jit(solution)/shard_map/spread_forward/pallas_call | solution.py:593
  287.8 24.6 %fusion.23.both_ref = f32[2048,2048]{1,0:T(8,128)} fusion(bf16[2048,2048]{1,0:T(8,128)(2,1)} %get-tuple-element.106.left_ref, bf16[2048,2048]{0,1:T(8,128)(2,1)} %all-gather.5.cloned.1.call-done), kind=kOutput, calls=%fused_computation.94 | convolution fusion | flops 17179869184 | bytes 33554432 | tf_op jit(solution)/shard_map/dot_general | solution.py:1347
  312.4 14.6 %gate_rows.1 = (bf16[2048,1024]{1,0:T(8,128)(2,1)}, bf16[2048,2048]{1,0:T(8,128)(2,1)}) custom-call(f32[2048,2048]{1,0:T(8,128)} %fusion.23.both_ref, f32[2048,1024]{1,0:T(8,128)} %get-tuple-element.108.grad_ref), custom_call_target="tpu_custom_call" | custom-call | bytes 30000000 | tf_op jit(solution)/shard_map/gate_rows/pallas_call | solution.py:201
  327.0 14.1 %fusion.5 = bf16[2048,1024]{1,0:T(8,128)(2,1)} fusion(bf16[2048,2048]{1,0:T(8,128)(2,1)} %get-tuple-element.106.left_ref, bf16[2048,2048]{1,0:T(8,128)(2,1)} %get-tuple-element.113.both_ref), kind=kOutput, calls=%fused_computation.13 | convolution fusion | flops 8592031744 | bytes 16777216 | tf_op jit(solution)/shard_map/dot_general | solution.py:61
  341.2 14.2 %convolution_convert_fusion.2 = bf16[1024,2048]{1,0:T(8,128)(2,1)} fusion(bf16[2048,1024]{1,0:T(8,128)(2,1)} %get-tuple-element.110, bf16[2048,2048]{1,0:T(8,128)(2,1)} %copy-done), kind=kOutput, calls=%fused_computation.14 | convolution fusion | flops 8592031744 | bytes 16777216 | tf_op jit(solution)/shard_map/dot_general | solution.py:61
  355.5 11.9 %convolution_convert_fusion.1 = bf16[2048,2048]{1,0:T(8,128)(2,1)S(1)} fusion(bf16[2048,1024]{1,0:T(8,128)(2,1)} %get-tuple-element.110, bf16[1024,2048]{1,0:T(8,128)(2,1)} %all-gather.3.cloned.1.call-done.down_ref), kind=kOutput, calls=%fused_computation.6 | convolution fusion | flops 8594128896 | bytes 16777216 | tf_op jit(solution)/shard_map/dot_general | solution.py:1350
  369.0 4.9 slice.154.grad_ref
  379.8 22.3 %convolution_convert_fusion.part_ref = bf16[2048,2048]{1,0:T(8,128)(2,1)} fusion(bf16[2048,2048]{1,0:T(8,128)(2,1)S(1)} %bitcast.62, bf16[2048,2048]{0,1:T(8,128)(2,1)} %all-gather.5.cloned.1.call-done), kind=kOutput, calls=%fused_computation.5 | convolution fusion | flops 17184063488 | bytes 25165824 | tf_op jit(solution)/shard_map/dot_general | solution.py:53
  404.5 66.9 %spread_backward.1 = (bf16[1024,2048]{1,0:T(8,128)(2,1)}, f32[256,2048]{1,0:T(8,128)}, f32[8,2048]{1,0:T(8,128)}, bf16[2048,1024]{1,0:T(8,128)(2,1)}) custom-call(bf16[2048,2048]{1,0:T(8,128)(2,1)} %convolution_convert_fusion.part_ref, f32[256,2048]{1,0:T(8,128)} %get-tuple-element.105.middle_ref, bf16[256,2048]{1,0:T(8,128)(2,1)} %slice.154.grad_ref, ...), custom_call_target="tpu_custom_call" | custom-call | bytes 204000000 | tf_op jit(solution)/shard_map/spread_backward/pallas_call | solution.py:720
  485.7 13.3 %attention_backward.1._ = bf16[1024,1024]{1,0:T(8,128)(2,1)S(1)} custom-call(s32[1]{0:T(128)} %bitcast.rank_ref, bf16[1024,1024]{1,0:T(8,128)(2,1)} %copy-done.18, bf16[1024,512]{1,0:T(8,128)(2,1)S(1)} %convolution_convert_fusion.7.grad_ref, f32[1024,512]{1,0:T(8,128)} %get-tuple-element.118.lse_ref, f32[1024,128]{1,0:T(8,128)S(1)} %copy-done.7, ...), custom_call_target="tpu_custom_call" | custom-call | bytes 39000000 | tf_op jit(solution)/shard_map/attention_backward/pallas_call | solution.py:172
  499.1 6.1 convolution_convert_fusion.5.part_ref
  505.3 7.0 convolution_convert_fusion.4.refs_1_
  518.9 6.6 multiply_reduce_fusion.2
  525.5 5.2 select_select_fusion.refs_5_.early_ref
  532.3 112.9 %finish.1 = (f32[1024,2048]{1,0:T(8,128)}, f32[8,512]{1,0:T(8,128)}, f32[256,1024]{1,0:T(8,128)}, f32[64,2048]{1,0:T(8,128)}) custom-call(bf16[1024,2048]{1,0:T(8,128)(2,1)} %convolution_convert_fusion.5.part_ref, bf16[256,2048]{1,0:T(8,128)(2,1)} %copy-done.45, f32[256,2048]{1,0:T(8,128)} %get-tuple-element.121.total_ref, f32[1,2048]{1,0:T(1,128)} %bitcast.71, ...), custom_call_target="tpu_custom_call" | custom-call | bytes 255000000 | tf_op jit(solution)/shard_map/finish/pallas_call | solution.py:940
  645.3 4.2 add_convert_fusion
  666.0 16.5 %gate_up_step.1 = (f32[2,256,2048]{2,1,0:T(8,128)}, f32[2,256,2048]{2,1,0:T(8,128)}, f32[2,256,2048]{2,1,0:T(8,128)}, f32[8,256]{1,0:T(8,128)}) custom-call(s32[1]{0:T(128)} %bitcast.12.side_ref, f32[2,256,2048]{2,1,0:T(8,128)} %master_ref.2, f32[2,2,256,2048]{3,2,1,0:T(8,128)} %moment_ref.1, ...), custom_call_target="tpu_custom_call" | custom-call | bytes 48000000 | tf_op jit(solution)/shard_map/gate_up_step/pallas_call | solution.py:241
  685.6 9.8 %combine_all.1.packed_ref = f32[16,128]{1,0:T(8,128)} custom-call(f32[16,128]{1,0:T(8,128)} %select_select_fusion.refs_5_.early_ref, f32[8,128]{1,0:T(8,128)} %copy-done.37, f32[8,256]{1,0:T(8,128)} %get-tuple-element.134.gate_up_ref), custom_call_target="tpu_custom_call" | custom-call | bytes 30000000 | tf_op jit(solution)/shard_map/combine_all/pallas_call | solution.py:1187
  699.1 6.7 large_update.2
  (234 shorter events, 98.0 us)
Async XLA Ops:
  7.2 217.8 %all-gather.3.cloned.1.call-start = ((), (), s32[]{:S(2)}) async-start(), calls=%async_computation.3 | async-start | bytes 5242880 | tf_op jit(solution)/shard_map/all_gather | solution.py:1213
  10.0 277.9 %all-gather.5.cloned.1.call-start = ((), (), s32[]{:S(2)}) async-start(), calls=%async_computation.4 | async-start | bytes 10485760 | tf_op jit(solution)/shard_map/all_gather | solution.py:1213
  14.8 26.4 %collective-permute-start = (bf16[256,2048]{0,1:T(8,128)(2,1)}, bf16[256,2048]{0,1:T(8,128)(2,1)}, u32[]{:S(2)}, u32[]{:S(2)}) collective-permute-start(bf16[256,2048]{0,1:T(8,128)(2,1)} %pad_maximum_fusion.4), channel_id=1, source_target_pairs={{0,4},{4,0},{8,12},{12,8},{16,20},{20,16},{24,28},{28,24},{1,5},{5... | collective-permute-start | bytes 3145736 | tf_op jit(solution)/shard_map/ppermute | solution.py:1210
  17.7 26.2 %copy-start.31 = (s32[1,1024]{1,0:T(1,128)S(1)}, s32[1,1024]{1,0:T(1,128)}, u32[]{:S(2)}) copy-start(s32[1,1024]{1,0:T(1,128)} %param.19) | copy-start | bytes 12292
  17.7 26.5 %copy-start.33 = (f32[2,256]{1,0:T(2,128)S(1)}, f32[2,256]{1,0:T(2,128)}, u32[]{:S(2)}) copy-start(f32[2,256]{1,0:T(2,128)} %refs_4_.3) | copy-start | bytes 6148
  43.9 472.2 %reduce-scatter.4.cloned.1.call-start = ((), (), s32[]{:S(2)}) async-start(), calls=%async_computation.5 | async-start | bytes 5242880 | tf_op jit(solution)/shard_map/reduce_scatter | solution.py:1216
  44.2 162.3 %copy-start.10 = (s32[1024,1]{1,0:T(8,128)}, s32[1024,1]{1,0:T(8,128)S(1)}, u32[]{:S(2)}) copy-start(s32[1024,1]{1,0:T(8,128)S(1)} %copy.55.seg_col_ref) | copy-start | bytes 12292
  47.1 159.3 %copy-start.6 = (f32[1024,128]{1,0:T(8,128)}, f32[1024,128]{1,0:T(8,128)S(1)}, u32[]{:S(2)}) copy-start(f32[1024,128]{1,0:T(8,128)S(1)} %get-tuple-element.213.cos_ref) | copy-start | bytes 1572868
  47.2 159.3 %copy-start.8 = (f32[1024,128]{1,0:T(8,128)}, f32[1024,128]{1,0:T(8,128)S(1)}, u32[]{:S(2)}) copy-start(f32[1024,128]{1,0:T(8,128)S(1)} %get-tuple-element.214.sin_ref) | copy-start | bytes 1572868
  48.9 151.2 %copy-start.53 = (bf16[1024,2048]{1,0:T(8,128)(2,1)}, bf16[1024,2048]{1,0:T(8,128)(2,1)S(1)}, u32[]{:S(2)}) copy-start(bf16[1024,2048]{1,0:T(8,128)(2,1)S(1)} %get-tuple-element.171) | copy-start | bytes 12582916
  49.2 150.9 %copy-start.60 = (f32[1024]{0:T(1024)}, f32[1024]{0:T(1024)S(1)}, u32[]{:S(2)}) copy-start(f32[1024]{0:T(1024)S(1)} %add_rsqrt_fusion) | copy-start | bytes 12292
  341.2 174.9 %reduce-scatter.6.cloned.1.call-start = ((), (), s32[]{:S(2)}) async-start(), calls=%async_computation.6 | async-start | bytes 5242880 | tf_op jit(solution)/shard_map/reduce_scatter | solution.py:1216
  355.5 295.6 %reduce-scatter.8.cloned.1.call-start = ((), (), s32[]{:S(2)}) async-start(), calls=%async_computation.7 | async-start | bytes 5242880 | tf_op jit(solution)/shard_map/reduce_scatter | solution.py:1216
  368.6 7.2 collective-permute-start.1
  375.8 26.3 %copy-start.51 = (bf16[1024,2048]{1,0:T(8,128)(2,1)}, bf16[1024,2048]{1,0:T(8,128)(2,1)S(1)}, u32[]{:S(2)}) copy-start(bf16[1024,2048]{1,0:T(8,128)(2,1)S(1)} %collective-permute-done.1) | copy-start | bytes 12582916
  378.1 25.4 %collective-permute-start.3 = (bf16[256,2048]{1,0:T(8,128)(2,1)S(1)}, bf16[256,2048]{1,0:T(8,128)(2,1)S(1)}, u32[]{:S(2)}, u32[]{:S(2)}) collective-permute-start(bf16[256,2048]{1,0:T(8,128)(2,1)S(1)} %get-tuple-element.173), channel_id=1, source_target_pairs={{0,4},{4,0},{8,12},{12,8},{16,20},{20,16},{24,28},{28,24},{1,5},{5... | collective-permute-start | bytes 3145736 | tf_op jit(solution)/shard_map/ppermute | solution.py:1210
  477.4 53.3 %collective-permute-start.2 = (bf16[256,2048]{1,0:T(8,128)(2,1)}, bf16[256,2048]{1,0:T(8,128)(2,1)S(1)}, u32[]{:S(2)}, u32[]{:S(2)}) collective-permute-start(bf16[256,2048]{1,0:T(8,128)(2,1)} %get-tuple-element.172), channel_id=1, source_target_pairs={{0,4},{4,0},{8,12},{12,8},{16,20},{20,16},{24,28},{28,24},{1,5},{5... | collective-permute-start | bytes 3145736 | tf_op jit(solution)/shard_map/ppermute | solution.py:1210
  481.9 163.3 %collective-permute-start.4 = (bf16[256,2048]{1,0:T(8,128)(2,1)}, bf16[256,2048]{1,0:T(8,128)(2,1)}, u32[]{:S(2)}, u32[]{:S(2)}) collective-permute-start(bf16[256,2048]{1,0:T(8,128)(2,1)} %add_convert_fusion.1), channel_id=1, source_target_pairs={{0,2},{1,3},{2,0},{3,1},{4,6},{5,7},{6,4},{7,5},{8,10},{9,11},{10,... | collective-permute-start | bytes 3145736 | tf_op jit(solution)/shard_map/ppermute | solution.py:1207
  518.0 13.5 %collective-permute-start.5 = (bf16[256,1024]{1,0:T(8,128)(2,1)}, bf16[256,1024]{1,0:T(8,128)(2,1)S(1)}, u32[]{:S(2)}, u32[]{:S(2)}) collective-permute-start(bf16[256,1024]{1,0:T(8,128)(2,1)} %pick_rows.2), channel_id=1, source_target_pairs={{0,4},{4,0},{8,12},{12,8},{16,20},{20,16},{24,28},{28,24},{1,5},{5... | collective-permute-start | bytes 1572872 | tf_op jit(solution)/shard_map/ppermute | solution.py:1210
  532.3 112.9 %copy-start.48 = (f32[256,2048]{1,0:T(8,128)S(1)}, f32[256,2048]{1,0:T(8,128)}, u32[]{:S(2)}) copy-start(f32[256,2048]{1,0:T(8,128)} %get-tuple-element.105.middle_ref) | copy-start | bytes 6291460
  649.5 33.0 %collective-permute-start.6 = (bf16[256,2048]{1,0:T(8,128)(2,1)}, bf16[256,2048]{1,0:T(8,128)(2,1)}, u32[]{:S(2)}, u32[]{:S(2)}) collective-permute-start(bf16[256,2048]{1,0:T(8,128)(2,1)} %add_convert_fusion), channel_id=1, source_target_pairs={{0,2},{1,3},{2,0},{3,1},{4,6},{5,7},{6,4},{7,5},{8,10},{9,11},{10,... | collective-permute-start | bytes 3145736 | tf_op jit(solution)/shard_map/ppermute | solution.py:1207
  652.9 13.1 %collective-permute-start.7 = (bf16[256,1024]{1,0:T(8,128)(2,1)}, bf16[256,1024]{1,0:T(8,128)(2,1)}, u32[]{:S(2)}, u32[]{:S(2)}) collective-permute-start(bf16[256,1024]{1,0:T(8,128)(2,1)} %pick_rows.3), channel_id=1, source_target_pairs={{0,4},{4,0},{8,12},{12,8},{16,20},{20,16},{24,28},{28,24},{1,5},{5... | collective-permute-start | bytes 1572872 | tf_op jit(solution)/shard_map/ppermute | solution.py:1210
  653.5 29.0 %copy-start.35 = (f32[2,256]{1,0:T(2,128)}, f32[2,256]{1,0:T(2,128)S(1)}, u32[]{:S(2)}) copy-start(f32[2,256]{1,0:T(2,128)S(1)} %constant_dynamic-slice_fusion.grad_gains_ref) | copy-start | bytes 6148
  685.6 23.9 %collective-permute-start.8 = (bf16[512,2048]{1,0:T(8,128)(2,1)}, bf16[512,2048]{1,0:T(8,128)(2,1)}, u32[]{:S(2)}, u32[]{:S(2)}) collective-permute-start(bf16[512,2048]{1,0:T(8,128)(2,1)} %pad_maximum_fusion.3), channel_id=1, source_target_pairs={{0,1},{1,0},{2,3},{3,2},{4,5},{5,4},{6,7},{7,6},{8,9},{9,8},{10,11... | collective-permute-start | bytes 6291464 | tf_op jit(solution)/shard_map/ppermute | solution.py:1207
  (58 other events, 317.9 us)
Sparse Core Ops, SparseCore 0:
  10.2 101.1 all-gather.2
  113.5 164.0 all-gather.4
  341.3 81.2 reduce-scatter.3
  425.4 77.2 reduce-scatter.5
  504.9 97.2 reduce-scatter.7

commit v6 on v5

--- a/solution.py
+++ b/solution.py
@@ -217,14 +217,15 @@
 
 def gate_up_step(side_ref, master_ref, moment_ref, *refs):
     (gate_mine, up_mine, gate_theirs, up_theirs), (grad_ref, second_ref, direction_ref, sums_ref) = refs[:4], refs[4:]
-    part, place, which = pl.program_id(0), pl.program_id(1), pl.program_id(2)
+    part, place = pl.program_id(0), pl.program_id(1)
     mine = jnp.where(part == 0, gate_mine[...], up_mine[...])
     theirs = jnp.where(part == 0, gate_theirs[...], up_theirs[...])
-    grad = jnp.where(which == side_ref[0], mine, theirs).astype(F32)
+    first = side_ref[0] == 0
+    grad = jnp.concatenate([jnp.where(first, mine, theirs), jnp.where(first, theirs, mine)], 1).astype(F32)
     second, direction = lamb_direction(master_ref[0], moment_ref[0, 0], moment_ref[1, 0], grad)
     grad_ref[0], second_ref[0], direction_ref[0] = grad, second, direction
 
-    @pl.when((part == 0) & (place == 0) & (which == 0))
+    @pl.when((part == 0) & (place == 0))
     def _():
         sums_ref[...] = jnp.zeros(sums_ref.shape, F32)
 
@@ -234,7 +235,7 @@
 def call_gate_up_step(line, side, master, moments, summed, theirs):
     _, shard, units = master.shape
     block = units // (2 * line)
-    whole = pl.BlockSpec((1, shard, block), lambda g, p, w, side: (g, 0, p * 2 + w))
+    whole = pl.BlockSpec((1, shard, 2 * block), lambda g, p, side: (g, 0, p))
     shape = jax.ShapeDtypeStruct(master.shape, F32)
     gate_place = lambda g, p: jnp.where(g == 0, p, line - 1)
     up_place = lambda g, p: jnp.where(g == 1, p, 0)
@@ -242,18 +243,18 @@
         gate_up_step,
         grid_spec=pltpu.PrefetchScalarGridSpec(
             num_scalar_prefetch=1,
-            grid=(2, line, 2),
+            grid=(2, line),
             in_specs=[
                 whole,
-                pl.BlockSpec((2, 1, shard, block), lambda g, p, w, side: (0, g, 0, p * 2 + w)),
-                pl.BlockSpec((shard, block), lambda g, p, w, side: (side[0], gate_place(g, p))),
-                pl.BlockSpec((shard, block), lambda g, p, w, side: (side[0], up_place(g, p))),
-                pl.BlockSpec((shard, block), lambda g, p, w, side: (0, gate_place(g, p))),
-                pl.BlockSpec((shard, block), lambda g, p, w, side: (0, up_place(g, p))),
+                pl.BlockSpec((2, 1, shard, 2 * block), lambda g, p, side: (0, g, 0, p)),
+                pl.BlockSpec((shard, block), lambda g, p, side: (side[0], gate_place(g, p))),
+                pl.BlockSpec((shard, block), lambda g, p, side: (side[0], up_place(g, p))),
+                pl.BlockSpec((shard, block), lambda g, p, side: (0, gate_place(g, p))),
+                pl.BlockSpec((shard, block), lambda g, p, side: (0, up_place(g, p))),
             ],
-            out_specs=[whole, whole, whole, pl.BlockSpec((8, block), lambda g, p, w, side: (0, 0))],
+            out_specs=[whole, whole, whole, pl.BlockSpec((8, 2 * block), lambda g, p, side: (0, 0))],
         ),
-        out_shape=[shape, shape, shape, jax.ShapeDtypeStruct((8, block), F32)],
+        out_shape=[shape, shape, shape, jax.ShapeDtypeStruct((8, 2 * block), F32)],
         cost_estimate=lasting(16),
         name="gate_up_step",
     )(side, master, moments, *summed, *theirs)

time: 733 us -> 729 us (level)
  transfers between devices with their start and end apart: 14 -> 14, of which waited for: 5 -> 5; matrix products, arithmetic and copies ran while one was open for 17% -> 18% of each run, Pallas kernels for 63% -> 62%
where the time goes in v6:
time: 729 us; the launch traced here: 723 us
  Pallas kernels  466 us (64%)
  matrix products  117 us (16%)
  other arithmetic  45 us (6%)
  local copies, waits for them, and re-layouts  38.2 us (5%)
  waiting for transfers between devices  30.5 us (4%)
  between operations  15.7 us (2%)
  starting transfers between devices  10.7 us (1%)
    pallas_call x1, Pallas kernels, call_gather_weights(): pl.pallas_call(functools.partial(gather_weights, line), in_specs=[hbm] *...  143 us
    pallas_call x1, Pallas kernels, call_finish(): pl.pallas_call(functools.partial(finish, line), in_specs=[*[WHOLE] * 7, *...  113 us
    pallas_call x1, Pallas kernels, call_spread_backward(): pl.pallas_call(spread_backward, in_specs=[*[WHOLE] * 4, hbm, hbm, hbm], o...  66.9 us
    pallas_call x1, Pallas kernels, call_spread_forward(): pl.pallas_call(spread_forward, in_specs=[*[WHOLE] * 3, hbm, hbm], out_spe...  62.8 us
    dot_general x4, matrix products, dot_tn(): lax.dot_general(left, right, (((0,), (0,)), ((), ())), preferred_element_...  39.1 us
    dot_general x3, matrix products, dot_nt(): lax.dot_general(left, right, (((1,), (1,)), ((), ())), preferred_element_...  30.7 us
    unnamed x148, local copies, waits for them, and re-layouts  29 us
    ppermute x5, waiting for transfers between devices, swap_side(): return lax.ppermute(value, 'dp', [(i, i ^ 1) for i in range(self.dp)])  28.5 us
  transfers between devices with their start and end apart: 14, of which 5 were waited for; matrix products, arithmetic and copies ran while one was open for 18% of the time, Pallas kernels for 62%

profile of v6, /device:TPU:0, one launch (start us, length us, event | category | flops | bytes accessed | tf_op | source)
XLA Modules:
  0.0 723.3 jit_solution(17973378424226386191)
XLA Ops:
  18.0 23.2 %collective-permute-done = bf16[256,2048]{0,1:T(8,128)(2,1)} collective-permute-done((bf16[256,2048]{0,1:T(8,128)(2,1)}, bf16[256,2048]{0,1:T(8,128)(2,1)}, u32[]{:S(2)}, u32[]{:S(2)}) %collective-permute-start) | collective-permute-done | bytes 1048608 | tf_op jit(solution)/shard_map/ppermute | solution.py:1211
  52.4 143.0 %gather_weights.1 = (bf16[2048,1024]{1,0:T(8,128)(2,1)S(1)}, bf16[512,2048]{1,0:T(8,128)(2,1)S(1)}, f32[64,256]{1,0:T(8,128)S(1)}, bf16[2048,2048]{1,0:T(8,128)(2,1)S(1)}) custom-call(bf16[256,1024]{1,0:T(8,128)(2,1)S(1)} %slice_dynamic-update-slice_fusion.2.own_ref, bf16[64,2048]{1,0:T(8,128)(2,1)S(1)} %get-tuple-element.194.out_ref, ...), custom_call_target="tpu_custom_call" | custom-call | bytes 360000000 | tf_op jit(solution)/shard_map/gather_weights/pallas_call | solution.py:1143
  200.1 6.3 fusion.12.qkv_ref
  206.5 11.8 %attention_forward.1 = (bf16[1024,512]{1,0:T(8,128)(2,1)S(1)}, bf16[1024,1024]{1,0:T(8,128)(2,1)S(1)}, f32[1024,512]{1,0:T(8,128)}, f32[2,8,128]{2,1,0:T(8,128)S(1)}) custom-call(s32[1]{0:T(128)} %bitcast.rank_ref, f32[1024,1024]{1,0:T(8,128)} %fusion.12.qkv_ref, f32[1024,128]{1,0:T(8,128)S(1)} %get-tuple-element.213.cos_ref, ...), custom_call_target="tpu_custom_call" | custom-call | bytes 36000000 | tf_op jit(solution)/shard_map/attention_forward/pallas_call | solution.py:149
  220.7 4.4 convolution_convert_fusion.3.part_ref
  225.0 62.8 %spread_forward.1 = (bf16[2048,2048]{1,0:T(8,128)(2,1)}, f32[256,2048]{1,0:T(8,128)}, f32[2048,1024]{1,0:T(8,128)}) custom-call(bf16[1024,2048]{1,0:T(8,128)(2,1)} %convolution_convert_fusion.3.part_ref, bf16[256,2048]{1,0:T(8,128)(2,1)} %copy-done.45, f32[1,2048]{1,0:T(1,128)} %bitcast.69, bf16[2048,2048]{1,0:T(8,128)(2,1)} %copy-done, ...), custom_call_target="tpu_custom_call" | custom-call | bytes 192000000 | tf_op jit(solution)/shard_map/spread_forward/pallas_call | solution.py:594
  287.8 24.6 %fusion.23.both_ref = f32[2048,2048]{1,0:T(8,128)} fusion(bf16[2048,2048]{1,0:T(8,128)(2,1)} %get-tuple-element.106.left_ref, bf16[2048,2048]{0,1:T(8,128)(2,1)} %all-gather.5.cloned.1.call-done), kind=kOutput, calls=%fused_computation.94 | convolution fusion | flops 17179869184 | bytes 33554432 | tf_op jit(solution)/shard_map/dot_general | solution.py:1348
  312.4 14.6 %gate_rows.1 = (bf16[2048,1024]{1,0:T(8,128)(2,1)}, bf16[2048,2048]{1,0:T(8,128)(2,1)}) custom-call(f32[2048,2048]{1,0:T(8,128)} %fusion.23.both_ref, f32[2048,1024]{1,0:T(8,128)} %get-tuple-element.108.grad_ref), custom_call_target="tpu_custom_call" | custom-call | bytes 30000000 | tf_op jit(solution)/shard_map/gate_rows/pallas_call | solution.py:201
  327.0 14.1 %fusion.5 = bf16[2048,1024]{1,0:T(8,128)(2,1)} fusion(bf16[2048,2048]{1,0:T(8,128)(2,1)} %get-tuple-element.106.left_ref, bf16[2048,2048]{1,0:T(8,128)(2,1)} %get-tuple-element.113.both_ref), kind=kOutput, calls=%fused_computation.13 | convolution fusion | flops 8592031744 | bytes 16777216 | tf_op jit(solution)/shard_map/dot_general | solution.py:61
  341.2 14.2 %convolution_convert_fusion.2 = bf16[1024,2048]{1,0:T(8,128)(2,1)} fusion(bf16[2048,1024]{1,0:T(8,128)(2,1)} %get-tuple-element.110, bf16[2048,2048]{1,0:T(8,128)(2,1)} %copy-done), kind=kOutput, calls=%fused_computation.14 | convolution fusion | flops 8592031744 | bytes 16777216 | tf_op jit(solution)/shard_map/dot_general | solution.py:61
  355.5 11.9 %convolution_convert_fusion.1 = bf16[2048,2048]{1,0:T(8,128)(2,1)S(1)} fusion(bf16[2048,1024]{1,0:T(8,128)(2,1)} %get-tuple-element.110, bf16[1024,2048]{1,0:T(8,128)(2,1)} %all-gather.3.cloned.1.call-done.down_ref), kind=kOutput, calls=%fused_computation.6 | convolution fusion | flops 8594128896 | bytes 16777216 | tf_op jit(solution)/shard_map/dot_general | solution.py:1351
  369.0 4.9 slice.154.grad_ref
  379.8 22.3 %convolution_convert_fusion.part_ref = bf16[2048,2048]{1,0:T(8,128)(2,1)} fusion(bf16[2048,2048]{1,0:T(8,128)(2,1)S(1)} %bitcast.62, bf16[2048,2048]{0,1:T(8,128)(2,1)} %all-gather.5.cloned.1.call-done), kind=kOutput, calls=%fused_computation.5 | convolution fusion | flops 17184063488 | bytes 25165824 | tf_op jit(solution)/shard_map/dot_general | solution.py:53
  404.5 66.9 %spread_backward.1 = (bf16[1024,2048]{1,0:T(8,128)(2,1)}, f32[256,2048]{1,0:T(8,128)}, f32[8,2048]{1,0:T(8,128)}, bf16[2048,1024]{1,0:T(8,128)(2,1)}) custom-call(bf16[2048,2048]{1,0:T(8,128)(2,1)} %convolution_convert_fusion.part_ref, f32[256,2048]{1,0:T(8,128)} %get-tuple-element.105.middle_ref, bf16[256,2048]{1,0:T(8,128)(2,1)} %slice.154.grad_ref, ...), custom_call_target="tpu_custom_call" | custom-call | bytes 204000000 | tf_op jit(solution)/shard_map/spread_backward/pallas_call | solution.py:721
  485.7 13.3 %attention_backward.1._ = bf16[1024,1024]{1,0:T(8,128)(2,1)S(1)} custom-call(s32[1]{0:T(128)} %bitcast.rank_ref, bf16[1024,1024]{1,0:T(8,128)(2,1)} %copy-done.18, bf16[1024,512]{1,0:T(8,128)(2,1)S(1)} %convolution_convert_fusion.7.grad_ref, f32[1024,512]{1,0:T(8,128)} %get-tuple-element.118.lse_ref, f32[1024,128]{1,0:T(8,128)S(1)} %copy-done.7, ...), custom_call_target="tpu_custom_call" | custom-call | bytes 39000000 | tf_op jit(solution)/shard_map/attention_backward/pallas_call | solution.py:172
  499.1 6.1 convolution_convert_fusion.5.part_ref
  505.3 7.0 convolution_convert_fusion.4.refs_1_
  518.9 6.6 multiply_reduce_fusion.2
  525.5 5.2 select_select_fusion.refs_5_.early_ref
  532.3 112.9 %finish.1 = (f32[1024,2048]{1,0:T(8,128)}, f32[8,512]{1,0:T(8,128)}, f32[256,1024]{1,0:T(8,128)}, f32[64,2048]{1,0:T(8,128)}) custom-call(bf16[1024,2048]{1,0:T(8,128)(2,1)} %convolution_convert_fusion.5.part_ref, bf16[256,2048]{1,0:T(8,128)(2,1)} %copy-done.45, f32[256,2048]{1,0:T(8,128)} %get-tuple-element.121.total_ref, f32[1,2048]{1,0:T(1,128)} %bitcast.71, ...), custom_call_target="tpu_custom_call" | custom-call | bytes 255000000 | tf_op jit(solution)/shard_map/finish/pallas_call | solution.py:941
  645.3 4.2 add_convert_fusion
  666.0 12.7 %gate_up_step.1 = (f32[2,256,2048]{2,1,0:T(8,128)}, f32[2,256,2048]{2,1,0:T(8,128)}, f32[2,256,2048]{2,1,0:T(8,128)}, f32[8,512]{1,0:T(8,128)}) custom-call(s32[1]{0:T(128)} %bitcast.12.side_ref, f32[2,256,2048]{2,1,0:T(8,128)} %master_ref.2, f32[2,2,256,2048]{3,2,1,0:T(8,128)} %moment_ref.1, ...), custom_call_target="tpu_custom_call" | custom-call | bytes 48000000 | tf_op jit(solution)/shard_map/gate_up_step/pallas_call | solution.py:242
  681.9 9.8 %combine_all.1.packed_ref = f32[16,128]{1,0:T(8,128)} custom-call(f32[16,128]{1,0:T(8,128)} %select_select_fusion.refs_5_.early_ref, f32[8,128]{1,0:T(8,128)} %copy-done.37, f32[8,512]{1,0:T(8,128)} %get-tuple-element.134.gate_up_ref), custom_call_target="tpu_custom_call" | custom-call | bytes 30000000 | tf_op jit(solution)/shard_map/combine_all/pallas_call | solution.py:1188
  695.4 6.7 large_update.2
  (234 shorter events, 98.0 us)
Async XLA Ops:
  7.2 217.8 %all-gather.3.cloned.1.call-start = ((), (), s32[]{:S(2)}) async-start(), calls=%async_computation.3 | async-start | bytes 5242880 | tf_op jit(solution)/shard_map/all_gather | solution.py:1214
  10.0 277.9 %all-gather.5.cloned.1.call-start = ((), (), s32[]{:S(2)}) async-start(), calls=%async_computation.4 | async-start | bytes 10485760 | tf_op jit(solution)/shard_map/all_gather | solution.py:1214
  14.8 26.4 %collective-permute-start = (bf16[256,2048]{0,1:T(8,128)(2,1)}, bf16[256,2048]{0,1:T(8,128)(2,1)}, u32[]{:S(2)}, u32[]{:S(2)}) collective-permute-start(bf16[256,2048]{0,1:T(8,128)(2,1)} %pad_maximum_fusion.4), channel_id=1, source_target_pairs={{0,4},{4,0},{8,12},{12,8},{16,20},{20,16},{24,28},{28,24},{1,5},{5... | collective-permute-start | bytes 3145736 | tf_op jit(solution)/shard_map/ppermute | solution.py:1211
  17.7 26.2 %copy-start.31 = (s32[1,1024]{1,0:T(1,128)S(1)}, s32[1,1024]{1,0:T(1,128)}, u32[]{:S(2)}) copy-start(s32[1,1024]{1,0:T(1,128)} %param.19) | copy-start | bytes 12292
  17.7 26.5 %copy-start.33 = (f32[2,256]{1,0:T(2,128)S(1)}, f32[2,256]{1,0:T(2,128)}, u32[]{:S(2)}) copy-start(f32[2,256]{1,0:T(2,128)} %refs_4_.3) | copy-start | bytes 6148
  43.9 472.2 %reduce-scatter.4.cloned.1.call-start = ((), (), s32[]{:S(2)}) async-start(), calls=%async_computation.5 | async-start | bytes 5242880 | tf_op jit(solution)/shard_map/reduce_scatter | solution.py:1217
  44.2 162.3 %copy-start.10 = (s32[1024,1]{1,0:T(8,128)}, s32[1024,1]{1,0:T(8,128)S(1)}, u32[]{:S(2)}) copy-start(s32[1024,1]{1,0:T(8,128)S(1)} %copy.55.seg_col_ref) | copy-start | bytes 12292
  47.1 159.3 %copy-start.6 = (f32[1024,128]{1,0:T(8,128)}, f32[1024,128]{1,0:T(8,128)S(1)}, u32[]{:S(2)}) copy-start(f32[1024,128]{1,0:T(8,128)S(1)} %get-tuple-element.213.cos_ref) | copy-start | bytes 1572868
  47.2 159.3 %copy-start.8 = (f32[1024,128]{1,0:T(8,128)}, f32[1024,128]{1,0:T(8,128)S(1)}, u32[]{:S(2)}) copy-start(f32[1024,128]{1,0:T(8,128)S(1)} %get-tuple-element.214.sin_ref) | copy-start | bytes 1572868
  48.9 151.2 %copy-start.53 = (bf16[1024,2048]{1,0:T(8,128)(2,1)}, bf16[1024,2048]{1,0:T(8,128)(2,1)S(1)}, u32[]{:S(2)}) copy-start(bf16[1024,2048]{1,0:T(8,128)(2,1)S(1)} %get-tuple-element.171) | copy-start | bytes 12582916
  49.2 150.9 %copy-start.60 = (f32[1024]{0:T(1024)}, f32[1024]{0:T(1024)S(1)}, u32[]{:S(2)}) copy-start(f32[1024]{0:T(1024)S(1)} %add_rsqrt_fusion) | copy-start | bytes 12292
  341.2 174.9 %reduce-scatter.6.cloned.1.call-start = ((), (), s32[]{:S(2)}) async-start(), calls=%async_computation.6 | async-start | bytes 5242880 | tf_op jit(solution)/shard_map/reduce_scatter | solution.py:1217
  355.5 295.6 %reduce-scatter.8.cloned.1.call-start = ((), (), s32[]{:S(2)}) async-start(), calls=%async_computation.7 | async-start | bytes 5242880 | tf_op jit(solution)/shard_map/reduce_scatter | solution.py:1217
  368.6 7.2 %collective-permute-start.1 = (bf16[1024,2048]{1,0:T(8,128)(2,1)S(1)}, bf16[1024,2048]{1,0:T(8,128)(2,1)S(1)}, u32[]{:S(2)}, u32[]{:S(2)}) collective-permute-start(bf16[1024,2048]{1,0:T(8,128)(2,1)S(1)} %pad_maximum_fusion.1), channel_id=1, source_target_pairs={{0,1},{1,0},{2,3},{3,2},{4,5},{5,4},{6,7},{7,6},{8,9},{9,8},{10,11... | collective-permute-start | bytes 12582920 | tf_op jit(solution)/shard_map/ppermute | solution.py:1208
  375.8 26.3 %copy-start.51 = (bf16[1024,2048]{1,0:T(8,128)(2,1)}, bf16[1024,2048]{1,0:T(8,128)(2,1)S(1)}, u32[]{:S(2)}) copy-start(bf16[1024,2048]{1,0:T(8,128)(2,1)S(1)} %collective-permute-done.1) | copy-start | bytes 12582916
  378.1 25.4 %collective-permute-start.3 = (bf16[256,2048]{1,0:T(8,128)(2,1)S(1)}, bf16[256,2048]{1,0:T(8,128)(2,1)S(1)}, u32[]{:S(2)}, u32[]{:S(2)}) collective-permute-start(bf16[256,2048]{1,0:T(8,128)(2,1)S(1)} %get-tuple-element.173), channel_id=1, source_target_pairs={{0,4},{4,0},{8,12},{12,8},{16,20},{20,16},{24,28},{28,24},{1,5},{5... | collective-permute-start | bytes 3145736 | tf_op jit(solution)/shard_map/ppermute | solution.py:1211
  477.4 53.3 %collective-permute-start.2 = (bf16[256,2048]{1,0:T(8,128)(2,1)}, bf16[256,2048]{1,0:T(8,128)(2,1)S(1)}, u32[]{:S(2)}, u32[]{:S(2)}) collective-permute-start(bf16[256,2048]{1,0:T(8,128)(2,1)} %get-tuple-element.172), channel_id=1, source_target_pairs={{0,4},{4,0},{8,12},{12,8},{16,20},{20,16},{24,28},{28,24},{1,5},{5... | collective-permute-start | bytes 3145736 | tf_op jit(solution)/shard_map/ppermute | solution.py:1211
  481.9 163.3 %collective-permute-start.4 = (bf16[256,2048]{1,0:T(8,128)(2,1)}, bf16[256,2048]{1,0:T(8,128)(2,1)}, u32[]{:S(2)}, u32[]{:S(2)}) collective-permute-start(bf16[256,2048]{1,0:T(8,128)(2,1)} %add_convert_fusion.1), channel_id=1, source_target_pairs={{0,2},{1,3},{2,0},{3,1},{4,6},{5,7},{6,4},{7,5},{8,10},{9,11},{10,... | collective-permute-start | bytes 3145736 | tf_op jit(solution)/shard_map/ppermute | solution.py:1208
  518.0 13.5 %collective-permute-start.5 = (bf16[256,1024]{1,0:T(8,128)(2,1)}, bf16[256,1024]{1,0:T(8,128)(2,1)S(1)}, u32[]{:S(2)}, u32[]{:S(2)}) collective-permute-start(bf16[256,1024]{1,0:T(8,128)(2,1)} %pick_rows.2), channel_id=1, source_target_pairs={{0,4},{4,0},{8,12},{12,8},{16,20},{20,16},{24,28},{28,24},{1,5},{5... | collective-permute-start | bytes 1572872 | tf_op jit(solution)/shard_map/ppermute | solution.py:1211
  532.3 112.9 %copy-start.48 = (f32[256,2048]{1,0:T(8,128)S(1)}, f32[256,2048]{1,0:T(8,128)}, u32[]{:S(2)}) copy-start(f32[256,2048]{1,0:T(8,128)} %get-tuple-element.105.middle_ref) | copy-start | bytes 6291460
  649.5 29.2 %collective-permute-start.6 = (bf16[256,2048]{1,0:T(8,128)(2,1)}, bf16[256,2048]{1,0:T(8,128)(2,1)}, u32[]{:S(2)}, u32[]{:S(2)}) collective-permute-start(bf16[256,2048]{1,0:T(8,128)(2,1)} %add_convert_fusion), channel_id=1, source_target_pairs={{0,2},{1,3},{2,0},{3,1},{4,6},{5,7},{6,4},{7,5},{8,10},{9,11},{10,... | collective-permute-start | bytes 3145736 | tf_op jit(solution)/shard_map/ppermute | solution.py:1208
  652.9 13.1 %collective-permute-start.7 = (bf16[256,1024]{1,0:T(8,128)(2,1)}, bf16[256,1024]{1,0:T(8,128)(2,1)}, u32[]{:S(2)}, u32[]{:S(2)}) collective-permute-start(bf16[256,1024]{1,0:T(8,128)(2,1)} %pick_rows.3), channel_id=1, source_target_pairs={{0,4},{4,0},{8,12},{12,8},{16,20},{20,16},{24,28},{28,24},{1,5},{5... | collective-permute-start | bytes 1572872 | tf_op jit(solution)/shard_map/ppermute | solution.py:1211
  653.5 25.2 %copy-start.35 = (f32[2,256]{1,0:T(2,128)}, f32[2,256]{1,0:T(2,128)S(1)}, u32[]{:S(2)}) copy-start(f32[2,256]{1,0:T(2,128)S(1)} %constant_dynamic-slice_fusion.grad_gains_ref) | copy-start | bytes 6148
  681.9 23.9 %collective-permute-start.8 = (bf16[512,2048]{1,0:T(8,128)(2,1)}, bf16[512,2048]{1,0:T(8,128)(2,1)}, u32[]{:S(2)}, u32[]{:S(2)}) collective-permute-start(bf16[512,2048]{1,0:T(8,128)(2,1)} %pad_maximum_fusion.3), channel_id=1, source_target_pairs={{0,1},{1,0},{2,3},{3,2},{4,5},{5,4},{6,7},{7,6},{8,9},{9,8},{10,11... | collective-permute-start | bytes 6291464 | tf_op jit(solution)/shard_map/ppermute | solution.py:1208
  (58 other events, 314.2 us)
Sparse Core Ops, SparseCore 0:
  10.2 101.1 all-gather.2
  113.5 164.0 all-gather.4
  341.3 81.2 reduce-scatter.3
  425.4 77.2 reduce-scatter.5
  504.9 97.2 reduce-scatter.7
